TPU v7x, 512 devices: a whole 4x8x8 slice. The times are simulated.
512 devices in a mesh: layer: 4 (over y_lo), latent: 128 (over x, z, y_hi, core).
Axes of the slice: x: 4, y: 8 (y_hi: 2, y_lo: 4; y = y_hi * 4 + y_lo), z: 8, core: 2. Of those that a mesh axis runs over, the one named last changes fastest.
Arguments:
- inputs: bfloat16 [4, 192, 5120], P('layer', None, 'latent'), may hold values from -6 to 6
- targets: bfloat16 [4, 192, 5120], P('layer', None, 'latent'), may hold values from -6 to 6
- encoder: bfloat16 [4, 8192, 5120], P('layer', 'latent'), may hold values from -0.078125 to 0.078125
- threshold: float32 [4, 8192], P('layer', 'latent'), may hold values from 0.1 to 1
- decoders: bfloat16 [4, 4, 8192, 5120], P('layer', None, 'latent'), may hold values from -0.25 to 0.25
- out_bias: bfloat16 [4, 5120], P('layer', 'latent'), may hold values from -3 to 3
- positions: int32 [192], replicated, may hold values from 0 to 95, as said below
Outputs:
- grad_encoder: float32 [4, 8192, 5120], P('layer', 'latent')
- grad_threshold: float32 [4, 8192], P('layer', 'latent')
Inputs may be any that keep to these rules, and one draw needn't show every extreme that they name: `positions`: each token's position within its packed document; the first document covers exactly the first 96 tokens, and later documents start in the second half.
All inputs are finite; a program needn't handle non-finite values.
Results may differ from a plain program's by a relative error of at most 0.0045.
Values may be sent and summed in bfloat16 or wider, within the bound.
No kernel may reach another device: no remote copies, remote signals or barrier semaphores. Data moves between devices by JAX's collectives and lax.ppermute only.
A program may use at most 64 MiB of HBM per device.

v0:
```python
import jax
import jax.numpy as jnp
from jax import lax
from jax.sharding import PartitionSpec as P


def smooth_gate(shifted):
    sig = jax.nn.sigmoid(4.0 * shifted)
    return (shifted * sig, sig + 4.0 * shifted * sig * (1.0 - sig))


def body(inputs, targets, encoder, threshold, decoders, out_bias, positions):
    layers = lax.axis_size("layer")
    section = lax.axis_index("layer")
    token_mask = (positions > 0).astype(jnp.float32)[:, None]
    whole_inputs = lax.all_gather(inputs[0], "latent", axis=1, tiled=True)
    preact = lax.dot_general(
        whole_inputs, encoder[0], (((1,), (1,)), ((), ())), preferred_element_type=jnp.float32
    )
    activity, gate_slope = smooth_gate(preact - threshold[0][None, :])
    code_block = activity.astype(jnp.bfloat16)
    local_decoders = decoders[0]
    sources = jnp.arange(layers, dtype=jnp.int32)
    earlier = sources <= section
    gathered_codes = lax.all_gather(code_block[None], "layer", axis=0, tiled=True)
    masked_codes = jnp.where(earlier[:, None, None], gathered_codes, jnp.zeros_like(gathered_codes))
    recon_part = jnp.einsum(
        "ltf,lfd->td", masked_codes, local_decoders, preferred_element_type=jnp.float32
    )
    recon_sum = lax.psum_scatter(recon_part, "latent", scatter_dimension=1, tiled=True)
    error_part = (
        token_mask
        * (recon_sum + out_bias[0].astype(jnp.float32)[None, :] - targets[0].astype(jnp.float32))
        / layers
    ).astype(jnp.bfloat16)
    error_full = lax.all_gather(error_part, "latent", axis=1, tiled=True)
    back_terms = jnp.einsum(
        "td,lfd->ltf", error_full, local_decoders, preferred_element_type=jnp.float32
    )
    back_terms = jnp.where(earlier[:, None, None], back_terms, jnp.zeros_like(back_terms))
    code_grad = lax.psum_scatter(back_terms, "layer", scatter_dimension=0, tiled=True)[0]
    z_grad = code_grad * gate_slope
    grad_threshold = -jnp.sum(z_grad, axis=0)
    grad_encoder = lax.dot_general(
        z_grad.astype(jnp.bfloat16),
        whole_inputs,
        (((0,), (0,)), ((), ())),
        preferred_element_type=jnp.float32,
    )
    return (grad_encoder[None], grad_threshold[None])


def solution(mesh):
    in_specs = (
        P("layer", None, "latent"),
        P("layer", None, "latent"),
        P("layer", "latent", None),
        P("layer", "latent"),
        P("layer", None, "latent", None),
        P("layer", "latent"),
        P(),
    )
    out_specs = (P("layer", "latent", None), P("layer", "latent"))
    return jax.shard_map(body, mesh=mesh, in_specs=in_specs, out_specs=out_specs, check_vma=False)
```

profile of v0, /device:TPU:1, one launch (start us, length us, event | category | flops | bytes accessed | tf_op | source)
XLA Modules:
  0.0 1147.5 jit_solution(16072891392297345322)
XLA Ops:
  7.2 0.0 copy-start
  7.2 0.0 all-gather.8.cloned.1.call-start
  7.2 0.7 all-gather.8.cloned.1.call-update
  7.9 0.0 reduce-scatter.3.cloned.1.call-start
  8.0 138.9 %all-gather.8.cloned.1.call-done = bf16[1,192,5120]{1,2,0:T(8,128)(2,1)} async-done(((bf16[1,192,40]{1,2,0:T(8,128)(2,1)}), bf16[1,192,5120]{1,2,0:T(8,128)(2,1)}) %all-gather.8.cloned.1.call-update) | async-done | bytes 1966096 | tf_op jit(solution)/shard_map/all_gather | solution.py:16
  146.8 2.4 fusion.17
  149.3 11.0 all-gather.2
  160.3 0.0 copy-done
  160.3 3.5 convolution_bitcast_fusion
  163.8 0.0 copy-start.3
  163.8 0.0 copy-start.2
  163.8 0.0 copy-start.1
  163.8 0.0 reduce-scatter.3.cloned.1.call-update
  163.8 0.0 all-gather.6.cloned.1.call-start
  163.9 0.6 copy-done.3
  164.4 0.0 copy-done.2
  164.5 811.6 %reduce-scatter.3.cloned.1.call-done = f32[192,40]{0,1:T(8,128)} async-done(((f32[192,5120]{0,1:T(8,128)}), f32[192,40]{0,1:T(8,128)}) %reduce-scatter.3.cloned.1.call-update) | async-done | bytes 30736 | tf_op jit(solution)/shard_map/reduce_scatter | solution.py:30
  976.1 0.0 copy-done.1
  976.1 1.5 fusion.26
  977.6 0.0 all-gather.6.cloned.1.call-update
  977.6 0.0 reduce-scatter.5.cloned.1.call-start
  977.6 133.5 %all-gather.6.cloned.1.call-done = bf16[192,5120]{0,1:T(8,128)(2,1)} async-done(((bf16[192,40]{0,1:T(8,128)(2,1)}), bf16[192,5120]{0,1:T(8,128)(2,1)}) %all-gather.6.cloned.1.call-update) | async-done | bytes 1966096 | tf_op jit(solution)/shard_map/all_gather | solution.py:36
  1111.2 3.3 fusion.12
  1114.4 0.0 reduce-scatter.5.cloned.1.call-update
  1114.5 21.3 %reduce-scatter.5.cloned.1.call-done = f32[1,192,64]{1,2,0:T(8,128)} async-done(((f32[4,192,64]{1,2,0:T(8,128)}), f32[1,192,64]{1,2,0:T(8,128)}) %reduce-scatter.5.cloned.1.call-update) | async-done | bytes 49168 | tf_op jit(solution)/shard_map/reduce_scatter | solution.py:41
  1135.8 1.0 fusion.30
  1136.8 0.5 negate_bitcast_fusion
  1137.3 3.7 convolution_bitcast_fusion.1
  (4 shorter events, 0.0 us)
Async XLA Ops:
  7.2 153.1 %copy-start = (bf16[1,4,64,5120]{3,2,1,0:T(8,128)(2,1)S(1)}, bf16[1,4,64,5120]{3,2,1,0:T(8,128)(2,1)}, u32[]{:S(2)}) copy-start(bf16[1,4,64,5120]{3,2,1,0:T(8,128)(2,1)} %param.11) | copy-start | bytes 7864324
  7.2 139.7 %all-gather.8.cloned.1.call-start = ((), (), s32[]{:S(2)}) async-start(), calls=%async_computation.5 | async-start | bytes 2641920 | tf_op jit(solution)/shard_map/all_gather | solution.py:16
  7.9 968.2 %reduce-scatter.3.cloned.1.call-start = ((), (), s32[]{:S(2)}) async-start(), calls=%async_computation.2 | async-start | bytes 5283840 | tf_op jit(solution)/shard_map/reduce_scatter | solution.py:30
  163.8 0.7 copy-start.3
  163.8 0.7 copy-start.2
  163.8 812.3 %copy-start.1 = (bf16[1,192,40]{1,2,0:T(8,128)(2,1)S(1)}, bf16[1,192,40]{1,2,0:T(8,128)(2,1)}, u32[]{:S(2)}) copy-start(bf16[1,192,40]{1,2,0:T(8,128)(2,1)} %param.8) | copy-start | bytes 46084
  163.8 947.3 %all-gather.6.cloned.1.call-start = ((), (), s32[]{:S(2)}) async-start(), calls=%async_computation.3 | async-start | bytes 2641920 | tf_op jit(solution)/shard_map/all_gather | solution.py:36
  977.6 158.2 %reduce-scatter.5.cloned.1.call-start = ((), (), s32[]{:S(2)}) async-start(), calls=%async_computation.4 | async-start | bytes 327680 | tf_op jit(solution)/shard_map/reduce_scatter | solution.py:41
Sparse Core Ops, SparseCore 0:
  12.7 134.1 all-gather.7
  163.9 812.1 reduce-scatter.2
  982.2 128.9 all-gather.5
  1114.6 21.1 reduce-scatter.4
where the time goes:
time: 1150 us
  waiting for transfers between devices  1110 us (97%)
  between operations  13.8 us (1%)
  matrix products  12.9 us (1%)
    reduce_scatter x1, waiting for transfers between devices, body(): lax.psum_scatter(recon_part, 'latent', scatter_dimension=1, tiled=True)  812 us
    all_gather x1, waiting for transfers between devices, body(): whole_inputs = lax.all_gather(inputs[0], 'latent', axis=1, tiled=True)  139 us
    all_gather x1, waiting for transfers between devices, body(): error_full = lax.all_gather(error_part, 'latent', axis=1, tiled=True)  134 us
  transfers between devices with their start and end apart: 4, of which 4 were waited for; matrix products, arithmetic and copies ran while one was open for 0% of the time, Pallas kernels for 0%

commit v1 on v0

v1 whole, which is shorter than its diff:
```python
import jax
import jax.numpy as jnp
from jax import lax
from jax.sharding import Mesh, PartitionSpec as P

F32 = jnp.float32
BF16 = jnp.bfloat16


def smooth_gate(shifted):
    sig = jax.nn.sigmoid(4.0 * shifted)
    return (shifted * sig, sig + 4.0 * shifted * sig * (1.0 - sig))


def size_of(axes):
    count = 1
    for name in axes:
        count *= lax.axis_size(name)
    return count


def spread(block, axes):
    count = size_of(axes)
    copies = jnp.broadcast_to(block[None], (count,) + block.shape)
    return lax.all_to_all(copies, axes, 0, 0, tiled=True)


def swap(block):
    return lax.ppermute(block, "core", [(0, 1), (1, 0)])


def body(inputs, targets, encoder, threshold, decoders, out_bias, positions):
    layers = lax.axis_size("layer")
    section = lax.axis_index("layer")
    first = lax.axis_index("core") == 0
    inputs_t = inputs[0].T
    targets_t = targets[0].T
    width, tokens = inputs_t.shape
    half = tokens // 2
    latents = threshold.shape[1]

    def mine(array):
        return jnp.where(first, array[:, :half], array[:, half:])

    def other(array):
        return jnp.where(first, array[:, half:], array[:, :half])

    def row(vector):
        return jnp.pad(vector.astype(F32), (0, half - vector.shape[0]))[None]

    rows = jnp.concatenate([row(out_bias[0]), row(threshold[0])], axis=0)
    packed = jnp.concatenate([other(inputs_t).astype(F32), other(targets_t).astype(F32), rows], axis=0)
    received = swap(packed)
    other_encoder = swap(encoder[0])
    other_decoders = swap(decoders[0])

    def pair(own, sent):
        return jnp.where(first, jnp.concatenate([own, sent], axis=0), jnp.concatenate([sent, own], axis=0))

    own_inputs = pair(mine(inputs_t), received[:width].astype(BF16))
    own_targets = pair(mine(targets_t).astype(F32), received[width : 2 * width])
    own_bias = pair(out_bias[0].astype(F32), received[2 * width, :width])
    other_threshold = received[2 * width + 1, :latents]
    own_mask = mine((positions > 0).astype(F32)[None, :])

    block = spread(own_inputs, ("z", "yh")).reshape(-1, half)
    whole_inputs = spread(block, ("x",)).reshape(-1, half)
    other_inputs = swap(whole_inputs)

    def encode(part, bias):
        preact = lax.dot_general(part, whole_inputs, (((1,), (0,)), ((), ())), preferred_element_type=F32)
        return smooth_gate(preact - bias[:, None])

    activity_a, slope_a = encode(encoder[0], threshold[0])
    activity_b, slope_b = encode(other_encoder, other_threshold)
    code_block = jnp.concatenate([activity_a.astype(BF16), activity_b.astype(BF16)], axis=0)
    codes = spread(code_block, ("layer",))
    earlier = (jnp.arange(layers, dtype=jnp.int32) <= section)[:, None, None]
    codes = jnp.where(earlier, codes, jnp.zeros_like(codes))

    def decode(part, code):
        return lax.dot_general(part, code, (((0, 1), (0, 1)), ((), ())), preferred_element_type=F32)

    recon = decode(decoders[0], codes[:, :latents]) + decode(other_decoders, codes[:, latents:])
    recon = recon.astype(BF16)
    count_x = lax.axis_size("x")
    recon = lax.all_to_all(recon.reshape(count_x, -1, half), ("x",), 0, 0, tiled=True)
    recon = jnp.sum(recon.astype(F32), axis=0)
    recon = lax.all_to_all(recon.reshape(size_of(("z", "yh")), -1, half), ("z", "yh"), 0, 0, tiled=True)
    recon = jnp.sum(recon, axis=0)
    error = (own_mask * (recon + own_bias[:, None] - own_targets) / layers).astype(BF16)
    block = spread(error, ("z", "yh")).reshape(-1, half)
    error_full = spread(block, ("x",)).reshape(-1, half)

    def back(part):
        return lax.dot_general(part, error_full, (((2,), (0,)), ((), ())), preferred_element_type=F32)

    back_terms = jnp.concatenate([back(decoders[0]), back(other_decoders)], axis=1)
    back_terms = jnp.where(earlier, back_terms, jnp.zeros_like(back_terms))
    code_grad = jnp.sum(lax.all_to_all(back_terms, ("layer",), 0, 0, tiled=True), axis=0)
    z_a = code_grad[:latents] * slope_a
    z_b = code_grad[latents:] * slope_b
    z_c = swap(z_b)
    grad_threshold = -jnp.sum(z_a + z_c, axis=1)

    def outer(grad, source):
        return lax.dot_general(grad.astype(BF16), source, (((1,), (1,)), ((), ())), preferred_element_type=F32)

    grad_encoder = outer(z_a, whole_inputs) + outer(z_c, other_inputs)
    return (grad_encoder[None], grad_threshold[None])


LATENT = ("x", "z", "yh", "core")


def split_mesh(mesh, parts):
    devices = mesh.devices.reshape((mesh.devices.shape[0],) + parts)
    return Mesh(devices, ("layer",) + LATENT)


def solution(mesh, parts=(4, 8, 2, 2)):
    in_specs = (
        P("layer", None, LATENT),
        P("layer", None, LATENT),
        P("layer", LATENT, None),
        P("layer", LATENT),
        P("layer", None, LATENT, None),
        P("layer", LATENT),
        P(),
    )
    out_specs = (P("layer", LATENT, None), P("layer", LATENT))
    fine = split_mesh(mesh, parts)
    return jax.shard_map(body, mesh=fine, in_specs=in_specs, out_specs=out_specs, check_vma=False)
```

time: 1150 us -> 180 us (0.16)
  waiting for transfers between devices: 1110 us -> 28 us
  blocking collectives: 11 us -> 72.9 us
  starting transfers between devices: 0.16 us -> 52.8 us
  between operations: 13.8 us -> 0.95 us
    reduce_scatter x2 -> x0, waiting for transfers between devices: 833 us -> none  [the longest x1 812 us: body(): lax.psum_scatter(recon_part, 'latent', scatter_dimension=1, tiled=True)]
    all_gather x2 -> x0, waiting for transfers between devices: 272 us -> none  [the longest x1 139 us: body(): whole_inputs = lax.all_gather(inputs[0], 'latent', axis=1, tiled=True)]
    all_to_all x0 -> x4, blocking collectives: none -> 72.9 us  [the longest x3 60.3 us: spread(): return lax.all_to_all(copies, axes, 0, 0, tiled=True)]
    ppermute x0 -> x5, starting transfers between devices: none -> 26.6 us  [swap(): return lax.ppermute(block, 'core', [(0, 1), (1, 0)])]
    all_to_all x0 -> x4, waiting for transfers between devices: none -> 26.4 us  [the longest x1 14.7 us: body(): lax.all_to_all(recon.reshape(size_of(('z', 'yh')), -1, half), ('z', 'yh')...]
    all_to_all x0 -> x4, starting transfers between devices: none -> 26.2 us  [the longest x2 10.6 us: spread(): return lax.all_to_all(copies, axes, 0, 0, tiled=True)]
  transfers between devices with their start and end apart: 4 -> 9, of which waited for: 4 -> 5; matrix products, arithmetic and copies ran while one was open for 0% -> 5% of each run, Pallas kernels for 0% -> 0%
where the time goes in v1:
time: 180 us; the launch traced here: 179 us
  blocking collectives  72.9 us (41%)
  starting transfers between devices  52.8 us (29%)
  waiting for transfers between devices  28 us (16%)
  matrix products  11.7 us (6%)
  local copies, waits for them, and re-layouts  10.2 us (6%)
  other arithmetic  2.87 us (2%)
    all_to_all x3, blocking collectives, spread(): return lax.all_to_all(copies, axes, 0, 0, tiled=True)  60.3 us
    ppermute x5, starting transfers between devices, swap(): return lax.ppermute(block, 'core', [(0, 1), (1, 0)])  26.6 us
    all_to_all x1, waiting for transfers between devices, body(): lax.all_to_all(recon.reshape(size_of(('z', 'yh')), -1, half), ('z', 'yh')...  14.7 us
    all_to_all x1, blocking collectives, body(): lax.all_to_all(recon.reshape(count_x, -1, half), ('x',), 0, 0, tiled=True)  12.6 us
    all_to_all x2, waiting for transfers between devices, spread(): return lax.all_to_all(copies, axes, 0, 0, tiled=True)  11.7 us
    all_to_all x2, starting transfers between devices, spread(): return lax.all_to_all(copies, axes, 0, 0, tiled=True)  10.6 us
    all_to_all x1, starting transfers between devices, body(): lax.all_to_all(back_terms, ('layer',), 0, 0, tiled=True)  8.2 us
    all_to_all x1, starting transfers between devices, body(): lax.all_to_all(recon.reshape(size_of(('z', 'yh')), -1, half), ('z', 'yh')...  7.33 us
  transfers between devices with their start and end apart: 9, of which 5 were waited for; matrix products, arithmetic and copies ran while one was open for 5% of the time, Pallas kernels for 0%

profile of v1, /device:TPU:1, one launch (start us, length us, event | category | flops | bytes accessed | tf_op | source)
XLA Modules:
  0.0 179.5 jit_solution(12233952828997638089)
XLA Ops:
  0.6 8.9 %collective-permute-start.2 = (bf16[4,64,5120]{2,1,0:T(8,128)(2,1)}, bf16[4,64,5120]{2,1,0:T(8,128)(2,1)}, u32[]{:S(2)}, u32[]{:S(2)}) collective-permute-start(bf16[4,64,5120]{2,1,0:T(8,128)(2,1)} %bitcast.72), channel_id=1, source_target_pairs={{0,1},{1,0},{2,3},{3,2},{4,5},{5,4},{6,7},{7,6},{8,9},{9,8},{10,11... | collective-permute-start | bytes 7864328 | tf_op jit(solution)/shard_map/ppermute | solution.py:29
  9.6 0.7 bitcast_convert_fusion
  10.2 0.7 pad_bitcast_fusion
  10.9 0.9 select_convert_fusion
  11.8 1.9 %collective-permute-start = (f32[82,96]{1,0:T(8,128)S(1)}, f32[82,96]{1,0:T(8,128)S(1)}, u32[]{:S(2)}, u32[]{:S(2)}) collective-permute-start(f32[82,96]{1,0:T(8,128)S(1)} %pad_maximum_fusion), channel_id=1, source_target_pairs={{0,1},{1,0},{2,3},{3,2},{4,5},{5,4},{6,7},{7,6},{8,9},{9,8},{10,11... | collective-permute-start | bytes 94472 | tf_op jit(solution)/shard_map/ppermute | solution.py:29
  13.7 1.2 collective-permute-done
  15.0 22.8 %all_to_all.40 = bf16[16,80,96]{2,1,0:T(8,128)(2,1)S(1)} all-to-all(bf16[16,80,96]{2,1,0:T(8,128)(2,1)S(1)} %broadcast_in_dim.75), channel_id=1, replica_groups=mesh['layer'=4,'x'=4,'z'=8,'yh'=2,'core'=2] {'z','yh'}, dimensions={0} | all-to-all | bytes 491520 | tf_op jit(solution)/shard_map/all_to_all | solution.py:25
  37.8 0.2 copy.29
  38.0 0.0 copy-start.5
  38.0 1.0 broadcast_in_dim.77
  39.0 4.0 %all-to-all-start.1 = ((bf16[4,1280,96]{1,2,0:T(8,128)(2,1)}), bf16[4,1280,96]{1,2,0:T(8,128)(2,1)S(1)}, u32[]{:S(2)}, u32[]{:S(2)}) async-start(bf16[4,1280,96]{1,2,0:T(8,128)(2,1)} %broadcast_in_dim.77), calls=%async_computation.1 | async-start | bytes 1966080 | tf_op jit(solution)/shard_map/all_to_all | solution.py:25
  43.0 4.5 %collective-permute-start.1 = (bf16[64,5120]{1,0:T(8,128)(2,1)S(1)}, bf16[64,5120]{1,0:T(8,128)(2,1)}, u32[]{:S(2)}, u32[]{:S(2)}) collective-permute-start(bf16[64,5120]{1,0:T(8,128)(2,1)S(1)} %bitcast.83), channel_id=1, source_target_pairs={{0,1},{1,0},{2,3},{3,2},{4,5},{5,4},{6,7},{7,6},{8,9},{9,8},{10,11... | collective-permute-start | bytes 1966088 | tf_op jit(solution)/shard_map/ppermute | solution.py:29
  47.5 7.0 %all-to-all-done.1 = bf16[4,1280,96]{1,2,0:T(8,128)(2,1)S(1)} async-done(((bf16[4,1280,96]{1,2,0:T(8,128)(2,1)}), bf16[4,1280,96]{1,2,0:T(8,128)(2,1)S(1)}, u32[]{:S(2)}, u32[]{:S(2)}) %all-to-all-start.1) | async-done | bytes 983072 | tf_op jit(solution)/shard_map/all_to_all | solution.py:25
  54.6 0.1 copy.45
  54.6 0.0 copy-start.1
  54.7 0.0 copy-start
  54.7 0.5 multiply_convert_fusion.1
  55.2 0.0 collective-permute-done.1
  55.2 0.4 copy-done.1
  55.6 1.8 multiply_convert_fusion
  57.4 0.1 copy.31
  57.5 0.6 broadcast_in_dim.78
  58.2 6.6 %all-to-all-start.2 = ((bf16[4,128,96]{1,2,0:T(8,128)(2,1)}), bf16[4,128,96]{1,2,0:T(8,128)(2,1)S(1)}, u32[]{:S(2)}, u32[]{:S(2)}) async-start(bf16[4,128,96]{1,2,0:T(8,128)(2,1)} %broadcast_in_dim.78), calls=%async_computation.2 | async-start | bytes 196608 | tf_op jit(solution)/shard_map/all_to_all | solution.py:25
  64.8 4.7 %all-to-all-done.2 = bf16[4,128,96]{1,2,0:T(8,128)(2,1)S(1)} async-done(((bf16[4,128,96]{1,2,0:T(8,128)(2,1)}), bf16[4,128,96]{1,2,0:T(8,128)(2,1)S(1)}, u32[]{:S(2)}, u32[]{:S(2)}) %all-to-all-start.2) | async-done | bytes 98336 | tf_op jit(solution)/shard_map/all_to_all | solution.py:25
  69.5 0.1 copy.32
  69.6 0.1 broadcast_select_fusion
  69.7 0.6 convolution_bitcast_fusion.1
  70.3 0.0 collective-permute-done.2
  70.3 2.4 %fusion.1 = bf16[96,5120]{1,0:T(8,128)(2,1)S(1)} fusion(f32[96,5120]{1,0:T(8,128)S(1)} %convolution_bitcast_fusion.1, bf16[4,64,5120]{2,1,0:T(8,128)(2,1)} %collective-permute-done.2, bf16[4,128,96]{2,1,0:T(8,128)(2,1)S(1)} %broadcast_select_fusion), kind=kOutput, calls=%fused_computation.3 | convolution fusion | flops 252641280 | bytes 5636096 | tf_op jit(solution)/shard_map/dot_general | solution.py:82
  72.7 0.1 copy.47
  72.7 0.0 copy-start.6
  72.7 12.6 %all_to_all.41 = bf16[4,1280,96]{1,2,0:T(8,128)(2,1)S(1)} all-to-all(bf16[4,1280,96]{1,2,0:T(8,128)(2,1)S(1)} %bitcast.79), channel_id=1, replica_groups=mesh['layer'=4,'x'=4,'z'=8,'yh'=2,'core'=2] {'x'}, dimensions={0} | all-to-all | bytes 1966080 | tf_op jit(solution)/shard_map/all_to_all | solution.py:87
  85.3 0.1 convert_reduce_fusion
  85.5 1.1 copy.35
  86.6 7.3 %all-to-all-start.4 = ((f32[16,80,96]{2,1,0:T(8,128)}), f32[16,80,96]{2,1,0:T(8,128)S(1)}, u32[]{:S(2)}, u32[]{:S(2)}) async-start(f32[16,80,96]{2,1,0:T(8,128)} %bitcast.80), calls=%async_computation.4 | async-start | bytes 1310720 | tf_op jit(solution)/shard_map/all_to_all | solution.py:89
  93.9 0.1 fusion.14
  94.0 0.1 broadcast_select_fusion.2
  94.1 14.7 %all-to-all-done.4 = f32[16,80,96]{2,1,0:T(8,128)S(1)} async-done(((f32[16,80,96]{2,1,0:T(8,128)}), f32[16,80,96]{2,1,0:T(8,128)S(1)}, u32[]{:S(2)}, u32[]{:S(2)}) %all-to-all-start.4) | async-done | bytes 491552 | tf_op jit(solution)/shard_map/all_to_all | solution.py:89
  108.8 0.1 reduce_sum.37
  108.8 0.1 fusion.10
  109.0 24.7 %all_to_all.42 = bf16[16,80,96]{2,1,0:T(8,128)(2,1)S(1)} all-to-all(bf16[16,80,96]{2,1,0:T(8,128)(2,1)S(1)} %broadcast_in_dim.80), channel_id=1, replica_groups=mesh['layer'=4,'x'=4,'z'=8,'yh'=2,'core'=2] {'z','yh'}, dimensions={0} | all-to-all | bytes 491520 | tf_op jit(solution)/shard_map/all_to_all | solution.py:25
  133.6 0.2 copy.36
  133.8 0.1 broadcast_in_dim.82
  133.9 12.7 %all_to_all.43 = bf16[4,1280,96]{1,2,0:T(8,128)(2,1)S(1)} all-to-all(bf16[4,1280,96]{1,2,0:T(8,128)(2,1)S(1)} %broadcast_in_dim.82), channel_id=1, replica_groups=mesh['layer'=4,'x'=4,'z'=8,'yh'=2,'core'=2] {'x'}, dimensions={0} | all-to-all | bytes 1966080 | tf_op jit(solution)/shard_map/all_to_all | solution.py:25
  146.6 1.7 copy.37
  148.4 2.8 %reshape.166 = bf16[5120,96,1]{0,1,2:T(8,128)(2,1)} reshape(bf16[4,1280,96]{1,0,2:T(4,128)(2,1)} %copy.37) | data formatting | bytes 1966080 | tf_op jit(solution)/shard_map/reshape | solution.py:93
  151.1 2.1 %convolution_bitcast_fusion.3 = f32[4,64,96]{2,1,0:T(8,128)S(1)} fusion(bf16[5120,96,1]{0,1,2:T(8,128)(2,1)} %reshape.166, bf16[1,4,64,5120]{3,2,1,0:T(8,128)(2,1)S(1)} %copy-done), kind=kOutput, calls=%fused_computation.8 | convolution fusion | flops 251658240 | bytes 3702784 | tf_op jit(solution)/shard_map/dot_general | solution.py:96
  153.3 0.0 copy-start.2
  153.3 2.6 %convolution_bitcast_fusion.2 = f32[4,64,96]{2,1,0:T(8,128)S(1)} fusion(bf16[5120,96,1]{0,1,2:T(8,128)(2,1)S(1)} %copy-done.3, bf16[4,64,5120]{2,1,0:T(8,128)(2,1)} %collective-permute-done.2), kind=kOutput, calls=%fused_computation.7 | convolution fusion | flops 251658240 | bytes 3702784 | tf_op jit(solution)/shard_map/dot_general | solution.py:96
  155.9 0.1 maximum_select_fusion
  156.0 0.8 copy.38
  156.8 8.2 %all-to-all-start.7 = ((f32[4,128,96]{1,2,0:T(8,128)}), f32[4,128,96]{1,2,0:T(8,128)S(1)}, u32[]{:S(2)}, u32[]{:S(2)}) async-start(f32[4,128,96]{1,2,0:T(8,128)} %copy.38), calls=%async_computation.7 | async-start | bytes 393216 | tf_op jit(solution)/shard_map/all_to_all | solution.py:100
  165.0 5.1 %collective-permute-start.4 = (bf16[5120,96]{0,1:T(8,128)(2,1)S(1)}, bf16[5120,96]{0,1:T(8,128)(2,1)S(1)}, u32[]{:S(2)}, u32[]{:S(2)}) collective-permute-start(bf16[5120,96]{0,1:T(8,128)(2,1)S(1)} %bitcast.75), channel_id=1, source_target_pairs={{0,1},{1,0},{2,3},{3,2},{4,5},{5,4},{6,7},{7,6},{8,9},{9,8},{10,11... | collective-permute-start | bytes 2949128 | tf_op jit(solution)/shard_map/ppermute | solution.py:29
  170.1 0.0 all-to-all-done.7
  170.2 0.1 fusion.18
  170.2 0.1 copy.43
  170.4 6.2 %collective-permute-start.3 = (f32[64,96]{1,0:T(8,128)S(1)}, f32[64,96]{1,0:T(8,128)S(1)}, u32[]{:S(2)}, u32[]{:S(2)}) collective-permute-start(f32[64,96]{1,0:T(8,128)S(1)} %add_multiply_fusion), channel_id=1, source_target_pairs={{0,1},{1,0},{2,3},{3,2},{4,5},{5,4},{6,7},{7,6},{8,9},{9,8},{10,11... | collective-permute-start | bytes 73736 | tf_op jit(solution)/shard_map/ppermute | solution.py:29
  176.6 0.1 copy.42
  176.7 0.4 fusion.12
  177.0 0.4 collective-permute-done.3
  177.4 0.1 add_reduce_fusion
  177.6 0.5 negate_bitcast_fusion
  178.1 0.0 collective-permute-done.4
  178.1 1.4 fusion.2
  (21 shorter events, 0.2 us)
Async XLA Ops:
  0.6 42.4 %copy-start.4 = (bf16[1,64,5120]{2,1,0:T(8,128)(2,1)S(1)}, bf16[1,64,5120]{2,1,0:T(8,128)(2,1)}, u32[]{:S(2)}) copy-start(bf16[1,64,5120]{2,1,0:T(8,128)(2,1)} %param.9) | copy-start | bytes 1966084
  0.6 69.6 %collective-permute-start.2 = (bf16[4,64,5120]{2,1,0:T(8,128)(2,1)}, bf16[4,64,5120]{2,1,0:T(8,128)(2,1)}, u32[]{:S(2)}, u32[]{:S(2)}) collective-permute-start(bf16[4,64,5120]{2,1,0:T(8,128)(2,1)} %bitcast.72), channel_id=1, source_target_pairs={{0,1},{1,0},{2,3},{3,2},{4,5},{5,4},{6,7},{7,6},{8,9},{9,8},{10,11... | collective-permute-start | bytes 7864328 | tf_op jit(solution)/shard_map/ppermute | solution.py:29
  11.8 3.1 %collective-permute-start = (f32[82,96]{1,0:T(8,128)S(1)}, f32[82,96]{1,0:T(8,128)S(1)}, u32[]{:S(2)}, u32[]{:S(2)}) collective-permute-start(f32[82,96]{1,0:T(8,128)S(1)} %pad_maximum_fusion), channel_id=1, source_target_pairs={{0,1},{1,0},{2,3},{3,2},{4,5},{5,4},{6,7},{7,6},{8,9},{9,8},{10,11... | collective-permute-start | bytes 94472 | tf_op jit(solution)/shard_map/ppermute | solution.py:29
  38.0 16.7 %copy-start.5 = (f32[1,64]{1,0:T(1,128)S(1)}, f32[1,64]{1,0:T(1,128)}, u32[]{:S(2)}) copy-start(f32[1,64]{1,0:T(1,128)} %param.10) | copy-start | bytes 772
  39.0 15.6 %all-to-all-start.1 = ((bf16[4,1280,96]{1,2,0:T(8,128)(2,1)}), bf16[4,1280,96]{1,2,0:T(8,128)(2,1)S(1)}, u32[]{:S(2)}, u32[]{:S(2)}) async-start(bf16[4,1280,96]{1,2,0:T(8,128)(2,1)} %broadcast_in_dim.77), calls=%async_computation.1 | async-start | bytes 1966080 | tf_op jit(solution)/shard_map/all_to_all | solution.py:25
  43.0 12.2 %collective-permute-start.1 = (bf16[64,5120]{1,0:T(8,128)(2,1)S(1)}, bf16[64,5120]{1,0:T(8,128)(2,1)}, u32[]{:S(2)}, u32[]{:S(2)}) collective-permute-start(bf16[64,5120]{1,0:T(8,128)(2,1)S(1)} %bitcast.83), channel_id=1, source_target_pairs={{0,1},{1,0},{2,3},{3,2},{4,5},{5,4},{6,7},{7,6},{8,9},{9,8},{10,11... | collective-permute-start | bytes 1966088 | tf_op jit(solution)/shard_map/ppermute | solution.py:29
  54.6 0.9 copy-start.1
  54.7 15.0 %copy-start = (bf16[1,4,64,5120]{3,2,1,0:T(8,128)(2,1)S(1)}, bf16[1,4,64,5120]{3,2,1,0:T(8,128)(2,1)}, u32[]{:S(2)}) copy-start(bf16[1,4,64,5120]{3,2,1,0:T(8,128)(2,1)} %param.11) | copy-start | bytes 7864324
  58.2 11.3 %all-to-all-start.2 = ((bf16[4,128,96]{1,2,0:T(8,128)(2,1)}), bf16[4,128,96]{1,2,0:T(8,128)(2,1)S(1)}, u32[]{:S(2)}, u32[]{:S(2)}) async-start(bf16[4,128,96]{1,2,0:T(8,128)(2,1)} %broadcast_in_dim.78), calls=%async_computation.2 | async-start | bytes 196608 | tf_op jit(solution)/shard_map/all_to_all | solution.py:25
  72.7 21.2 %copy-start.6 = (s32[192]{0:T(256)S(1)}, s32[192]{0:T(256)}, u32[]{:S(2)}) copy-start(s32[192]{0:T(256)} %param.13) | copy-start | bytes 2308
  86.6 22.2 %all-to-all-start.4 = ((f32[16,80,96]{2,1,0:T(8,128)}), f32[16,80,96]{2,1,0:T(8,128)S(1)}, u32[]{:S(2)}, u32[]{:S(2)}) async-start(f32[16,80,96]{2,1,0:T(8,128)} %bitcast.80), calls=%async_computation.4 | async-start | bytes 1310720 | tf_op jit(solution)/shard_map/all_to_all | solution.py:89
  151.1 2.1 %copy-start.3 = (bf16[5120,96,1]{0,1,2:T(8,128)(2,1)S(1)}, bf16[5120,96,1]{0,1,2:T(8,128)(2,1)}, u32[]{:S(2)}) copy-start(bf16[5120,96,1]{0,1,2:T(8,128)(2,1)} %reshape.166) | copy-start | bytes 2949124
  153.3 11.8 %copy-start.2 = (bf16[4,12,8,1280]{3,2,0,1:T(8,128)(2,1)S(1)}, bf16[4,12,8,1280]{3,2,0,1:T(8,128)(2,1)}, u32[]{:S(2)}) copy-start(bf16[4,12,8,1280]{3,2,0,1:T(8,128)(2,1)} %copy-done.1) | copy-start | bytes 2949124
  156.8 13.3 %all-to-all-start.7 = ((f32[4,128,96]{1,2,0:T(8,128)}), f32[4,128,96]{1,2,0:T(8,128)S(1)}, u32[]{:S(2)}, u32[]{:S(2)}) async-start(f32[4,128,96]{1,2,0:T(8,128)} %copy.38), calls=%async_computation.7 | async-start | bytes 393216 | tf_op jit(solution)/shard_map/all_to_all | solution.py:100
  165.0 13.0 %collective-permute-start.4 = (bf16[5120,96]{0,1:T(8,128)(2,1)S(1)}, bf16[5120,96]{0,1:T(8,128)(2,1)S(1)}, u32[]{:S(2)}, u32[]{:S(2)}) collective-permute-start(bf16[5120,96]{0,1:T(8,128)(2,1)S(1)} %bitcast.75), channel_id=1, source_target_pairs={{0,1},{1,0},{2,3},{3,2},{4,5},{5,4},{6,7},{7,6},{8,9},{9,8},{10,11... | collective-permute-start | bytes 2949128 | tf_op jit(solution)/shard_map/ppermute | solution.py:29
  170.4 7.1 %collective-permute-start.3 = (f32[64,96]{1,0:T(8,128)S(1)}, f32[64,96]{1,0:T(8,128)S(1)}, u32[]{:S(2)}, u32[]{:S(2)}) collective-permute-start(f32[64,96]{1,0:T(8,128)S(1)} %add_multiply_fusion), channel_id=1, source_target_pairs={{0,1},{1,0},{2,3},{3,2},{4,5},{5,4},{6,7},{7,6},{8,9},{9,8},{10,11... | collective-permute-start | bytes 73736 | tf_op jit(solution)/shard_map/ppermute | solution.py:29

commit v2 on v1

v2 whole, which is shorter than its diff:
```python
import jax
import jax.numpy as jnp
from jax import lax
from jax.sharding import Mesh, PartitionSpec as P

F32 = jnp.float32
BF16 = jnp.bfloat16
NEAR = ("x", "zl")
FAR = ("zh", "yh")


def smooth_gate(shifted):
    sig = jax.nn.sigmoid(4.0 * shifted)
    return (shifted * sig, sig + 4.0 * shifted * sig * (1.0 - sig))


def size_of(axes):
    count = 1
    for name in axes:
        count *= lax.axis_size(name)
    return count


def exchange(blocks, axes):
    return lax.all_to_all(blocks, axes, 0, 0, tiled=True)


def spread(block, axes):
    return exchange(jnp.broadcast_to(block[None], (size_of(axes),) + block.shape), axes)


def swap(block):
    return lax.ppermute(block, "core", [(0, 1), (1, 0)])


def to_owner(block):
    high, low = lax.axis_size("zh"), lax.axis_size("zl")
    pairs = [(a * high + b, b * low + a) for a in range(low) for b in range(high)]
    return lax.ppermute(block, ("zh", "zl"), pairs)


def body(inputs, targets, encoder, threshold, decoders, out_bias, positions):
    layers = lax.axis_size("layer")
    section = lax.axis_index("layer")
    first = lax.axis_index("core") == 0
    width, tokens = inputs.shape[2], inputs.shape[1]
    half = tokens // 2
    latents = threshold.shape[1]
    xs, zh, zl, yh = (lax.axis_size(name) for name in ("x", "zh", "zl", "yh"))

    def halves(array):
        return jnp.stack([array[:, :half], array[:, half:]])

    def mine(pair):
        return jnp.where(first, pair[0], pair[1])

    def other(pair):
        return jnp.where(first, pair[1], pair[0])

    input_halves = halves(inputs[0].T)
    sends = jnp.broadcast_to(input_halves[None], (zh * yh,) + input_halves.shape)
    block = exchange(sends.reshape((-1, width, half)), FAR + ("core",)).reshape(-1, half)

    def row(vector):
        return jnp.pad(vector.astype(F32), (0, half - vector.shape[0]))[None]

    target_halves = halves(targets[0].T).astype(F32)
    rows = jnp.concatenate([row(out_bias[0]), row(threshold[0])], axis=0)
    received = swap(jnp.concatenate([other(target_halves), rows], axis=0))
    other_encoder = swap(encoder[0])
    other_decoders = swap(decoders[0])
    other_threshold = received[width + 1, :latents]

    def both(own, sent):
        return jnp.where(first, jnp.concatenate([own, sent], axis=0), jnp.concatenate([sent, own], axis=0))

    own_targets = both(mine(target_halves), received[:width])
    own_bias = both(out_bias[0].astype(F32), received[width, :width])
    offset = to_owner(own_targets - own_bias[:, None])
    own_mask = mine(halves((positions > 0).astype(F32)[None, :]))

    whole_inputs = spread(block, NEAR).reshape(xs, zl, zh, yh * 2 * width, half)
    whole_inputs = whole_inputs.transpose(0, 2, 1, 3, 4).reshape(-1, half)
    other_inputs = swap(whole_inputs)

    def encode(part, bias):
        preact = lax.dot_general(part, whole_inputs, (((1,), (0,)), ((), ())), preferred_element_type=F32)
        return smooth_gate(preact - bias[:, None])

    activity_a, slope_a = encode(encoder[0], threshold[0])
    activity_b, slope_b = encode(other_encoder, other_threshold)
    slope_c = swap(slope_b)
    code_block = jnp.concatenate([activity_a.astype(BF16), activity_b.astype(BF16)], axis=0)
    codes = spread(code_block, ("layer",))
    earlier = (jnp.arange(layers, dtype=jnp.int32) <= section)[:, None, None]
    codes = jnp.where(earlier, codes, jnp.zeros_like(codes))

    def decode(part, code):
        return lax.dot_general(part, code, (((0, 1), (0, 1)), ((), ())), preferred_element_type=F32)

    recon = decode(decoders[0], codes[:, :latents]) + decode(other_decoders, codes[:, latents:])
    recon = exchange(recon.astype(BF16).reshape(xs * zl, -1, half), NEAR)
    recon = jnp.sum(recon.astype(F32), axis=0)
    recon = exchange(recon.reshape(zh * yh, -1, half), FAR)
    recon = jnp.sum(recon, axis=0)
    error = (own_mask * (recon - offset) / layers).astype(BF16)
    block = spread(error, FAR).reshape(-1, half)
    error_full = spread(block, NEAR).reshape(-1, half)

    def back(part):
        return lax.dot_general(part, error_full, (((2,), (0,)), ((), ())), preferred_element_type=F32)

    back_a, back_b = back(decoders[0]), back(other_decoders)
    back_terms = jnp.stack([jnp.where(first, back_a, back_b), jnp.where(first, back_b, back_a)], axis=1)
    back_terms = jnp.where(earlier[:, None], back_terms, jnp.zeros_like(back_terms))
    code_grad = exchange(back_terms.reshape((-1, latents, half)), ("layer", "core"))
    code_grad = jnp.sum(code_grad.reshape(layers, 2, latents, half), axis=0)
    z_a = mine(code_grad) * slope_a
    z_c = other(code_grad) * slope_c
    grad_threshold = -jnp.sum(z_a + z_c, axis=1)

    def outer(grad, source):
        return lax.dot_general(grad.astype(BF16), source, (((1,), (1,)), ((), ())), preferred_element_type=F32)

    grad_encoder = outer(z_a, whole_inputs) + outer(z_c, other_inputs)
    return (grad_encoder[None], grad_threshold[None])


LATENT = ("x", "zh", "zl", "yh", "core")


def solution(mesh, parts=(4, 4, 2, 2, 2)):
    in_specs = (
        P("layer", None, LATENT),
        P("layer", None, LATENT),
        P("layer", LATENT, None),
        P("layer", LATENT),
        P("layer", None, LATENT, None),
        P("layer", LATENT),
        P(),
    )
    out_specs = (P("layer", LATENT, None), P("layer", LATENT))
    devices = mesh.devices.reshape((mesh.devices.shape[0],) + parts)
    fine = Mesh(devices, ("layer",) + LATENT)
    return jax.shard_map(body, mesh=fine, in_specs=in_specs, out_specs=out_specs, check_vma=False)
```

time: 180 us -> 170 us (0.944)
  waiting for transfers between devices: 28 us -> 51.5 us
  blocking collectives: 72.9 us -> 49.7 us
  starting transfers between devices: 52.8 us -> 39.8 us
  matrix products: 11.7 us -> 14.9 us
    all_to_all x4 -> x6, waiting for transfers between devices: 26.4 us -> 50.5 us  [exchange(): return lax.all_to_all(blocks, axes, 0, 0, tiled=True)]
    all_to_all x4 -> x2, blocking collectives: 72.9 us -> 49.7 us  [exchange(): return lax.all_to_all(blocks, axes, 0, 0, tiled=True)]
    ppermute x5, starting transfers between devices: 26.6 us -> 11 us  [swap(): return lax.ppermute(block, 'core', [(0, 1), (1, 0)])]
    all_to_all x4 -> x6, starting transfers between devices: 26.2 us -> 28.1 us  [exchange(): return lax.all_to_all(blocks, axes, 0, 0, tiled=True)]
  transfers between devices with their start and end apart: 9 -> 12, of which waited for: 5 -> 7; matrix products, arithmetic and copies ran while one was open for 5% -> 7% of each run, Pallas kernels for 0% -> 0%
where the time goes in v2:
time: 170 us; the launch traced here: 169 us
  waiting for transfers between devices  51.5 us (30%)
  blocking collectives  49.7 us (29%)
  starting transfers between devices  39.8 us (23%)
  matrix products  14.9 us (9%)
  local copies, waits for them, and re-layouts  8.65 us (5%)
  other arithmetic  3.47 us (2%)
    all_to_all x6, waiting for transfers between devices, exchange(): return lax.all_to_all(blocks, axes, 0, 0, tiled=True)  50.5 us
    all_to_all x2, blocking collectives, exchange(): return lax.all_to_all(blocks, axes, 0, 0, tiled=True)  49.7 us
    all_to_all x6, starting transfers between devices, exchange(): return lax.all_to_all(blocks, axes, 0, 0, tiled=True)  28.1 us
    ppermute x5, starting transfers between devices, swap(): return lax.ppermute(block, 'core', [(0, 1), (1, 0)])  11 us
    dot_general x2, matrix products, back(): lax.dot_general(part, error_full, (((2,), (0,)), ((), ())), preferred_ele...  5.14 us
    dot_general x2, matrix products, decode(): lax.dot_general(part, code, (((0, 1), (0, 1)), ((), ())), preferred_eleme...  4.7 us
  transfers between devices with their start and end apart: 12, of which 7 were waited for; matrix products, arithmetic and copies ran while one was open for 7% of the time, Pallas kernels for 0%

profile of v2, /device:TPU:1, one launch (start us, length us, event | category | flops | bytes accessed | tf_op | source)
XLA Modules:
  0.0 169.0 jit_solution(1428841662364930388)
XLA Ops:
  0.6 0.9 slice_bitcast_fusion.3
  1.5 0.0 copy-start.5
  1.6 0.0 copy-start.3
  1.6 30.0 %all_to_all.40 = bf16[16,40,96]{2,1,0:T(8,128)(2,1)S(1)} all-to-all(bf16[16,40,96]{2,1,0:T(8,128)(2,1)S(1)} %bitcast.110), channel_id=1, replica_groups=mesh['layer'=4,'x'=4,'zh'=4,'zl'=2,'yh'=2,'core'=2] {'zh','yh','core'}, dimensions={0} | all-to-all | bytes 245760 | tf_op jit(solution)/shard_map/all_to_all | solution.py:25
  31.6 0.1 copy.26
  31.7 1.0 broadcast_in_dim.84
  32.8 4.7 %all-to-all-start.1 = ((bf16[8,640,96]{1,2,0:T(8,128)(2,1)}), bf16[8,640,96]{1,2,0:T(8,128)(2,1)S(1)}, u32[]{:S(2)}, u32[]{:S(2)}) async-start(bf16[8,640,96]{1,2,0:T(8,128)(2,1)} %broadcast_in_dim.84), calls=%async_computation.1 | async-start | bytes 1966080 | tf_op jit(solution)/shard_map/all_to_all | solution.py:25
  37.5 2.4 %collective-permute-start.2 = (bf16[4,64,5120]{2,1,0:T(8,128)(2,1)}, bf16[4,64,5120]{2,1,0:T(8,128)(2,1)}, u32[]{:S(2)}, u32[]{:S(2)}) collective-permute-start(bf16[4,64,5120]{2,1,0:T(8,128)(2,1)} %bitcast.26), channel_id=1, source_target_pairs={{0,1},{1,0},{2,3},{3,2},{4,5},{5,4},{6,7},{7,6},{8,9},{9,8},{10,11... | collective-permute-start | bytes 7864328 | tf_op jit(solution)/shard_map/ppermute | solution.py:33
  39.9 1.9 %collective-permute-start = (bf16[64,5120]{1,0:T(8,128)(2,1)S(1)}, bf16[64,5120]{1,0:T(8,128)(2,1)}, u32[]{:S(2)}, u32[]{:S(2)}) collective-permute-start(bf16[64,5120]{1,0:T(8,128)(2,1)S(1)} %bitcast.109), channel_id=1, source_target_pairs={{0,1},{1,0},{2,3},{3,2},{4,5},{5,4},{6,7},{7,6},{8,9},{9,8},{10,11... | collective-permute-start | bytes 1966088 | tf_op jit(solution)/shard_map/ppermute | solution.py:33
  41.9 0.1 slice_bitcast_fusion.1
  42.0 2.4 %collective-permute-start.1 = (f32[42,96]{1,0:T(8,128)S(1)}, f32[42,96]{1,0:T(8,128)S(1)}, u32[]{:S(2)}, u32[]{:S(2)}) collective-permute-start(f32[42,96]{1,0:T(8,128)S(1)} %pad_maximum_fusion.2), channel_id=1, source_target_pairs={{0,1},{1,0},{2,3},{3,2},{4,5},{5,4},{6,7},{7,6},{8,9},{9,8},{10,11... | collective-permute-start | bytes 48392 | tf_op jit(solution)/shard_map/ppermute | solution.py:33
  44.4 0.9 collective-permute-done.1
  45.4 6.8 %all-to-all-done.1 = bf16[8,640,96]{1,2,0:T(8,128)(2,1)S(1)} async-done(((bf16[8,640,96]{1,2,0:T(8,128)(2,1)}), bf16[8,640,96]{1,2,0:T(8,128)(2,1)S(1)}, u32[]{:S(2)}, u32[]{:S(2)}) %all-to-all-start.1) | async-done | bytes 983072 | tf_op jit(solution)/shard_map/all_to_all | solution.py:25
  52.2 0.8 copy.27
  52.9 0.1 copy.28
  53.1 1.0 multiply_convert_fusion.2
  54.1 0.0 collective-permute-done
  54.1 2.1 %multiply_convert_fusion.1 = (bf16[64,96]{1,0:T(8,128)(2,1)S(1)}, f32[64,96]{1,0:T(8,128)}) fusion(f32[64]{0:T(128)S(1)} %slice_bitcast_fusion.5, bf16[64,5120]{1,0:T(8,128)(2,1)} %collective-permute-done, bf16[5120,96]{1,0:T(8,128)(2,1)S(1)} %bitcast.103), kind=kOutput, calls=%fused_computation.27 | convolution fusion | flops 62982144 | bytes 1675520 | tf_op jit(solution)/shard_map/dot_general | solution.py:87
  56.2 0.1 copy.29
  56.3 0.7 broadcast_in_dim.87
  56.9 3.3 %all-to-all-start.2 = ((bf16[4,128,96]{1,2,0:T(8,128)(2,1)}), bf16[4,128,96]{1,2,0:T(8,128)(2,1)S(1)}, u32[]{:S(2)}, u32[]{:S(2)}) async-start(bf16[4,128,96]{1,2,0:T(8,128)(2,1)} %broadcast_in_dim.87), calls=%async_computation.2 | async-start | bytes 196608 | tf_op jit(solution)/shard_map/all_to_all | solution.py:25
  60.3 4.6 %all-to-all-done.2 = bf16[4,128,96]{1,2,0:T(8,128)(2,1)S(1)} async-done(((bf16[4,128,96]{1,2,0:T(8,128)(2,1)}), bf16[4,128,96]{1,2,0:T(8,128)(2,1)S(1)}, u32[]{:S(2)}, u32[]{:S(2)}) %all-to-all-start.2) | async-done | bytes 98336 | tf_op jit(solution)/shard_map/all_to_all | solution.py:25
  64.9 0.1 copy.30
  65.0 0.1 broadcast_select_fusion
  65.1 2.3 %convolution_bitcast_fusion.1 = f32[96,5120]{1,0:T(8,128)S(1)} fusion(bf16[4,128,96]{2,1,0:T(8,128)(2,1)S(1)} %broadcast_select_fusion, bf16[1,4,64,5120]{3,2,1,0:T(8,128)(2,1)} %param.11), kind=kOutput, calls=%fused_computation.2 | convolution fusion | flops 251658240 | bytes 4653056 | tf_op jit(solution)/shard_map/dot_general | solution.py:99
  67.5 0.0 collective-permute-done.2
  67.5 2.4 %fusion.1 = bf16[96,5120]{1,0:T(8,128)(2,1)S(1)} fusion(f32[96,5120]{1,0:T(8,128)S(1)} %convolution_bitcast_fusion.1, bf16[4,64,5120]{2,1,0:T(8,128)(2,1)} %collective-permute-done.2, bf16[4,128,96]{2,1,0:T(8,128)(2,1)S(1)} %broadcast_select_fusion), kind=kOutput, calls=%fused_computation.3 | convolution fusion | flops 252641280 | bytes 5636096 | tf_op jit(solution)/shard_map/dot_general | solution.py:99
  69.9 0.0 copy-start.4
  69.9 1.0 copy.41
  70.9 3.6 %all-to-all-start.3 = ((bf16[8,640,96]{1,2,0:T(8,128)(2,1)}), bf16[8,640,96]{1,2,0:T(8,128)(2,1)S(1)}, u32[]{:S(2)}, u32[]{:S(2)}) async-start(bf16[8,640,96]{1,2,0:T(8,128)(2,1)} %bitcast.101), calls=%async_computation.3 | async-start | bytes 1966080 | tf_op jit(solution)/shard_map/all_to_all | solution.py:25
  74.5 0.0 slice-start
  74.5 0.1 broadcast_select_fusion.1
  74.6 12.2 %all-to-all-done.3 = bf16[8,640,96]{1,2,0:T(8,128)(2,1)S(1)} async-done(((bf16[8,640,96]{1,2,0:T(8,128)(2,1)}), bf16[8,640,96]{1,2,0:T(8,128)(2,1)S(1)}, u32[]{:S(2)}, u32[]{:S(2)}) %all-to-all-start.3) | async-done | bytes 983072 | tf_op jit(solution)/shard_map/all_to_all | solution.py:25
  86.7 0.1 convert_reduce_fusion
  86.9 0.9 copy.33
  87.8 4.7 %all-to-all-start.4 = ((f32[8,80,96]{2,1,0:T(8,128)}), f32[8,80,96]{2,1,0:T(8,128)S(1)}, u32[]{:S(2)}, u32[]{:S(2)}) async-start(f32[8,80,96]{2,1,0:T(8,128)} %bitcast.30), calls=%async_computation.4 | async-start | bytes 655360 | tf_op jit(solution)/shard_map/all_to_all | solution.py:25
  92.5 0.1 fusion.7
  92.6 0.7 collective-permute-start.3
  93.2 0.1 fusion.11
  93.3 12.0 %all-to-all-done.4 = f32[8,80,96]{2,1,0:T(8,128)S(1)} async-done(((f32[8,80,96]{2,1,0:T(8,128)}), f32[8,80,96]{2,1,0:T(8,128)S(1)}, u32[]{:S(2)}, u32[]{:S(2)}) %all-to-all-start.4) | async-done | bytes 245792 | tf_op jit(solution)/shard_map/all_to_all | solution.py:25
  105.4 19.7 %all_to_all.41 = bf16[8,80,96]{2,1,0:T(8,128)(2,1)S(1)} all-to-all(bf16[8,80,96]{2,1,0:T(8,128)(2,1)S(1)} %broadcast_in_dim.89), channel_id=1, replica_groups=mesh['layer'=4,'x'=4,'zh'=4,'zl'=2,'yh'=2,'core'=2] {'zh','yh'}, dimensions={0} | all-to-all | bytes 245760 | tf_op jit(solution)/shard_map/all_to_all | solution.py:25
  125.1 0.1 copy.34
  125.2 1.0 broadcast_in_dim.91
  126.2 3.6 %all-to-all-start.6 = ((bf16[8,640,96]{1,2,0:T(8,128)(2,1)}), bf16[8,640,96]{1,2,0:T(8,128)(2,1)S(1)}, u32[]{:S(2)}, u32[]{:S(2)}) async-start(bf16[8,640,96]{1,2,0:T(8,128)(2,1)} %broadcast_in_dim.91), calls=%async_computation.6 | async-start | bytes 1966080 | tf_op jit(solution)/shard_map/all_to_all | solution.py:25
  129.8 0.1 broadcast_in_dim.76
  129.9 0.1 broadcast_in_dim.77
  130.0 11.2 %all-to-all-done.6 = bf16[8,640,96]{1,2,0:T(8,128)(2,1)S(1)} async-done(((bf16[8,640,96]{1,2,0:T(8,128)(2,1)}), bf16[8,640,96]{1,2,0:T(8,128)(2,1)S(1)}, u32[]{:S(2)}, u32[]{:S(2)}) %all-to-all-start.6) | async-done | bytes 983072 | tf_op jit(solution)/shard_map/all_to_all | solution.py:25
  141.2 0.3 copy.35
  141.5 0.4 reshape.102
  142.0 2.6 %fusion.12 = f32[96,4,64]{0,2,1:T(8,128)S(1)} fusion(bf16[5120,96,1]{0,1,2:T(8,128)(2,1)S(1)} %reshape.102, bf16[1,4,64,5120]{3,2,1,0:T(8,128)(2,1)} %param.11), kind=kOutput, calls=%fused_computation.54 | convolution fusion | flops 251658240 | bytes 3702784 | tf_op jit(solution)/shard_map/dot_general | solution.py:111
  144.5 2.6 %select_bitcast_fusion.1 = (f32[4,1,64,96]{3,2,0,1:T(8,128)S(1)}, f32[4,1,64,96]{3,2,0,1:T(8,128)S(1)}) fusion(f32[96,4,64]{0,2,1:T(8,128)S(1)} %fusion.12, pred[]{:T(512)S(6)} %eq.3, bf16[5120,96,1]{0,1,2:T(8,128)(2,1)S(1)} %reshape.102, bf16[4,64,5120]{2,1,0:T(8,128)(2,1)} %collective-permute-done.2), kind=kOutput, calls=%fused_computation.15 | convolution fusion | flops 251707392 | bytes 3899393 | tf_op jit(solution)/shard_map/dot_general | solution.py:111
  147.2 0.8 bitcast_select_fusion
  148.0 8.2 %all-to-all-start.7 = ((f32[8,64,96]{2,1,0:T(8,128)}), f32[8,64,96]{2,1,0:T(8,128)S(1)}, u32[]{:S(2)}, u32[]{:S(2)}) async-start(f32[8,64,96]{2,1,0:T(8,128)} %bitcast_select_fusion), calls=%async_computation.7 | async-start | bytes 524288 | tf_op jit(solution)/shard_map/all_to_all | solution.py:25
  156.2 0.6 copy.37
  156.8 1.9 %collective-permute-start.5 = (bf16[5120,96]{0,1:T(8,128)(2,1)S(1)}, bf16[5120,96]{0,1:T(8,128)(2,1)S(1)}, u32[]{:S(2)}, u32[]{:S(2)}) collective-permute-start(bf16[5120,96]{0,1:T(8,128)(2,1)S(1)} %copy.37), channel_id=1, source_target_pairs={{0,1},{1,0},{2,3},{3,2},{4,5},{5,4},{6,7},{7,6},{8,9},{9,8},{10,11... | collective-permute-start | bytes 2949128 | tf_op jit(solution)/shard_map/ppermute | solution.py:33
  158.7 2.4 %collective-permute-start.4 = (f32[64,96]{1,0:T(8,128)}, f32[64,96]{1,0:T(8,128)}, u32[]{:S(2)}, u32[]{:S(2)}) collective-permute-start(f32[64,96]{1,0:T(8,128)} %get-tuple-element.10), channel_id=1, source_target_pairs={{0,1},{1,0},{2,3},{3,2},{4,5},{5,4},{6,7},{7,6},{8,9},{9,8},{10,11... | collective-permute-start | bytes 73736 | tf_op jit(solution)/shard_map/ppermute | solution.py:33
  161.1 3.8 %all-to-all-done.7 = f32[8,64,96]{2,1,0:T(8,128)S(1)} async-done(((f32[8,64,96]{2,1,0:T(8,128)}), f32[8,64,96]{2,1,0:T(8,128)S(1)}, u32[]{:S(2)}, u32[]{:S(2)}) %all-to-all-start.7) | async-done | bytes 196640 | tf_op jit(solution)/shard_map/all_to_all | solution.py:25
  164.9 0.7 reduce_sum.38
  165.6 0.0 collective-permute-done.4
  165.6 0.9 add_reduce_fusion
  166.5 0.5 negate_bitcast_fusion
  167.0 0.6 fusion.9
  167.6 0.0 collective-permute-done.5
  167.6 1.4 fusion.2
  (28 shorter events, 0.2 us)
Async XLA Ops:
  1.5 38.4 %copy-start = (bf16[1,64,5120]{2,1,0:T(8,128)(2,1)S(1)}, bf16[1,64,5120]{2,1,0:T(8,128)(2,1)}, u32[]{:S(2)}) copy-start(bf16[1,64,5120]{2,1,0:T(8,128)(2,1)} %param.9) | copy-start | bytes 1966084
  1.5 40.3 %copy-start.2 = (bf16[1,192,40]{1,2,0:T(8,128)(2,1)S(1)}, bf16[1,192,40]{1,2,0:T(8,128)(2,1)}, u32[]{:S(2)}) copy-start(bf16[1,192,40]{1,2,0:T(8,128)(2,1)} %param.8) | copy-start | bytes 46084
  1.5 40.4 %copy-start.5 = (bf16[1,40]{1,0:T(2,128)(2,1)S(1)}, bf16[1,40]{1,0:T(2,128)(2,1)}, u32[]{:S(2)}) copy-start(bf16[1,40]{1,0:T(2,128)(2,1)} %param.12) | copy-start | bytes 244
  1.6 40.4 %copy-start.3 = (f32[1,64]{1,0:T(1,128)S(1)}, f32[1,64]{1,0:T(1,128)}, u32[]{:S(2)}) copy-start(f32[1,64]{1,0:T(1,128)} %param.10) | copy-start | bytes 772
  32.8 19.4 %all-to-all-start.1 = ((bf16[8,640,96]{1,2,0:T(8,128)(2,1)}), bf16[8,640,96]{1,2,0:T(8,128)(2,1)S(1)}, u32[]{:S(2)}, u32[]{:S(2)}) async-start(bf16[8,640,96]{1,2,0:T(8,128)(2,1)} %broadcast_in_dim.84), calls=%async_computation.1 | async-start | bytes 1966080 | tf_op jit(solution)/shard_map/all_to_all | solution.py:25
  37.5 30.0 %collective-permute-start.2 = (bf16[4,64,5120]{2,1,0:T(8,128)(2,1)}, bf16[4,64,5120]{2,1,0:T(8,128)(2,1)}, u32[]{:S(2)}, u32[]{:S(2)}) collective-permute-start(bf16[4,64,5120]{2,1,0:T(8,128)(2,1)} %bitcast.26), channel_id=1, source_target_pairs={{0,1},{1,0},{2,3},{3,2},{4,5},{5,4},{6,7},{7,6},{8,9},{9,8},{10,11... | collective-permute-start | bytes 7864328 | tf_op jit(solution)/shard_map/ppermute | solution.py:33
  39.9 14.2 %collective-permute-start = (bf16[64,5120]{1,0:T(8,128)(2,1)S(1)}, bf16[64,5120]{1,0:T(8,128)(2,1)}, u32[]{:S(2)}, u32[]{:S(2)}) collective-permute-start(bf16[64,5120]{1,0:T(8,128)(2,1)S(1)} %bitcast.109), channel_id=1, source_target_pairs={{0,1},{1,0},{2,3},{3,2},{4,5},{5,4},{6,7},{7,6},{8,9},{9,8},{10,11... | collective-permute-start | bytes 1966088 | tf_op jit(solution)/shard_map/ppermute | solution.py:33
  42.0 3.4 %collective-permute-start.1 = (f32[42,96]{1,0:T(8,128)S(1)}, f32[42,96]{1,0:T(8,128)S(1)}, u32[]{:S(2)}, u32[]{:S(2)}) collective-permute-start(f32[42,96]{1,0:T(8,128)S(1)} %pad_maximum_fusion.2), channel_id=1, source_target_pairs={{0,1},{1,0},{2,3},{3,2},{4,5},{5,4},{6,7},{7,6},{8,9},{9,8},{10,11... | collective-permute-start | bytes 48392 | tf_op jit(solution)/shard_map/ppermute | solution.py:33
  45.4 29.1 %copy-start.1 = (f32[42,96]{1,0:T(8,128)}, f32[42,96]{1,0:T(8,128)S(1)}, u32[]{:S(2)}) copy-start(f32[42,96]{1,0:T(8,128)S(1)} %collective-permute-done.1) | copy-start | bytes 48388
  56.9 8.0 %all-to-all-start.2 = ((bf16[4,128,96]{1,2,0:T(8,128)(2,1)}), bf16[4,128,96]{1,2,0:T(8,128)(2,1)S(1)}, u32[]{:S(2)}, u32[]{:S(2)}) async-start(bf16[4,128,96]{1,2,0:T(8,128)(2,1)} %broadcast_in_dim.87), calls=%async_computation.2 | async-start | bytes 196608 | tf_op jit(solution)/shard_map/all_to_all | solution.py:25
  69.9 4.6 %copy-start.4 = (s32[192]{0:T(256)S(1)}, s32[192]{0:T(256)}, u32[]{:S(2)}) copy-start(s32[192]{0:T(256)} %param.13) | copy-start | bytes 2308
  70.9 15.8 %all-to-all-start.3 = ((bf16[8,640,96]{1,2,0:T(8,128)(2,1)}), bf16[8,640,96]{1,2,0:T(8,128)(2,1)S(1)}, u32[]{:S(2)}, u32[]{:S(2)}) async-start(bf16[8,640,96]{1,2,0:T(8,128)(2,1)} %bitcast.101), calls=%async_computation.3 | async-start | bytes 1966080 | tf_op jit(solution)/shard_map/all_to_all | solution.py:25
  74.5 18.0 %slice-start = ((f32[42,96]{1,0:T(8,128)}), f32[40,96]{1,0:T(8,128)S(1)}, s32[]{:S(2)}) async-start(f32[42,96]{1,0:T(8,128)} %copy-done.1), calls=%async_computation.8 | async-start | bytes 40960 | tf_op jit(solution)/shard_map/slice | solution.py:77
  87.8 17.5 %all-to-all-start.4 = ((f32[8,80,96]{2,1,0:T(8,128)}), f32[8,80,96]{2,1,0:T(8,128)S(1)}, u32[]{:S(2)}, u32[]{:S(2)}) async-start(f32[8,80,96]{2,1,0:T(8,128)} %bitcast.30), calls=%async_computation.4 | async-start | bytes 655360 | tf_op jit(solution)/shard_map/all_to_all | solution.py:25
  92.6 12.7 %collective-permute-start.3 = (f32[80,96]{1,0:T(8,128)S(1)}, f32[80,96]{1,0:T(8,128)S(1)}, u32[]{:S(2)}, u32[]{:S(2)}) collective-permute-start(f32[80,96]{1,0:T(8,128)S(1)} %fusion.7), channel_id=1, source_target_pairs={{0,0},{4,8},{8,16},{12,24},{16,4},{20,12},{24,20},{28,28},{1,1},{5... | collective-permute-start | bytes 92168 | tf_op jit(solution)/shard_map/ppermute | solution.py:39
  126.2 15.0 %all-to-all-start.6 = ((bf16[8,640,96]{1,2,0:T(8,128)(2,1)}), bf16[8,640,96]{1,2,0:T(8,128)(2,1)S(1)}, u32[]{:S(2)}, u32[]{:S(2)}) async-start(bf16[8,640,96]{1,2,0:T(8,128)(2,1)} %broadcast_in_dim.91), calls=%async_computation.6 | async-start | bytes 1966080 | tf_op jit(solution)/shard_map/all_to_all | solution.py:25
  148.0 16.9 %all-to-all-start.7 = ((f32[8,64,96]{2,1,0:T(8,128)}), f32[8,64,96]{2,1,0:T(8,128)S(1)}, u32[]{:S(2)}, u32[]{:S(2)}) async-start(f32[8,64,96]{2,1,0:T(8,128)} %bitcast_select_fusion), calls=%async_computation.7 | async-start | bytes 524288 | tf_op jit(solution)/shard_map/all_to_all | solution.py:25
  156.8 10.8 %collective-permute-start.5 = (bf16[5120,96]{0,1:T(8,128)(2,1)S(1)}, bf16[5120,96]{0,1:T(8,128)(2,1)S(1)}, u32[]{:S(2)}, u32[]{:S(2)}) collective-permute-start(bf16[5120,96]{0,1:T(8,128)(2,1)S(1)} %copy.37), channel_id=1, source_target_pairs={{0,1},{1,0},{2,3},{3,2},{4,5},{5,4},{6,7},{7,6},{8,9},{9,8},{10,11... | collective-permute-start | bytes 2949128 | tf_op jit(solution)/shard_map/ppermute | solution.py:33
  158.7 6.8 %collective-permute-start.4 = (f32[64,96]{1,0:T(8,128)}, f32[64,96]{1,0:T(8,128)}, u32[]{:S(2)}, u32[]{:S(2)}) collective-permute-start(f32[64,96]{1,0:T(8,128)} %get-tuple-element.10), channel_id=1, source_target_pairs={{0,1},{1,0},{2,3},{3,2},{4,5},{5,4},{6,7},{7,6},{8,9},{9,8},{10,11... | collective-permute-start | bytes 73736 | tf_op jit(solution)/shard_map/ppermute | solution.py:33

commit v3 on v2

v3 whole, which is shorter than its diff:
```python
import functools

import jax
import jax.numpy as jnp
from jax import lax
from jax.experimental import pallas as pl
from jax.experimental.pallas import tpu as pltpu
from jax.sharding import Mesh, PartitionSpec as P

F32 = jnp.float32
BF16 = jnp.bfloat16
NEAR = ("x", "zl")
FAR = ("zh", "yh")
ANY = pl.BlockSpec(memory_space=pl.ANY)
VMEM = pl.BlockSpec(memory_space=pltpu.VMEM)
MIB = 1 << 20


def dot(left, right, dims):
    return lax.dot_general(left, right, (dims, ((), ())), preferred_element_type=F32)


def size_of(axes):
    count = 1
    for name in axes:
        count *= lax.axis_size(name)
    return count


def exchange(blocks, axes):
    return lax.all_to_all(blocks, axes, 0, 0, tiled=True)


def swap(block):
    return lax.ppermute(block, "core", [(0, 1), (1, 0)])


def to_owner(block):
    high, low = lax.axis_size("zh"), lax.axis_size("zl")
    pairs = [(a * high + b, b * low + a) for a in range(low) for b in range(high)]
    return lax.ppermute(block, ("zh", "zl"), pairs)


def call(kernel, outs, operands, later=(), mib=16, flops=0):
    def run(*refs):
        kernel(*refs[: len(operands)], *refs[len(operands) + len(later) :])

    size = sum(o.size * o.dtype.itemsize for o in list(outs) + list(operands))
    return pl.pallas_call(
        run,
        out_shape=outs,
        in_specs=[VMEM] * len(operands) + [ANY] * len(later),
        out_specs=[VMEM] * len(outs),
        compiler_params=pltpu.CompilerParams(vmem_limit_bytes=mib * MIB),
        cost_estimate=pl.CostEstimate(flops=flops, bytes_accessed=size, transcendentals=0),
    )(*operands, *later)


def struct(shape, dtype):
    return jax.ShapeDtypeStruct(shape, dtype)


def flip_kernel(block_ref, out_ref):
    block = block_ref[...].astype(F32).T.astype(BF16)
    for k in range(out_ref.shape[0]):
        out_ref[k] = block


def encode_kernel(sizes, blocks_ref, own_ref, sent_ref, own_bias, sent_bias, whole_ref, code_ref, own_slope, sent_slope):
    xs, zh, zl, rest = sizes
    for x in range(xs):
        parts = [
            blocks_ref[x * zl + low, :, high * rest : (high + 1) * rest] for high in range(zh) for low in range(zl)
        ]
        width = len(parts) * rest
        whole_ref[:, x * width : (x + 1) * width] = jnp.concatenate(parts, axis=1)
    whole = whole_ref[...]
    codes = []
    for part, bias, slope in ((own_ref, own_bias, own_slope), (sent_ref, sent_bias, sent_slope)):
        shifted = dot(part[...], whole, ((1,), (1,))) - bias[...]
        sig = jax.nn.sigmoid(4.0 * shifted)
        slope[...] = sig + 4.0 * shifted * sig * (1.0 - sig)
        codes.append(shifted * sig)
    code = jnp.concatenate(codes, axis=0).T.astype(BF16)
    for layer in range(code_ref.shape[0]):
        code_ref[layer] = code


def decode_kernel(codes_ref, own_ref, sent_ref, out_ref):
    section = lax.axis_index("layer")
    layers, _, latents = codes_ref.shape
    latents //= 2
    codes = []
    for layer in range(layers):
        code = codes_ref[layer]
        codes.append(jnp.where(layer <= section, code, jnp.zeros_like(code)))
    own = jnp.concatenate([code[:, :latents] for code in codes], axis=1)
    sent = jnp.concatenate([code[:, latents:] for code in codes], axis=1)
    count, _, width = out_ref.shape
    for k in range(count):
        part = slice(k * width, (k + 1) * width)
        total = dot(own, own_ref[:, part], ((1,), (0,))) + dot(sent, sent_ref[:, part], ((1,), (0,)))
        out_ref[k] = total.astype(BF16)


def reduce_kernel(rows, parts_ref, offset_ref, out_ref):
    total = -offset_ref[...]
    for k in range(parts_ref.shape[0]):
        total += parts_ref[k].astype(F32)
    for k in range(out_ref.shape[0]):
        out_ref[k, :rows] = total[k * rows : (k + 1) * rows]
        if rows < out_ref.shape[1]:
            out_ref[k, rows:] = jnp.zeros((out_ref.shape[1] - rows, out_ref.shape[2]), F32)


def error_kernel(scale, parts_ref, mask_ref, out_ref):
    total = parts_ref[0]
    for k in range(1, parts_ref.shape[0]):
        total += parts_ref[k]
    error = (mask_ref[...] * total * scale).astype(BF16)
    for k in range(out_ref.shape[0]):
        out_ref[k] = error


def repeat_kernel(rows, parts_ref, out_ref):
    parts = [parts_ref[k].astype(F32)[:rows] for k in range(parts_ref.shape[0])]
    block = jnp.concatenate(parts, axis=0).astype(BF16)
    for k in range(out_ref.shape[0]):
        out_ref[k] = block


def back_kernel(error_ref, own_ref, sent_ref, out_ref):
    section = lax.axis_index("layer")
    first = lax.axis_index("core") == 0
    error = jnp.concatenate([error_ref[k] for k in range(error_ref.shape[0])], axis=1)
    own = dot(own_ref[...], error, ((1,), (1,)))
    sent = dot(sent_ref[...], error, ((1,), (1,)))
    latents = out_ref.shape[1]
    for layer in range(out_ref.shape[0] // 2):
        rows = slice(layer * latents, (layer + 1) * latents)
        kept = (layer <= section).astype(F32)
        out_ref[2 * layer] = jnp.where(first, own[rows], sent[rows]) * kept
        out_ref[2 * layer + 1] = jnp.where(first, sent[rows], own[rows]) * kept


def final_kernel(terms_ref, own_slope, sent_slope, own_ref, sent_ref, grad_ref, threshold_ref):
    first = lax.axis_index("core") == 0
    low, high = terms_ref[0], terms_ref[1]
    for k in range(2, terms_ref.shape[0], 2):
        low += terms_ref[k]
        high += terms_ref[k + 1]
    own = jnp.where(first, low, high) * own_slope[...]
    sent = jnp.where(first, high, low) * sent_slope[...]
    total = -jnp.sum(own + sent, axis=1, keepdims=True)
    threshold_ref[...] = jnp.broadcast_to(total, (total.shape[0], 128)).T[:1]
    grad = dot(own.astype(BF16), own_ref[...], ((1,), (0,)))
    grad_ref[...] = grad + dot(sent.astype(BF16), sent_ref[...], ((1,), (0,)))


def body(inputs, targets, encoder, threshold, decoders, out_bias, positions):
    layers = lax.axis_size("layer")
    first = lax.axis_index("core") == 0
    width, tokens = inputs.shape[2], inputs.shape[1]
    half = tokens // 2
    latents, model = encoder.shape[1], encoder.shape[2]
    xs, zh, zl, yh = (lax.axis_size(name) for name in ("x", "zh", "zl", "yh"))
    near, far = xs * zl, zh * yh
    wide, rows = model // near, half // far
    tall = -(-rows // 16) * 16
    place = lax.axis_index(FAR)

    def halves(array):
        return jnp.stack([array[:, :half], array[:, half:]])

    def mine(pair):
        return jnp.where(first, pair[0], pair[1])

    def other(pair):
        return jnp.where(first, pair[1], pair[0])

    input_halves = halves(inputs[0].T)
    sends = jnp.broadcast_to(input_halves[None], (far,) + input_halves.shape)
    block = exchange(sends.reshape((-1, width, half)), FAR + ("core",)).reshape(-1, half)

    def row(vector):
        return jnp.pad(vector.astype(F32), (0, half - vector.shape[0]))[None]

    target_halves = halves(targets[0].T).astype(F32)
    sides = jnp.concatenate([row(out_bias[0]), row(threshold[0])], axis=0)
    received = swap(jnp.concatenate([other(target_halves), sides], axis=0))
    other_encoder = swap(encoder[0])
    own_decoders = decoders[0].reshape(layers * latents, model)
    other_decoders = swap(own_decoders)
    other_threshold = received[width + 1, :latents]

    def both(own, sent):
        return jnp.where(first, jnp.concatenate([own, sent], axis=0), jnp.concatenate([sent, own], axis=0))

    own_targets = both(mine(target_halves), received[:width])
    own_bias = both(out_bias[0].astype(F32), received[width, :width])
    offset = to_owner(own_targets - own_bias[:, None])

    (sends,) = call(
        flip_kernel, [struct((near, half, wide), BF16)], [block], later=[received, other_encoder, other_decoders]
    )
    blocks = exchange(sends, NEAR)
    tile = jnp.tile(offset.T, (1, far))
    lane = lax.broadcasted_iota(jnp.int32, tile.shape, 1) // (2 * width)
    offset = jnp.where(lane == place, tile, jnp.zeros_like(tile))
    token_mask = (positions > 0).astype(F32)
    start = lax.axis_index("core") * half + place * rows
    own_mask = jnp.pad(lax.dynamic_slice(token_mask, (start,), (rows,)), (0, tall - rows))[:, None]

    whole, codes, own_slope, sent_slope = call(
        functools.partial(encode_kernel, (xs, zh, zl, wide // zh)),
        [
            struct((half, model), BF16),
            struct((layers, half, 2 * latents), BF16),
            struct((latents, half), F32),
            struct((latents, half), F32),
        ],
        [blocks, encoder[0], other_encoder, threshold[0][:, None], other_threshold[:, None]],
        flops=4 * half * latents * model,
    )
    codes = exchange(codes, ("layer",))
    other_whole = swap(whole)
    other_slope = swap(sent_slope)

    (parts,) = call(
        decode_kernel,
        [struct((near, half, wide), BF16)],
        [codes, own_decoders, other_decoders],
        flops=4 * layers * half * latents * model,
    )
    parts = exchange(parts, NEAR)
    (parts,) = call(
        functools.partial(reduce_kernel, rows),
        [struct((far, tall, wide), F32)],
        [parts, offset],
        later=[other_whole, other_slope],
    )
    parts = exchange(parts, FAR)
    (parts,) = call(
        functools.partial(error_kernel, 1.0 / layers), [struct((far, tall, wide), BF16)], [parts, own_mask]
    )
    parts = exchange(parts, FAR)
    (parts,) = call(functools.partial(repeat_kernel, rows), [struct((near, half, wide), BF16)], [parts])
    error = exchange(parts, NEAR)
    (terms,) = call(
        back_kernel,
        [struct((2 * layers, latents, half), F32)],
        [error, own_decoders, other_decoders],
        flops=4 * layers * half * latents * model,
    )
    terms = exchange(terms, ("layer", "core"))
    grad_encoder, grad_threshold = call(
        final_kernel,
        [struct((latents, model), F32), struct((1, latents), F32)],
        [terms, own_slope, other_slope, whole, other_whole],
        flops=4 * half * latents * model,
    )
    return (grad_encoder[None], grad_threshold)


LATENT = ("x", "zh", "zl", "yh", "core")


def solution(mesh, parts=(4, 4, 2, 2, 2)):
    in_specs = (
        P("layer", None, LATENT),
        P("layer", None, LATENT),
        P("layer", LATENT, None),
        P("layer", LATENT),
        P("layer", None, LATENT, None),
        P("layer", LATENT),
        P(),
    )
    out_specs = (P("layer", LATENT, None), P("layer", LATENT))
    devices = mesh.devices.reshape((mesh.devices.shape[0],) + parts)
    fine = Mesh(devices, ("layer",) + LATENT)
    return jax.shard_map(body, mesh=fine, in_specs=in_specs, out_specs=out_specs, check_vma=False)
```

time: 170 us -> 169 us (level)
  matrix products: 14.9 us -> 0 us
  waiting for transfers between devices: 51.5 us -> 38.3 us
  blocking collectives: 49.7 us -> 60 us
  Pallas kernels: 0 us -> 9.9 us
  starting transfers between devices: 39.8 us -> 49.1 us
  other arithmetic: 3.47 us -> 0.9 us
    dot_general x8 -> x0, matrix products: 14.9 us -> none  [the longest x2 5.14 us: back(): lax.dot_general(part, error_full, (((2,), (0,)), ((), ())), preferred_ele...]
    all_to_all x6 -> x4, waiting for transfers between devices: 50.5 us -> 36.3 us  [exchange(): return lax.all_to_all(blocks, axes, 0, 0, tiled=True)]
    all_to_all x2 -> x4, blocking collectives: 49.7 us -> 60 us  [exchange(): return lax.all_to_all(blocks, axes, 0, 0, tiled=True)]
    pallas_call x0 -> x8, Pallas kernels: none -> 9.9 us  [call(): pl.pallas_call(run, out_shape=outs, in_specs=[VMEM] * len(operands) + [AN...]
    ppermute x5, starting transfers between devices: 11 us -> 19.7 us  [swap(): return lax.ppermute(block, 'core', [(0, 1), (1, 0)])]
    unnamed x12 -> x18, local copies, waits for them, and re-layouts: 0.03 us -> 5.7 us
    broadcast_in_dim x9 -> x3, local copies, waits for them, and re-layouts: 3.22 us -> 0.78 us  [the longest x1 0.69 us: body(): sends = jnp.broadcast_to(input_halves[None], (far,) + input_halves.shape)]
    reshape x3 -> x0, local copies, waits for them, and re-layouts: 2.07 us -> none  [the longest x1 1.03 us: body(): recon = exchange(recon.astype(BF16).reshape(xs * zl, -1, half), NEAR)]
  transfers between devices with their start and end apart: 12 -> 10, of which waited for: 7 -> 6; matrix products, arithmetic and copies ran while one was open for 7% -> 3% of each run, Pallas kernels for 0% -> 0%
where the time goes in v3:
time: 169 us; the launch traced here: 168 us
  blocking collectives  60 us (36%)
  starting transfers between devices  49.1 us (29%)
  waiting for transfers between devices  38.3 us (23%)
  Pallas kernels  9.9 us (6%)
  local copies, waits for them, and re-layouts  9.36 us (6%)
    all_to_all x4, blocking collectives, exchange(): return lax.all_to_all(blocks, axes, 0, 0, tiled=True)  60 us
    all_to_all x4, waiting for transfers between devices, exchange(): return lax.all_to_all(blocks, axes, 0, 0, tiled=True)  36.3 us
    all_to_all x4, starting transfers between devices, exchange(): return lax.all_to_all(blocks, axes, 0, 0, tiled=True)  28.7 us
    ppermute x5, starting transfers between devices, swap(): return lax.ppermute(block, 'core', [(0, 1), (1, 0)])  19.7 us
    pallas_call x8, Pallas kernels, call(): pl.pallas_call(run, out_shape=outs, in_specs=[VMEM] * len(operands) + [AN...  9.9 us
    unnamed x18, local copies, waits for them, and re-layouts  5.7 us
  transfers between devices with their start and end apart: 10, of which 6 were waited for; matrix products, arithmetic and copies ran while one was open for 3% of the time, Pallas kernels for 0%

profile of v3, /device:TPU:1, one launch (start us, length us, event | category | flops | bytes accessed | tf_op | source)
XLA Modules:
  0.0 168.4 jit_solution(11586744024801353768)
XLA Ops:
  0.6 8.8 %collective-permute-start.2 = (bf16[256,5120]{1,0:T(8,128)(2,1)}, bf16[256,5120]{1,0:T(8,128)(2,1)S(1)}, u32[]{:S(2)}, u32[]{:S(2)}) collective-permute-start(bf16[256,5120]{1,0:T(8,128)(2,1)} %bitcast.40), channel_id=1, source_target_pairs={{0,1},{1,0},{2,3},{3,2},{4,5},{5,4},{6,7},{7,6},{8,9},{9,8},{10,11... | collective-permute-start | bytes 7864328 | tf_op jit(solution)/shard_map/ppermute | solution.py:35
  9.4 0.9 slice_bitcast_fusion.3
  10.3 0.7 broadcast_in_dim.22
  11.0 10.3 %all-to-all-start = ((bf16[16,40,96]{2,1,0:T(8,128)(2,1)}), bf16[16,40,96]{2,1,0:T(8,128)(2,1)S(1)}, u32[]{:S(2)}, u32[]{:S(2)}) async-start(bf16[16,40,96]{2,1,0:T(8,128)(2,1)} %bitcast.5), calls=%async_computation | async-start | bytes 327680 | tf_op jit(solution)/shard_map/all_to_all | solution.py:31
  21.3 2.0 %collective-permute-start.1 = (bf16[64,5120]{1,0:T(8,128)(2,1)}, bf16[64,5120]{1,0:T(8,128)(2,1)S(1)}, u32[]{:S(2)}, u32[]{:S(2)}) collective-permute-start(bf16[64,5120]{1,0:T(8,128)(2,1)} %bitcast.44), channel_id=1, source_target_pairs={{0,1},{1,0},{2,3},{3,2},{4,5},{5,4},{6,7},{7,6},{8,9},{9,8},{10,11... | collective-permute-start | bytes 1966088 | tf_op jit(solution)/shard_map/ppermute | solution.py:35
  23.4 0.9 slice_bitcast_fusion.1
  24.2 0.7 bitcast_convert_fusion
  24.9 0.7 pad_bitcast_fusion.1
  25.6 2.3 %collective-permute-start = (f32[42,96]{1,0:T(8,128)S(1)}, f32[42,96]{1,0:T(8,128)S(1)}, u32[]{:S(2)}, u32[]{:S(2)}) collective-permute-start(f32[42,96]{1,0:T(8,128)S(1)} %pad_maximum_fusion), channel_id=1, source_target_pairs={{0,1},{1,0},{2,3},{3,2},{4,5},{5,4},{6,7},{7,6},{8,9},{9,8},{10,11... | collective-permute-start | bytes 48392 | tf_op jit(solution)/shard_map/ppermute | solution.py:35
  27.9 0.8 collective-permute-done.refs_1_
  28.7 5.6 %all-to-all-done = bf16[16,40,96]{2,1,0:T(8,128)(2,1)S(1)} async-done(((bf16[16,40,96]{2,1,0:T(8,128)(2,1)}), bf16[16,40,96]{2,1,0:T(8,128)(2,1)S(1)}, u32[]{:S(2)}, u32[]{:S(2)}) %all-to-all-start) | async-done | bytes 122912 | tf_op jit(solution)/shard_map/all_to_all | solution.py:31
  34.3 0.0 collective-permute-done.1.refs_2_
  34.3 0.0 collective-permute-done.2.refs_3_.refs_2_
  34.3 0.0 copy-start.7
  34.3 0.1 shard_map.86
  34.5 0.0 copy-start.3
  34.5 0.9 copy-done.3
  35.4 4.7 %all-to-all-start.1 = ((bf16[8,96,640]{2,1,0:T(8,128)(2,1)}), bf16[8,96,640]{2,1,0:T(8,128)(2,1)}, u32[]{:S(2)}, u32[]{:S(2)}) async-start(bf16[8,96,640]{2,1,0:T(8,128)(2,1)} %copy-done.3), calls=%async_computation.1 | async-start | bytes 1966080 | tf_op jit(solution)/shard_map/all_to_all | solution.py:31
  40.2 0.0 copy-done.7
  40.2 0.1 copy.13.refs_3_
  40.3 0.1 copy.14.refs_4_
  40.4 14.6 %all-to-all-done.1.refs_0_ = bf16[8,96,640]{2,1,0:T(8,128)(2,1)} async-done(((bf16[8,96,640]{2,1,0:T(8,128)(2,1)}), bf16[8,96,640]{2,1,0:T(8,128)(2,1)}, u32[]{:S(2)}, u32[]{:S(2)}) %all-to-all-start.1) | async-done | bytes 983072 | tf_op jit(solution)/shard_map/all_to_all | solution.py:31
  54.9 0.0 copy-start.6
  54.9 1.1 copy-done.6
  56.0 2.2 %shard_map.87 = (bf16[96,5120]{1,0:T(8,128)(2,1)S(1)}, bf16[4,96,128]{2,1,0:T(8,128)(2,1)S(1)}, f32[64,96]{1,0:T(8,128)S(1)}, f32[64,96]{1,0:T(8,128)S(1)}) custom-call(bf16[8,96,640]{2,1,0:T(8,128)(2,1)} %all-to-all-done.1.refs_0_, bf16[64,5120]{1,0:T(8,128)(2,1)S(1)} %bitcast.45, bf16[64,5120]{1,0:T(8,128)(2,1)S(1)} %collective-permute-done.1.refs_2_, ...), custom_call_target="tpu_custom_call" | custom-call | flops 125829120 | bytes 3424768 | tf_op jit(solution)/shard_map/pallas_call | solution.py:49
  58.2 0.0 copy-start.4
  58.2 1.0 copy-done.4
  59.2 7.8 %all_to_all.40.refs_0_ = bf16[4,96,128]{2,1,0:T(8,128)(2,1)S(1)} all-to-all(bf16[4,96,128]{2,1,0:T(8,128)(2,1)S(1)} %get-tuple-element.8), channel_id=1, replica_groups=mesh['layer'=4,'x'=4,'zh'=4,'zl'=2,'yh'=2,'core'=2] {'layer'}, dimensions={0} | all-to-all | bytes 196608 | tf_op jit(solution)/shard_map/all_to_all | solution.py:31
  67.0 0.0 copy-start
  67.0 1.7 %copy-done = bf16[1,4,64,5120]{3,2,1,0:T(8,128)(2,1)S(1)} copy-done((bf16[1,4,64,5120]{3,2,1,0:T(8,128)(2,1)S(1)}, bf16[1,4,64,5120]{3,2,1,0:T(8,128)(2,1)}, u32[]{:S(2)}) %copy-start) | copy-done | bytes 2621464
  68.7 1.1 shard_map.88
  69.8 0.0 copy-start.2
  69.8 0.9 copy-done.2
  70.8 4.2 %all-to-all-start.3 = ((bf16[8,96,640]{2,1,0:T(8,128)(2,1)}), bf16[8,96,640]{2,1,0:T(8,128)(2,1)}, u32[]{:S(2)}, u32[]{:S(2)}) async-start(bf16[8,96,640]{2,1,0:T(8,128)(2,1)} %copy-done.2), calls=%async_computation.3 | async-start | bytes 1966080 | tf_op jit(solution)/shard_map/all_to_all | solution.py:31
  75.0 0.0 copy-start.8
  75.0 4.7 %collective-permute-start.4 = (bf16[96,5120]{1,0:T(8,128)(2,1)}, bf16[96,5120]{1,0:T(8,128)(2,1)}, u32[]{:S(2)}, u32[]{:S(2)}) collective-permute-start(bf16[96,5120]{1,0:T(8,128)(2,1)} %copy-done.4), channel_id=1, source_target_pairs={{0,1},{1,0},{2,3},{3,2},{4,5},{5,4},{6,7},{7,6},{8,9},{9,8},{10,11... | collective-permute-start | bytes 2949128 | tf_op jit(solution)/shard_map/ppermute | solution.py:35
  79.7 0.1 broadcast_select_fusion
  79.8 0.1 fusion.1
  79.9 0.7 collective-permute-start.3
  80.6 0.0 collective-permute-done.3
  80.6 0.2 copy.15
  80.8 1.9 %collective-permute-start.5 = (f32[64,96]{1,0:T(8,128)S(1)}, f32[64,96]{1,0:T(8,128)S(1)}, u32[]{:S(2)}, u32[]{:S(2)}) collective-permute-start(f32[64,96]{1,0:T(8,128)S(1)} %get-tuple-element.10), channel_id=1, source_target_pairs={{0,1},{1,0},{2,3},{3,2},{4,5},{5,4},{6,7},{7,6},{8,9},{9,8},{10,11... | collective-permute-start | bytes 73736 | tf_op jit(solution)/shard_map/ppermute | solution.py:35
  82.7 1.1 collective-permute-done.5.refs_3_.refs_2_
  83.9 0.0 collective-permute-done.4.refs_2_.refs_4_
  83.9 3.5 %all-to-all-done.3.refs_0_ = bf16[8,96,640]{2,1,0:T(8,128)(2,1)} async-done(((bf16[8,96,640]{2,1,0:T(8,128)(2,1)}), bf16[8,96,640]{2,1,0:T(8,128)(2,1)}, u32[]{:S(2)}, u32[]{:S(2)}) %all-to-all-start.3) | async-done | bytes 983072 | tf_op jit(solution)/shard_map/all_to_all | solution.py:31
  87.4 2.1 %shard_map.89 = f32[8,16,640]{2,1,0:T(8,128)} custom-call(bf16[8,96,640]{2,1,0:T(8,128)(2,1)} %all-to-all-done.3.refs_0_, f32[96,640]{1,0:T(8,128)S(1)} %fusion.refs_1_, bf16[96,5120]{1,0:T(8,128)(2,1)} %collective-permute-done.4.refs_2_.refs_4_, f32[64,96]{1,0:T(8,128)S(1)} %collective-permute-done.5.refs_3_.refs_2_), custom_call_target="tpu_custom_call" | custom-call | bytes 1556480 | tf_op jit(solution)/shard_map/pallas_call | solution.py:49
  89.4 9.4 %all-to-all-start.4 = ((f32[8,16,640]{2,1,0:T(8,128)}), f32[8,16,640]{2,1,0:T(8,128)S(1)}, u32[]{:S(2)}, u32[]{:S(2)}) async-start(f32[8,16,640]{2,1,0:T(8,128)} %shard_map.89), calls=%async_computation.4 | async-start | bytes 655360 | tf_op jit(solution)/shard_map/all_to_all | solution.py:31
  98.9 0.0 copy-done.8
  98.9 0.1 dynamic_slice.3
  99.0 0.1 copy.16.refs_1_
  99.1 12.7 %all-to-all-done.4.refs_0_ = f32[8,16,640]{2,1,0:T(8,128)S(1)} async-done(((f32[8,16,640]{2,1,0:T(8,128)}), f32[8,16,640]{2,1,0:T(8,128)S(1)}, u32[]{:S(2)}, u32[]{:S(2)}) %all-to-all-start.4) | async-done | bytes 327712 | tf_op jit(solution)/shard_map/all_to_all | solution.py:31
  111.8 0.0 copy-start.1
  111.8 0.1 shard_map.90
  111.9 17.7 %all_to_all.41.refs_0_ = bf16[8,16,640]{2,1,0:T(8,128)(2,1)S(1)} all-to-all(bf16[8,16,640]{2,1,0:T(8,128)(2,1)S(1)} %shard_map.90), channel_id=1, replica_groups=mesh['layer'=4,'x'=4,'zh'=4,'zl'=2,'yh'=2,'core'=2] {'zh','yh'}, dimensions={0} | all-to-all | bytes 327680 | tf_op jit(solution)/shard_map/all_to_all | solution.py:31
  129.6 0.1 shard_map.91
  129.7 18.8 %all_to_all.42.refs_0_ = bf16[8,96,640]{2,1,0:T(8,128)(2,1)S(1)} all-to-all(bf16[8,96,640]{2,1,0:T(8,128)(2,1)S(1)} %shard_map.91), channel_id=1, replica_groups=mesh['layer'=4,'x'=4,'zh'=4,'zl'=2,'yh'=2,'core'=2] {'x','zl'}, dimensions={0} | all-to-all | bytes 1966080 | tf_op jit(solution)/shard_map/all_to_all | solution.py:31
  148.5 0.0 copy-done.1
  148.5 0.0 copy-start.5
  148.5 1.5 shard_map.92
  150.0 15.7 %all_to_all.43.refs_0_ = f32[8,64,96]{2,1,0:T(8,128)S(1)} all-to-all(f32[8,64,96]{2,1,0:T(8,128)S(1)} %shard_map.92), channel_id=1, replica_groups=mesh['layer'=4,'x'=4,'zh'=4,'zl'=2,'yh'=2,'core'=2] {'layer','core'}, dimensions={0} | all-to-all | bytes 393216 | tf_op jit(solution)/shard_map/all_to_all | solution.py:31
  165.7 0.0 copy-done.5
  165.7 2.7 %shard_map.93 = (f32[64,5120]{1,0:T(8,128)}, f32[1,64]{1,0:T(1,128)}) custom-call(f32[8,64,96]{2,1,0:T(8,128)S(1)} %all_to_all.43.refs_0_, f32[64,96]{1,0:T(8,128)S(1)} %get-tuple-element.11.refs_1_, f32[64,96]{1,0:T(8,128)S(1)} %collective-permute-done.5.refs_3_.refs_2_, bf16[96,5120]{1,0:T(8,128)(2,1)S(1)} %copy-done.5, ...), custom_call_target="tpu_custom_call" | custom-call | flops 125829120 | bytes 3522816 | tf_op jit(solution)/shard_map/pallas_call | solution.py:49
  (13 shorter events, 0.1 us)
Async XLA Ops:
  0.6 33.7 %collective-permute-start.2 = (bf16[256,5120]{1,0:T(8,128)(2,1)}, bf16[256,5120]{1,0:T(8,128)(2,1)S(1)}, u32[]{:S(2)}, u32[]{:S(2)}) collective-permute-start(bf16[256,5120]{1,0:T(8,128)(2,1)} %bitcast.40), channel_id=1, source_target_pairs={{0,1},{1,0},{2,3},{3,2},{4,5},{5,4},{6,7},{7,6},{8,9},{9,8},{10,11... | collective-permute-start | bytes 7864328 | tf_op jit(solution)/shard_map/ppermute | solution.py:35
  11.0 23.3 %all-to-all-start = ((bf16[16,40,96]{2,1,0:T(8,128)(2,1)}), bf16[16,40,96]{2,1,0:T(8,128)(2,1)S(1)}, u32[]{:S(2)}, u32[]{:S(2)}) async-start(bf16[16,40,96]{2,1,0:T(8,128)(2,1)} %bitcast.5), calls=%async_computation | async-start | bytes 327680 | tf_op jit(solution)/shard_map/all_to_all | solution.py:31
  21.3 13.0 %collective-permute-start.1 = (bf16[64,5120]{1,0:T(8,128)(2,1)}, bf16[64,5120]{1,0:T(8,128)(2,1)S(1)}, u32[]{:S(2)}, u32[]{:S(2)}) collective-permute-start(bf16[64,5120]{1,0:T(8,128)(2,1)} %bitcast.44), channel_id=1, source_target_pairs={{0,1},{1,0},{2,3},{3,2},{4,5},{5,4},{6,7},{7,6},{8,9},{9,8},{10,11... | collective-permute-start | bytes 1966088 | tf_op jit(solution)/shard_map/ppermute | solution.py:35
  25.6 3.1 %collective-permute-start = (f32[42,96]{1,0:T(8,128)S(1)}, f32[42,96]{1,0:T(8,128)S(1)}, u32[]{:S(2)}, u32[]{:S(2)}) collective-permute-start(f32[42,96]{1,0:T(8,128)S(1)} %pad_maximum_fusion), channel_id=1, source_target_pairs={{0,1},{1,0},{2,3},{3,2},{4,5},{5,4},{6,7},{7,6},{8,9},{9,8},{10,11... | collective-permute-start | bytes 48392 | tf_op jit(solution)/shard_map/ppermute | solution.py:35
  34.3 5.8 %copy-start.7 = (f32[1,64]{1,0:T(1,128)S(1)}, f32[1,64]{1,0:T(1,128)}, u32[]{:S(2)}) copy-start(f32[1,64]{1,0:T(1,128)} %param.10) | copy-start | bytes 772
  34.5 0.9 copy-start.3
  35.4 19.5 %all-to-all-start.1 = ((bf16[8,96,640]{2,1,0:T(8,128)(2,1)}), bf16[8,96,640]{2,1,0:T(8,128)(2,1)}, u32[]{:S(2)}, u32[]{:S(2)}) async-start(bf16[8,96,640]{2,1,0:T(8,128)(2,1)} %copy-done.3), calls=%async_computation.1 | async-start | bytes 1966080 | tf_op jit(solution)/shard_map/all_to_all | solution.py:31
  54.9 1.1 copy-start.6
  58.2 1.0 copy-start.4
  67.0 1.7 %copy-start = (bf16[1,4,64,5120]{3,2,1,0:T(8,128)(2,1)S(1)}, bf16[1,4,64,5120]{3,2,1,0:T(8,128)(2,1)}, u32[]{:S(2)}) copy-start(bf16[1,4,64,5120]{3,2,1,0:T(8,128)(2,1)} %param.11) | copy-start | bytes 7864324
  69.8 1.0 copy-start.2
  70.8 16.6 %all-to-all-start.3 = ((bf16[8,96,640]{2,1,0:T(8,128)(2,1)}), bf16[8,96,640]{2,1,0:T(8,128)(2,1)}, u32[]{:S(2)}, u32[]{:S(2)}) async-start(bf16[8,96,640]{2,1,0:T(8,128)(2,1)} %copy-done.2), calls=%async_computation.3 | async-start | bytes 1966080 | tf_op jit(solution)/shard_map/all_to_all | solution.py:31
  75.0 23.9 %copy-start.8 = (s32[192]{0:T(256)S(1)}, s32[192]{0:T(256)}, u32[]{:S(2)}) copy-start(s32[192]{0:T(256)} %param.13) | copy-start | bytes 2308
  75.0 8.9 %collective-permute-start.4 = (bf16[96,5120]{1,0:T(8,128)(2,1)}, bf16[96,5120]{1,0:T(8,128)(2,1)}, u32[]{:S(2)}, u32[]{:S(2)}) collective-permute-start(bf16[96,5120]{1,0:T(8,128)(2,1)} %copy-done.4), channel_id=1, source_target_pairs={{0,1},{1,0},{2,3},{3,2},{4,5},{5,4},{6,7},{7,6},{8,9},{9,8},{10,11... | collective-permute-start | bytes 2949128 | tf_op jit(solution)/shard_map/ppermute | solution.py:35
  79.9 0.7 collective-permute-start.3
  80.8 3.1 %collective-permute-start.5 = (f32[64,96]{1,0:T(8,128)S(1)}, f32[64,96]{1,0:T(8,128)S(1)}, u32[]{:S(2)}, u32[]{:S(2)}) collective-permute-start(f32[64,96]{1,0:T(8,128)S(1)} %get-tuple-element.10), channel_id=1, source_target_pairs={{0,1},{1,0},{2,3},{3,2},{4,5},{5,4},{6,7},{7,6},{8,9},{9,8},{10,11... | collective-permute-start | bytes 73736 | tf_op jit(solution)/shard_map/ppermute | solution.py:35
  89.4 22.3 %all-to-all-start.4 = ((f32[8,16,640]{2,1,0:T(8,128)}), f32[8,16,640]{2,1,0:T(8,128)S(1)}, u32[]{:S(2)}, u32[]{:S(2)}) async-start(f32[8,16,640]{2,1,0:T(8,128)} %shard_map.89), calls=%async_computation.4 | async-start | bytes 655360 | tf_op jit(solution)/shard_map/all_to_all | solution.py:31
  111.8 36.7 %copy-start.1 = (bf16[1,4,64,5120]{3,2,1,0:T(8,128)(2,1)S(1)}, bf16[1,4,64,5120]{3,2,1,0:T(8,128)(2,1)}, u32[]{:S(2)}) copy-start(bf16[1,4,64,5120]{3,2,1,0:T(8,128)(2,1)} %param.11) | copy-start | bytes 7864324
  148.5 17.2 %copy-start.5 = (bf16[96,5120]{1,0:T(8,128)(2,1)S(1)}, bf16[96,5120]{1,0:T(8,128)(2,1)}, u32[]{:S(2)}) copy-start(bf16[96,5120]{1,0:T(8,128)(2,1)} %copy-done.4) | copy-start | bytes 2949124

commit v4 on v3

v4 whole, which is shorter than its diff:
```python
import functools

import jax
import jax.numpy as jnp
from jax import lax
from jax.experimental import pallas as pl
from jax.experimental.pallas import tpu as pltpu
from jax.sharding import Mesh, PartitionSpec as P

F32 = jnp.float32
BF16 = jnp.bfloat16
NEAR = ("x", "zl")
FAR = ("zh", "yh")
ANY = pl.BlockSpec(memory_space=pl.ANY)
SMEM = pl.BlockSpec(memory_space=pltpu.SMEM)
VMEM = pl.BlockSpec(memory_space=pltpu.VMEM)
MIB = 1 << 20


def dot(left, right, dims):
    return lax.dot_general(left, right, (dims, ((), ())), preferred_element_type=F32)


def size_of(axes):
    count = 1
    for name in axes:
        count *= lax.axis_size(name)
    return count


def exchange(blocks, axes):
    return lax.all_to_all(blocks, axes, 0, 0, tiled=True)


def swap(block):
    return lax.ppermute(block, "core", [(0, 1), (1, 0)])


def to_owner(block):
    high, low = lax.axis_size("zh"), lax.axis_size("zl")
    pairs = [(a * high + b, b * low + a) for a in range(low) for b in range(high)]
    return lax.ppermute(block, ("zh", "zl"), pairs)


def call(kernel, outs, operands, later=(), scratch=(), scalars=(), remote=(), weights=(), remote_outs=(), mib=16, flops=0):
    def run(*refs):
        kernel(*refs[: len(operands)], *refs[len(operands) + len(later) :])

    size = sum(o.size * o.dtype.itemsize for o in list(outs) + list(operands))
    return pl.pallas_call(
        run,
        out_shape=outs,
        in_specs=[SMEM if k in scalars else ANY if k in remote or k in weights else VMEM for k in range(len(operands))] + [ANY] * len(later),
        out_specs=[ANY if k in remote_outs else VMEM for k in range(len(outs))],
        scratch_shapes=scratch,
        compiler_params=pltpu.CompilerParams(vmem_limit_bytes=mib * MIB),
        cost_estimate=pl.CostEstimate(flops=flops, bytes_accessed=size, transcendentals=0),
    )(*operands, *later)


def start(source, target, semaphore):
    copy = pltpu.make_async_copy(source, target, semaphore)
    copy.start()
    return copy


def columns(count, width):
    return [slice(k * width, (k + 1) * width) for k in range(count)]


def struct(shape, dtype):
    return jax.ShapeDtypeStruct(shape, dtype)


def split_kernel(inputs_ref, targets_ref, bias_ref, threshold_ref, out_ref, own_ref, sent_ref):
    first = lax.axis_index("core") == 0
    width, half = out_ref.shape[1:]
    block = inputs_ref[...].astype(F32)
    low, high = block[:, :half].astype(BF16), block[:, half:].astype(BF16)
    for k in range(0, out_ref.shape[0], 2):
        out_ref[k] = low
        out_ref[k + 1] = high
    block = targets_ref[...].astype(F32)
    low, high = block[:, :half], block[:, half:]
    own_ref[:width, :half] = jnp.where(first, low, high)
    sent_ref[:width, :half] = jnp.where(first, high, low)
    for ref in (own_ref, sent_ref):
        ref[width : width + 1, :width] = bias_ref[...].astype(F32)
        ref[width + 1 : width + 2, : threshold_ref.shape[1]] = threshold_ref[...]


def column(row):
    return jnp.broadcast_to(row, (8, row.shape[1])).T[:, :1]


def offset_kernel(own_ref, sent_ref, out_ref):
    first = lax.axis_index("core") == 0
    width, half = out_ref.shape
    width //= 2
    own, sent = (
        ref[:width, :half] - column(ref[width : width + 1, :])[:width] for ref in (own_ref, sent_ref)
    )
    out_ref[:width] = jnp.where(first, own, sent)
    out_ref[width:] = jnp.where(first, sent, own)


def flip_kernel(block_ref, out_ref):
    block = block_ref[...].astype(F32).T.astype(BF16)
    for k in range(out_ref.shape[0]):
        out_ref[k] = block


def encode_kernel(
    sizes, blocks_hbm, own_hbm, sent_hbm, own_sides, sent_sides, whole_hbm, code_ref, own_slope, sent_slope,
    blocks, own, sent, whole_ref, sems,
):
    copies = [
        start(blocks_hbm, blocks, sems.at[0]),
        start(own_hbm, own, sems.at[1]),
        start(sent_hbm, sent, sems.at[2]),
    ]
    xs, zh, zl, rest = sizes[:4]
    copies[0].wait()
    for x in range(xs):
        parts = [blocks[x * zl + low, :, high * rest : (high + 1) * rest] for high in range(zh) for low in range(zl)]
        width = len(parts) * rest
        whole_ref[:, x * width : (x + 1) * width] = jnp.concatenate(parts, axis=1)
    out = start(whole_ref, whole_hbm, sems.at[3])
    whole = whole_ref[...]
    codes = []
    weights = ((copies[1], own, own_sides, own_slope), (copies[2], sent, sent_sides, sent_slope))
    for copy, part, sides, slope in weights:
        copy.wait()
        latents = part.shape[0]
        bias = column(sides[sizes[4] + 1 : sizes[4] + 2, :])[:latents]
        shifted = dot(part[...], whole, ((1,), (1,))) - bias
        sig = jax.nn.sigmoid(4.0 * shifted)
        slope[...] = sig + 4.0 * shifted * sig * (1.0 - sig)
        codes.append(shifted * sig)
    code = jnp.concatenate(codes, axis=0).T.astype(BF16)
    for layer in range(code_ref.shape[0]):
        code_ref[layer] = code
    out.wait()


def decode_kernel(codes_ref, own_hbm, sent_hbm, out_hbm, own_ref, sent_ref, out_ref, sems):
    count, _, width = out_ref.shape
    parts = columns(count, width)
    copies = []
    for k, part in enumerate(parts):
        copies.append(start(own_hbm.at[:, part], own_ref.at[:, part], sems.at[0, k]))
        copies.append(start(sent_hbm.at[:, part], sent_ref.at[:, part], sems.at[1, k]))
    section = lax.axis_index("layer")
    layers, _, latents = codes_ref.shape
    latents //= 2
    codes = []
    for layer in range(layers):
        code = codes_ref[layer]
        codes.append(jnp.where(layer <= section, code, jnp.zeros_like(code)))
    own = jnp.concatenate([code[:, :latents] for code in codes], axis=1)
    sent = jnp.concatenate([code[:, latents:] for code in codes], axis=1)
    results = []
    for k, part in enumerate(parts):
        copies[2 * k].wait()
        copies[2 * k + 1].wait()
        total = dot(own, own_ref[:, part], ((1,), (0,))) + dot(sent, sent_ref[:, part], ((1,), (0,)))
        out_ref[k] = total.astype(BF16)
        results.append(start(out_ref.at[k], out_hbm.at[k], sems.at[2, k]))
    for copy in results:
        copy.wait()


def reduce_kernel(rows, parts_hbm, offset_ref, out_ref, parts, sems):
    place = lax.axis_index(FAR)
    copies = [start(parts_hbm.at[k], parts.at[k], sems.at[k]) for k in range(parts.shape[0])]
    size = offset_ref.shape[0]
    tile = jnp.concatenate([offset_ref[...].T] * out_ref.shape[0], axis=1)
    lane = lax.broadcasted_iota(jnp.int32, tile.shape, 1)
    total = jnp.where((lane >= place * size) & (lane < (place + 1) * size), -tile, jnp.zeros_like(tile))
    for k, copy in enumerate(copies):
        copy.wait()
        total += parts[k].astype(F32)
    rest = out_ref.shape[1] - rows
    for k in range(out_ref.shape[0]):
        piece = total[k * rows : (k + 1) * rows]
        if rest > 0:
            piece = jnp.concatenate([piece, jnp.zeros((rest, piece.shape[1]), F32)], axis=0)
        out_ref[k] = piece.astype(BF16)


def error_kernel(rows, scale, positions_ref, parts_ref, out_ref):
    begin = (lax.axis_index("core") * parts_ref.shape[0] + lax.axis_index(FAR)) * rows
    row = lax.broadcasted_iota(jnp.int32, (parts_ref.shape[1], 1), 0)
    mask = jnp.zeros((parts_ref.shape[1], 1), F32)
    for k in range(rows):
        mask = jnp.where(row == k, (positions_ref[begin + k] > 0).astype(F32), mask)
    total = parts_ref[0].astype(F32)
    for k in range(1, parts_ref.shape[0]):
        total += parts_ref[k].astype(F32)
    error = (mask * total * scale).astype(BF16)
    for k in range(out_ref.shape[0]):
        out_ref[k] = error


def repeat_kernel(rows, parts_ref, out_ref):
    parts = [parts_ref[k].astype(F32)[:rows] for k in range(parts_ref.shape[0])]
    block = jnp.concatenate(parts, axis=0).astype(BF16)
    for k in range(out_ref.shape[0]):
        out_ref[k] = block


def back_kernel(error_ref, own_ref, sent_ref, out_ref):
    section = lax.axis_index("layer")
    first = lax.axis_index("core") == 0
    error = jnp.concatenate([error_ref[k] for k in range(error_ref.shape[0])], axis=1)
    own = dot(own_ref[...], error, ((1,), (1,)))
    sent = dot(sent_ref[...], error, ((1,), (1,)))
    latents = out_ref.shape[1]
    for layer in range(out_ref.shape[0] // 2):
        rows = slice(layer * latents, (layer + 1) * latents)
        kept = (layer <= section).astype(F32)
        out_ref[2 * layer] = (jnp.where(first, own[rows], sent[rows]) * kept).astype(BF16)
        out_ref[2 * layer + 1] = (jnp.where(first, sent[rows], own[rows]) * kept).astype(BF16)


def final_kernel(
    terms_ref, own_slope, sent_slope, own_hbm, sent_hbm, grad_hbm, threshold_ref, own_ref, sent_ref, grad_ref, sems
):
    parts = columns(sems.shape[1], own_ref.shape[1] // sems.shape[1])
    copies = []
    for k, part in enumerate(parts):
        copies.append(start(own_hbm.at[:, part], own_ref.at[:, part], sems.at[0, k]))
        copies.append(start(sent_hbm.at[:, part], sent_ref.at[:, part], sems.at[1, k]))
    first = lax.axis_index("core") == 0
    low, high = terms_ref[0].astype(F32), terms_ref[1].astype(F32)
    for k in range(2, terms_ref.shape[0], 2):
        low += terms_ref[k].astype(F32)
        high += terms_ref[k + 1].astype(F32)
    own = jnp.where(first, low, high) * own_slope[...]
    sent = jnp.where(first, high, low) * sent_slope[...]
    total = -jnp.sum(own + sent, axis=1, keepdims=True)
    threshold_ref[...] = jnp.broadcast_to(total, (total.shape[0], 128)).T[:1]
    own, sent = own.astype(BF16), sent.astype(BF16)
    results = []
    for k, part in enumerate(parts):
        copies[2 * k].wait()
        copies[2 * k + 1].wait()
        grad_ref[:, part] = dot(own, own_ref[:, part], ((1,), (0,))) + dot(sent, sent_ref[:, part], ((1,), (0,)))
        results.append(start(grad_ref.at[:, part], grad_hbm.at[:, part], sems.at[2, k]))
    for copy in results:
        copy.wait()


def body(inputs, targets, encoder, threshold, decoders, out_bias, positions):
    layers = lax.axis_size("layer")
    width, tokens = inputs.shape[2], inputs.shape[1]
    half = tokens // 2
    latents, model = encoder.shape[1], encoder.shape[2]
    xs, zh, zl, yh = (lax.axis_size(name) for name in ("x", "zh", "zl", "yh"))
    near, far = xs * zl, zh * yh
    wide, rows = model // near, half // far
    tall = -(-rows // 16) * 16

    side = struct((width + 8, 128), F32)
    sends, own_sides, sent_sides = call(
        split_kernel,
        [struct((2 * far, width, half), BF16), side, side],
        [inputs[0].T, targets[0].T, out_bias, threshold],
    )
    block = exchange(sends, FAR + ("core",)).reshape(-1, half)
    own_encoder = encoder[0]
    own_decoders = decoders[0].reshape(layers * latents, model)
    held = (block, own_encoder, own_decoders, sent_sides)
    block, sent_encoder, sent_decoders, sent_sides = lax.optimization_barrier(held)
    other_sides = swap(sent_sides)
    other_encoder = swap(sent_encoder)
    other_decoders = swap(sent_decoders)
    (sends,) = call(flip_kernel, [struct((near, half, wide), BF16)], [block])
    blocks = exchange(sends, NEAR)
    whole, codes, own_slope, sent_slope = call(
        functools.partial(encode_kernel, (xs, zh, zl, wide // zh, width)),
        [
            struct((half, model), BF16),
            struct((layers, half, 2 * latents), BF16),
            struct((latents, half), F32),
            struct((latents, half), F32),
        ],
        [blocks, own_encoder, other_encoder, own_sides, other_sides],
        scratch=[
            pltpu.VMEM((near, half, wide), BF16),
            pltpu.VMEM((latents, model), BF16),
            pltpu.VMEM((latents, model), BF16),
            pltpu.VMEM((half, model), BF16),
            pltpu.SemaphoreType.DMA((4,)),
        ],
        remote=[0],
        weights=[1, 2],
        remote_outs=[0],
        flops=4 * half * latents * model,
    )
    codes = exchange(codes, ("layer",))
    (offset,) = call(offset_kernel, [struct((2 * width, half), F32)], [own_sides, other_sides])
    offset = to_owner(offset)
    other_whole = swap(whole)
    other_slope = swap(sent_slope)

    (parts,) = call(
        decode_kernel,
        [struct((near, half, wide), BF16)],
        [codes, own_decoders, other_decoders],
        scratch=[
            pltpu.VMEM((layers * latents, model), BF16),
            pltpu.VMEM((layers * latents, model), BF16),
            pltpu.VMEM((near, half, wide), BF16),
            pltpu.SemaphoreType.DMA((3, near)),
        ],
        weights=[1, 2],
        remote_outs=[0],
        mib=62,
        flops=4 * layers * half * latents * model,
    )
    parts = exchange(parts, NEAR)
    parts, offset, other_whole, other_slope = lax.optimization_barrier((parts, offset, other_whole, other_slope))
    (parts,) = call(
        functools.partial(reduce_kernel, rows),
        [struct((far, tall, wide), BF16)],
        [parts, offset],
        scratch=[pltpu.VMEM((near, half, wide), BF16), pltpu.SemaphoreType.DMA((near,))],
        remote=[0],
    )
    parts = exchange(parts, FAR)
    (parts,) = call(
        functools.partial(error_kernel, rows, 1.0 / layers),
        [struct((far, tall, wide), BF16)],
        [positions, parts],
        scalars=[0],
    )
    parts = exchange(parts, FAR)
    (parts,) = call(functools.partial(repeat_kernel, rows), [struct((near, half, wide), BF16)], [parts])
    error = exchange(parts, NEAR)
    (terms,) = call(
        back_kernel,
        [struct((2 * layers, latents, half), BF16)],
        [error, own_decoders, other_decoders],
        flops=4 * layers * half * latents * model,
    )
    terms = exchange(terms, ("layer", "core"))
    grad_encoder, grad_threshold = call(
        final_kernel,
        [struct((latents, model), F32), struct((1, latents), F32)],
        [terms, own_slope, other_slope, whole, other_whole],
        scratch=[
            pltpu.VMEM((half, model), BF16),
            pltpu.VMEM((half, model), BF16),
            pltpu.VMEM((latents, model), F32),
            pltpu.SemaphoreType.DMA((3, 4)),
        ],
        weights=[3, 4],
        remote_outs=[0],
        flops=4 * half * latents * model,
    )
    return (grad_encoder[None], grad_threshold)


LATENT = ("x", "zh", "zl", "yh", "core")


def solution(mesh, parts=(4, 4, 2, 2, 2)):
    in_specs = (
        P("layer", None, LATENT),
        P("layer", None, LATENT),
        P("layer", LATENT, None),
        P("layer", LATENT),
        P("layer", None, LATENT, None),
        P("layer", LATENT),
        P(),
    )
    out_specs = (P("layer", LATENT, None), P("layer", LATENT))
    devices = mesh.devices.reshape((mesh.devices.shape[0],) + parts)
    fine = Mesh(devices, ("layer",) + LATENT)
    return jax.shard_map(body, mesh=fine, in_specs=in_specs, out_specs=out_specs, check_vma=False)
```

time: 169 us -> 160 us (0.947)
  blocking collectives: 60 us -> 101 us
  starting transfers between devices: 49.1 us -> 23.1 us
  waiting for transfers between devices: 38.3 us -> 13.6 us
  Pallas kernels: 9.9 us -> 17.6 us
  local copies, waits for them, and re-layouts: 9.36 us -> 3.79 us
    all_to_all x4 -> x6, blocking collectives: 60 us -> 101 us  [exchange(): return lax.all_to_all(blocks, axes, 0, 0, tiled=True)]
    all_to_all x4 -> x2, waiting for transfers between devices: 36.3 us -> 11.3 us  [exchange(): return lax.all_to_all(blocks, axes, 0, 0, tiled=True)]
    all_to_all x4 -> x2, starting transfers between devices: 28.7 us -> 9.19 us  [exchange(): return lax.all_to_all(blocks, axes, 0, 0, tiled=True)]
    pallas_call x8 -> x10, Pallas kernels: 9.9 us -> 17.6 us  [call(): pl.pallas_call(run, out_shape=outs, in_specs=[SMEM if k in scalars else A...]
    ppermute x5, starting transfers between devices: 19.7 us -> 13.3 us  [swap(): return lax.ppermute(block, 'core', [(0, 1), (1, 0)])]
    another operation x7 -> x0, local copies, waits for them, and re-layouts: 2.14 us -> none  [the longest x2 1.76 us: halves(): return jnp.stack([array[:, :half], array[:, half:]])]
    unnamed x18, local copies, waits for them, and re-layouts: 5.7 us -> 3.79 us
  transfers between devices with their start and end apart: 10 -> 8, of which waited for: 6 -> 4; matrix products, arithmetic and copies ran while one was open for 3% -> 0% of each run, Pallas kernels for 0% -> 2%
where the time goes in v4:
time: 160 us
  blocking collectives  101 us (63%)
  starting transfers between devices  23.1 us (14%)
  Pallas kernels  17.6 us (11%)
  waiting for transfers between devices  13.6 us (8%)
  local copies, waits for them, and re-layouts  3.79 us (2%)
    all_to_all x6, blocking collectives, exchange(): return lax.all_to_all(blocks, axes, 0, 0, tiled=True)  101 us
    pallas_call x10, Pallas kernels, call(): pl.pallas_call(run, out_shape=outs, in_specs=[SMEM if k in scalars else A...  17.6 us
    ppermute x5, starting transfers between devices, swap(): return lax.ppermute(block, 'core', [(0, 1), (1, 0)])  13.3 us
    all_to_all x2, waiting for transfers between devices, exchange(): return lax.all_to_all(blocks, axes, 0, 0, tiled=True)  11.3 us
    all_to_all x2, starting transfers between devices, exchange(): return lax.all_to_all(blocks, axes, 0, 0, tiled=True)  9.19 us
    unnamed x18, local copies, waits for them, and re-layouts  3.79 us
  transfers between devices with their start and end apart: 8, of which 4 were waited for; matrix products, arithmetic and copies ran while one was open for 0% of the time, Pallas kernels for 2%

profile of v4, /device:TPU:1, one launch (start us, length us, event | category | flops | bytes accessed | tf_op | source)
XLA Modules:
  0.0 159.6 jit_solution(16365612297365820405)
XLA Ops:
  0.6 0.0 copy-start.3
  0.6 0.0 copy-start.4
  0.7 0.8 copy-done.4
  1.4 0.0 copy-start.5
  1.4 0.7 copy-done.5
  2.2 0.0 copy-start.7
  2.2 0.7 copy-done.7
  2.8 0.0 copy-start.8
  2.8 0.7 copy-done.8
  3.5 0.1 shard_map.86
  3.6 29.9 %all_to_all.40 = bf16[16,40,96]{2,1,0:T(8,128)(2,1)S(1)} all-to-all(bf16[16,40,96]{2,1,0:T(8,128)(2,1)S(1)} %get-tuple-element.19), channel_id=1, replica_groups=mesh['layer'=4,'x'=4,'zh'=4,'zl'=2,'yh'=2,'core'=2] {'zh','yh','core'}, dimensions={0} | all-to-all | bytes 245760 | tf_op jit(solution)/shard_map/all_to_all | solution.py:32
  33.5 1.9 %collective-permute-start.2 = (bf16[256,5120]{1,0:T(8,128)(2,1)}, bf16[256,5120]{1,0:T(8,128)(2,1)}, u32[]{:S(2)}, u32[]{:S(2)}) collective-permute-start(bf16[256,5120]{1,0:T(8,128)(2,1)} %bitcast.10), channel_id=1, source_target_pairs={{0,1},{1,0},{2,3},{3,2},{4,5},{5,4},{6,7},{7,6},{8,9},{9,8},{10,11... | collective-permute-start | bytes 7864328 | tf_op jit(solution)/shard_map/ppermute | solution.py:36
  35.4 1.1 shard_map.87
  36.5 4.9 %all-to-all-start.1 = ((bf16[8,96,640]{2,1,0:T(8,128)(2,1)}), bf16[8,96,640]{2,1,0:T(8,128)(2,1)S(1)}, u32[]{:S(2)}, u32[]{:S(2)}) async-start(bf16[8,96,640]{2,1,0:T(8,128)(2,1)} %shard_map.87), calls=%async_computation.1 | async-start | bytes 1966080 | tf_op jit(solution)/shard_map/all_to_all | solution.py:32
  41.4 0.0 copy-done.3
  41.4 2.5 %collective-permute-start = (bf16[64,5120]{1,0:T(8,128)(2,1)S(1)}, bf16[64,5120]{1,0:T(8,128)(2,1)S(1)}, u32[]{:S(2)}, u32[]{:S(2)}) collective-permute-start(bf16[64,5120]{1,0:T(8,128)(2,1)S(1)} %bitcast.14), channel_id=1, source_target_pairs={{0,1},{1,0},{2,3},{3,2},{4,5},{5,4},{6,7},{7,6},{8,9},{9,8},{10,11... | collective-permute-start | bytes 1966088 | tf_op jit(solution)/shard_map/ppermute | solution.py:36
  43.9 1.9 %collective-permute-start.1 = (f32[48,128]{1,0:T(8,128)S(1)}, f32[48,128]{1,0:T(8,128)S(1)}, u32[]{:S(2)}, u32[]{:S(2)}) collective-permute-start(f32[48,128]{1,0:T(8,128)S(1)} %get-tuple-element.24), channel_id=1, source_target_pairs={{0,1},{1,0},{2,3},{3,2},{4,5},{5,4},{6,7},{7,6},{8,9},{9,8},{10,11... | collective-permute-start | bytes 73736 | tf_op jit(solution)/shard_map/ppermute | solution.py:36
  45.9 1.2 collective-permute-done.1.refs_4_.refs_1_
  47.0 0.0 collective-permute-done.refs_2_
  47.0 9.0 %all-to-all-done.1.refs_0_ = bf16[8,96,640]{2,1,0:T(8,128)(2,1)S(1)} async-done(((bf16[8,96,640]{2,1,0:T(8,128)(2,1)}), bf16[8,96,640]{2,1,0:T(8,128)(2,1)S(1)}, u32[]{:S(2)}, u32[]{:S(2)}) %all-to-all-start.1) | async-done | bytes 983072 | tf_op jit(solution)/shard_map/all_to_all | solution.py:32
  56.0 2.5 %shard_map.88 = (bf16[96,5120]{1,0:T(8,128)(2,1)}, bf16[4,96,128]{2,1,0:T(8,128)(2,1)S(1)}, f32[64,96]{1,0:T(8,128)S(1)}, f32[64,96]{1,0:T(8,128)S(1)}) custom-call(bf16[8,96,640]{2,1,0:T(8,128)(2,1)S(1)} %all-to-all-done.1.refs_0_, bf16[64,5120]{1,0:T(8,128)(2,1)S(1)} %bitcast.15, bf16[64,5120]{1,0:T(8,128)(2,1)S(1)} %collective-permute-done.refs_2_, ...), custom_call_target="tpu_custom_call" | custom-call | flops 125829120 | bytes 3473408 | tf_op jit(solution)/shard_map/pallas_call | solution.py:50
  58.5 7.9 %all_to_all.41.refs_0_ = bf16[4,96,128]{2,1,0:T(8,128)(2,1)} all-to-all(bf16[4,96,128]{2,1,0:T(8,128)(2,1)S(1)} %get-tuple-element.25), channel_id=1, replica_groups=mesh['layer'=4,'x'=4,'zh'=4,'zl'=2,'yh'=2,'core'=2] {'layer'}, dimensions={0} | all-to-all | bytes 196608 | tf_op jit(solution)/shard_map/all_to_all | solution.py:32
  66.4 0.0 collective-permute-done.2.refs_2_
  66.4 4.9 %shard_map.89 = bf16[8,96,640]{2,1,0:T(8,128)(2,1)} custom-call(bf16[4,96,128]{2,1,0:T(8,128)(2,1)} %all_to_all.41.refs_0_, bf16[256,5120]{1,0:T(8,128)(2,1)} %bitcast.11, bf16[256,5120]{1,0:T(8,128)(2,1)} %collective-permute-done.2.refs_2_), custom_call_target="tpu_custom_call" | custom-call | flops 503316480 | bytes 6324224 | tf_op jit(solution)/shard_map/pallas_call | solution.py:50
  71.3 0.0 copy-start.6
  71.3 4.3 %all-to-all-start.3 = ((bf16[8,96,640]{2,1,0:T(8,128)(2,1)}), bf16[8,96,640]{2,1,0:T(8,128)(2,1)}, u32[]{:S(2)}, u32[]{:S(2)}) async-start(bf16[8,96,640]{2,1,0:T(8,128)(2,1)} %shard_map.89), calls=%async_computation.3 | async-start | bytes 1966080 | tf_op jit(solution)/shard_map/all_to_all | solution.py:32
  75.6 4.8 %collective-permute-start.4 = (bf16[96,5120]{1,0:T(8,128)(2,1)}, bf16[96,5120]{1,0:T(8,128)(2,1)S(1)}, u32[]{:S(2)}, u32[]{:S(2)}) collective-permute-start(bf16[96,5120]{1,0:T(8,128)(2,1)} %get-tuple-element.27.refs_3_), channel_id=1, source_target_pairs={{0,1},{1,0},{2,3},{3,2},{4,5},{5,4},{6,7},{7,6},{8,9},{9,8},{10,11... | collective-permute-start | bytes 2949128 | tf_op jit(solution)/shard_map/ppermute | solution.py:36
  80.4 0.2 shard_map.90
  80.5 0.7 collective-permute-start.3
  81.2 0.0 copy-start
  81.2 2.2 %collective-permute-start.5 = (f32[64,96]{1,0:T(8,128)S(1)}, f32[64,96]{1,0:T(8,128)S(1)}, u32[]{:S(2)}, u32[]{:S(2)}) collective-permute-start(f32[64,96]{1,0:T(8,128)S(1)} %get-tuple-element.28), channel_id=1, source_target_pairs={{0,1},{1,0},{2,3},{3,2},{4,5},{5,4},{6,7},{7,6},{8,9},{9,8},{10,11... | collective-permute-start | bytes 73736 | tf_op jit(solution)/shard_map/ppermute | solution.py:36
  83.4 0.0 collective-permute-done.3.refs_1_
  83.4 1.2 collective-permute-done.5.refs_2_
  84.6 0.0 collective-permute-done.4.refs_4_
  84.6 0.0 copy-start.1
  84.6 0.9 copy-done.1
  85.5 2.3 %all-to-all-done.3.refs_0_ = bf16[8,96,640]{2,1,0:T(8,128)(2,1)} async-done(((bf16[8,96,640]{2,1,0:T(8,128)(2,1)}), bf16[8,96,640]{2,1,0:T(8,128)(2,1)}, u32[]{:S(2)}, u32[]{:S(2)}) %all-to-all-start.3) | async-done | bytes 983072 | tf_op jit(solution)/shard_map/all_to_all | solution.py:32
  87.9 1.5 shard_map.91
  89.4 18.5 %all_to_all.42.refs_1_ = bf16[8,16,640]{2,1,0:T(8,128)(2,1)S(1)} all-to-all(bf16[8,16,640]{2,1,0:T(8,128)(2,1)S(1)} %shard_map.91), channel_id=1, replica_groups=mesh['layer'=4,'x'=4,'zh'=4,'zl'=2,'yh'=2,'core'=2] {'zh','yh'}, dimensions={0} | all-to-all | bytes 327680 | tf_op jit(solution)/shard_map/all_to_all | solution.py:32
  108.0 0.0 copy-done.6
  108.0 0.6 shard_map.92
  108.6 15.2 %all_to_all.43.refs_0_ = bf16[8,16,640]{2,1,0:T(8,128)(2,1)S(1)} all-to-all(bf16[8,16,640]{2,1,0:T(8,128)(2,1)S(1)} %shard_map.92), channel_id=1, replica_groups=mesh['layer'=4,'x'=4,'zh'=4,'zl'=2,'yh'=2,'core'=2] {'zh','yh'}, dimensions={0} | all-to-all | bytes 327680 | tf_op jit(solution)/shard_map/all_to_all | solution.py:32
  123.8 0.1 shard_map.93
  123.9 16.0 %all_to_all.44.refs_0_ = bf16[8,96,640]{2,1,0:T(8,128)(2,1)S(1)} all-to-all(bf16[8,96,640]{2,1,0:T(8,128)(2,1)S(1)} %shard_map.93), channel_id=1, replica_groups=mesh['layer'=4,'x'=4,'zh'=4,'zl'=2,'yh'=2,'core'=2] {'x','zl'}, dimensions={0} | all-to-all | bytes 1966080 | tf_op jit(solution)/shard_map/all_to_all | solution.py:32
  139.9 0.0 copy-done
  139.9 0.0 copy-start.2
  139.9 3.3 %shard_map.94 = bf16[8,64,96]{2,1,0:T(8,128)(2,1)S(1)} custom-call(bf16[8,96,640]{2,1,0:T(8,128)(2,1)S(1)} %all_to_all.44.refs_0_, bf16[256,5120]{1,0:T(8,128)(2,1)S(1)} %bitcast.12, bf16[256,5120]{1,0:T(8,128)(2,1)} %collective-permute-done.2.refs_2_), custom_call_target="tpu_custom_call" | custom-call | flops 503316480 | bytes 6324224 | tf_op jit(solution)/shard_map/pallas_call | solution.py:50
  143.2 13.1 %all_to_all.45.refs_0_ = bf16[8,64,96]{2,1,0:T(8,128)(2,1)S(1)} all-to-all(bf16[8,64,96]{2,1,0:T(8,128)(2,1)S(1)} %shard_map.94), channel_id=1, replica_groups=mesh['layer'=4,'x'=4,'zh'=4,'zl'=2,'yh'=2,'core'=2] {'layer','core'}, dimensions={0} | all-to-all | bytes 196608 | tf_op jit(solution)/shard_map/all_to_all | solution.py:32
  156.3 0.0 copy-done.2
  156.3 3.3 %shard_map.95 = (f32[64,5120]{1,0:T(8,128)}, f32[1,64]{1,0:T(1,128)}) custom-call(bf16[8,64,96]{2,1,0:T(8,128)(2,1)S(1)} %all_to_all.45.refs_0_, f32[64,96]{1,0:T(8,128)S(1)} %get-tuple-element.31.refs_1_, f32[64,96]{1,0:T(8,128)S(1)} %collective-permute-done.5.refs_2_, bf16[96,5120]{1,0:T(8,128)(2,1)} %get-tuple-element.27.refs_3_, ...), custom_call_target="tpu_custom_call" | custom-call | flops 125829120 | bytes 3424512 | tf_op jit(solution)/shard_map/pallas_call | solution.py:50
Async XLA Ops:
  0.6 40.8 %copy-start.3 = (bf16[1,64,5120]{2,1,0:T(8,128)(2,1)S(1)}, bf16[1,64,5120]{2,1,0:T(8,128)(2,1)}, u32[]{:S(2)}) copy-start(bf16[1,64,5120]{2,1,0:T(8,128)(2,1)} %param.9) | copy-start | bytes 1966084
  0.6 0.8 copy-start.4
  1.4 0.7 copy-start.5
  2.2 0.7 copy-start.7
  2.8 0.7 copy-start.8
  33.5 32.9 %collective-permute-start.2 = (bf16[256,5120]{1,0:T(8,128)(2,1)}, bf16[256,5120]{1,0:T(8,128)(2,1)}, u32[]{:S(2)}, u32[]{:S(2)}) collective-permute-start(bf16[256,5120]{1,0:T(8,128)(2,1)} %bitcast.10), channel_id=1, source_target_pairs={{0,1},{1,0},{2,3},{3,2},{4,5},{5,4},{6,7},{7,6},{8,9},{9,8},{10,11... | collective-permute-start | bytes 7864328 | tf_op jit(solution)/shard_map/ppermute | solution.py:36
  36.5 19.5 %all-to-all-start.1 = ((bf16[8,96,640]{2,1,0:T(8,128)(2,1)}), bf16[8,96,640]{2,1,0:T(8,128)(2,1)S(1)}, u32[]{:S(2)}, u32[]{:S(2)}) async-start(bf16[8,96,640]{2,1,0:T(8,128)(2,1)} %shard_map.87), calls=%async_computation.1 | async-start | bytes 1966080 | tf_op jit(solution)/shard_map/all_to_all | solution.py:32
  41.4 5.6 %collective-permute-start = (bf16[64,5120]{1,0:T(8,128)(2,1)S(1)}, bf16[64,5120]{1,0:T(8,128)(2,1)S(1)}, u32[]{:S(2)}, u32[]{:S(2)}) collective-permute-start(bf16[64,5120]{1,0:T(8,128)(2,1)S(1)} %bitcast.14), channel_id=1, source_target_pairs={{0,1},{1,0},{2,3},{3,2},{4,5},{5,4},{6,7},{7,6},{8,9},{9,8},{10,11... | collective-permute-start | bytes 1966088 | tf_op jit(solution)/shard_map/ppermute | solution.py:36
  43.9 3.1 %collective-permute-start.1 = (f32[48,128]{1,0:T(8,128)S(1)}, f32[48,128]{1,0:T(8,128)S(1)}, u32[]{:S(2)}, u32[]{:S(2)}) collective-permute-start(f32[48,128]{1,0:T(8,128)S(1)} %get-tuple-element.24), channel_id=1, source_target_pairs={{0,1},{1,0},{2,3},{3,2},{4,5},{5,4},{6,7},{7,6},{8,9},{9,8},{10,11... | collective-permute-start | bytes 73736 | tf_op jit(solution)/shard_map/ppermute | solution.py:36
  71.3 36.6 %copy-start.6 = (s32[192]{0:T(256)S(1)}, s32[192]{0:T(256)}, u32[]{:S(2)}) copy-start(s32[192]{0:T(256)} %refs_0_.1) | copy-start | bytes 2308
  71.3 16.5 %all-to-all-start.3 = ((bf16[8,96,640]{2,1,0:T(8,128)(2,1)}), bf16[8,96,640]{2,1,0:T(8,128)(2,1)}, u32[]{:S(2)}, u32[]{:S(2)}) async-start(bf16[8,96,640]{2,1,0:T(8,128)(2,1)} %shard_map.89), calls=%async_computation.3 | async-start | bytes 1966080 | tf_op jit(solution)/shard_map/all_to_all | solution.py:32
  75.6 9.0 %collective-permute-start.4 = (bf16[96,5120]{1,0:T(8,128)(2,1)}, bf16[96,5120]{1,0:T(8,128)(2,1)S(1)}, u32[]{:S(2)}, u32[]{:S(2)}) collective-permute-start(bf16[96,5120]{1,0:T(8,128)(2,1)} %get-tuple-element.27.refs_3_), channel_id=1, source_target_pairs={{0,1},{1,0},{2,3},{3,2},{4,5},{5,4},{6,7},{7,6},{8,9},{9,8},{10,11... | collective-permute-start | bytes 2949128 | tf_op jit(solution)/shard_map/ppermute | solution.py:36
  80.5 2.9 %collective-permute-start.3 = (f32[80,96]{1,0:T(8,128)S(1)}, f32[80,96]{1,0:T(8,128)S(1)}, u32[]{:S(2)}, u32[]{:S(2)}) collective-permute-start(f32[80,96]{1,0:T(8,128)S(1)} %shard_map.90), channel_id=1, source_target_pairs={{0,0},{4,8},{8,16},{12,24},{16,4},{20,12},{24,20},{28,28},{1,1},{5... | collective-permute-start | bytes 92168 | tf_op jit(solution)/shard_map/ppermute | solution.py:42
  81.2 58.6 %copy-start = (bf16[1,4,64,5120]{3,2,1,0:T(8,128)(2,1)S(1)}, bf16[1,4,64,5120]{3,2,1,0:T(8,128)(2,1)}, u32[]{:S(2)}) copy-start(bf16[1,4,64,5120]{3,2,1,0:T(8,128)(2,1)} %param.11) | copy-start | bytes 7864324
  81.2 3.4 %collective-permute-start.5 = (f32[64,96]{1,0:T(8,128)S(1)}, f32[64,96]{1,0:T(8,128)S(1)}, u32[]{:S(2)}, u32[]{:S(2)}) collective-permute-start(f32[64,96]{1,0:T(8,128)S(1)} %get-tuple-element.28), channel_id=1, source_target_pairs={{0,1},{1,0},{2,3},{3,2},{4,5},{5,4},{6,7},{7,6},{8,9},{9,8},{10,11... | collective-permute-start | bytes 73736 | tf_op jit(solution)/shard_map/ppermute | solution.py:36
  84.6 1.0 copy-start.1
  139.9 16.4 %copy-start.2 = (bf16[96,5120]{1,0:T(8,128)(2,1)S(1)}, bf16[96,5120]{1,0:T(8,128)(2,1)}, u32[]{:S(2)}) copy-start(bf16[96,5120]{1,0:T(8,128)(2,1)} %copy-done.1) | copy-start | bytes 2949124

commit v5 on v4

v5 whole, which is shorter than its diff:
```python
import functools

import jax
import jax.numpy as jnp
from jax import lax
from jax.experimental import pallas as pl
from jax.experimental.pallas import tpu as pltpu
from jax.sharding import Mesh, PartitionSpec as P

F32 = jnp.float32
BF16 = jnp.bfloat16
NEAR = ("x", "zl")
FAR = ("zh", "yh")
ANY = pl.BlockSpec(memory_space=pl.ANY)
VMEM = pl.BlockSpec(memory_space=pltpu.VMEM)
MIB = 1 << 20


def dot(left, right, dims):
    return lax.dot_general(left, right, (dims, ((), ())), preferred_element_type=F32)


def size_of(axes):
    count = 1
    for name in axes:
        count *= lax.axis_size(name)
    return count


def exchange(blocks, axes):
    return lax.all_to_all(blocks, axes, 0, 0, tiled=True)


def swap(block):
    return lax.ppermute(block, "core", [(0, 1), (1, 0)])


def to_owner(block):
    high, low = lax.axis_size("zh"), lax.axis_size("zl")
    pairs = [(a * high + b, b * low + a) for a in range(low) for b in range(high)]
    return lax.ppermute(block, ("zh", "zl"), pairs)


def call(kernel, outs, operands, later=(), scratch=(), remote=(), remote_outs=(), mib=16, flops=0):
    def run(*refs):
        kernel(*refs[: len(operands)], *refs[len(operands) + len(later) :])

    size = sum(o.size * o.dtype.itemsize for o in list(outs) + list(operands))
    return pl.pallas_call(
        run,
        out_shape=outs,
        in_specs=[ANY if k in remote else VMEM for k in range(len(operands))] + [ANY] * len(later),
        out_specs=[ANY if k in remote_outs else VMEM for k in range(len(outs))],
        scratch_shapes=scratch,
        compiler_params=pltpu.CompilerParams(vmem_limit_bytes=mib * MIB),
        cost_estimate=pl.CostEstimate(flops=flops, bytes_accessed=size, transcendentals=0),
    )(*operands, *later)


def start(source, target, semaphore):
    copy = pltpu.make_async_copy(source, target, semaphore)
    copy.start()
    return copy


def columns(count, width):
    return [slice(k * width, (k + 1) * width) for k in range(count)]


def struct(shape, dtype):
    return jax.ShapeDtypeStruct(shape, dtype)


def split_kernel(inputs_ref, targets_ref, bias_ref, threshold_ref, out_ref, own_ref, sent_ref):
    first = lax.axis_index("core") == 0
    width, half = out_ref.shape[1:]
    block = inputs_ref[...].astype(F32)
    low, high = block[:, :half].astype(BF16), block[:, half:].astype(BF16)
    for k in range(0, out_ref.shape[0], 2):
        out_ref[k] = low
        out_ref[k + 1] = high
    block = targets_ref[...].astype(F32)
    low, high = block[:, :half], block[:, half:]
    own_ref[:width, :half] = jnp.where(first, low, high)
    sent_ref[:width, :half] = jnp.where(first, high, low)
    for ref in (own_ref, sent_ref):
        ref[width : width + 1, :width] = bias_ref[...].astype(F32)
        ref[width + 1 : width + 2, : threshold_ref.shape[1]] = threshold_ref[...]


def column(row):
    return jnp.broadcast_to(row, (8, row.shape[1])).T[:, :1]


def offset_kernel(own_ref, sent_ref, out_ref):
    first = lax.axis_index("core") == 0
    width, half = out_ref.shape
    width //= 2
    own, sent = (
        ref[:width, :half] - column(ref[width : width + 1, :])[:width] for ref in (own_ref, sent_ref)
    )
    out_ref[:width] = jnp.where(first, own, sent)
    out_ref[width:] = jnp.where(first, sent, own)


def flip_kernel(block_ref, out_ref):
    block = block_ref[...].astype(F32).T.astype(BF16)
    for k in range(out_ref.shape[0]):
        out_ref[k] = block


def encode_kernel(
    sizes, blocks_ref, own_hbm, sent_hbm, own_sides, sent_sides, whole_hbm, code_ref, own_slope, sent_slope,
    weights, whole_ref, sems,
):
    xs, zh, zl, rest, width = sizes
    latents = own_slope.shape[0]
    copies = [
        start(own_hbm, weights.at[:latents], sems.at[0]),
        start(sent_hbm, weights.at[latents:], sems.at[1]),
    ]
    for x in range(xs):
        parts = [blocks_ref[x * zl + low, :, high * rest : (high + 1) * rest] for high in range(zh) for low in range(zl)]
        size = len(parts) * rest
        whole_ref[:, x * size : (x + 1) * size] = jnp.concatenate(parts, axis=1)
    out = start(whole_ref, whole_hbm, sems.at[2])
    for copy in copies:
        copy.wait()
    bias = [column(sides[width + 1 : width + 2, :])[:latents] for sides in (own_sides, sent_sides)]
    shifted = dot(weights[...], whole_ref[...], ((1,), (1,))) - jnp.concatenate(bias, axis=0)
    sig = jax.nn.sigmoid(4.0 * shifted)
    slope = sig + 4.0 * shifted * sig * (1.0 - sig)
    own_slope[...] = slope[:latents]
    sent_slope[...] = slope[latents:]
    code = (shifted * sig).T.astype(BF16)
    for layer in range(code_ref.shape[0]):
        code_ref[layer] = code
    out.wait()


def decode_kernel(codes_ref, own_hbm, sent_hbm, out_hbm, own_ref, sent_ref, total_ref, out_ref, sems):
    layers, _, latents = codes_ref.shape
    latents //= 2
    copies = []
    for k, (source, target) in enumerate(((own_hbm, own_ref), (sent_hbm, sent_ref))):
        for layer in range(layers):
            rows = slice(layer * latents, (layer + 1) * latents)
            copies.append(start(source.at[rows], target.at[rows], sems.at[k, layer]))
    section = lax.axis_index("layer")
    codes = []
    for layer in range(layers):
        code = codes_ref[layer]
        codes.append(jnp.where(layer <= section, code, jnp.zeros_like(code)))
    own = jnp.concatenate([code[:, :latents] for code in codes], axis=1)
    sent = jnp.concatenate([code[:, latents:] for code in codes], axis=1)
    parts = columns(out_ref.shape[0], out_ref.shape[2])
    for copy in copies[:layers]:
        copy.wait()
    for k, part in enumerate(parts):
        total_ref[k] = dot(own, own_ref[:, part], ((1,), (0,)))
    for copy in copies[layers:]:
        copy.wait()
    results = []
    for k, part in enumerate(parts):
        out_ref[k] = (total_ref[k] + dot(sent, sent_ref[:, part], ((1,), (0,)))).astype(BF16)
        results.append(start(out_ref.at[k], out_hbm.at[k], sems.at[2, k]))
    for copy in results:
        copy.wait()


def reduce_kernel(parts_hbm, offset_ref, out_ref, parts, sems):
    place = lax.axis_index(FAR)
    copies = [start(parts_hbm.at[k], parts.at[k], sems.at[k]) for k in range(parts.shape[0])]
    size = offset_ref.shape[0]
    tile = jnp.concatenate([offset_ref[...].T] * (parts.shape[2] // size), axis=1)
    lane = lax.broadcasted_iota(jnp.int32, tile.shape, 1)
    total = jnp.where((lane >= place * size) & (lane < (place + 1) * size), -tile, jnp.zeros_like(tile))
    for k, copy in enumerate(copies):
        copy.wait()
        total += parts[k].astype(F32)
    total = total.astype(BF16)
    for k in range(out_ref.shape[0]):
        out_ref[k] = total


def error_kernel(scale, positions_ref, parts_ref, out_ref):
    half = parts_ref.shape[1]
    token_mask = (positions_ref[...] > 0).astype(F32)
    mask = jnp.where(lax.axis_index("core") == 0, token_mask[:, :half], token_mask[:, half:])
    total = parts_ref[0].astype(F32)
    for k in range(1, parts_ref.shape[0]):
        total += parts_ref[k].astype(F32)
    error = (column(mask) * total * scale).astype(BF16)
    for k in range(out_ref.shape[0]):
        out_ref[k] = error


def back_kernel(error_ref, own_ref, sent_ref, out_ref):
    section = lax.axis_index("layer")
    first = lax.axis_index("core") == 0
    error = jnp.concatenate([error_ref[k] for k in range(error_ref.shape[0])], axis=1)
    own = dot(own_ref[...], error, ((1,), (1,)))
    sent = dot(sent_ref[...], error, ((1,), (1,)))
    latents = out_ref.shape[1]
    for layer in range(out_ref.shape[0] // 2):
        rows = slice(layer * latents, (layer + 1) * latents)
        kept = (layer <= section).astype(F32)
        out_ref[2 * layer] = (jnp.where(first, own[rows], sent[rows]) * kept).astype(BF16)
        out_ref[2 * layer + 1] = (jnp.where(first, sent[rows], own[rows]) * kept).astype(BF16)


def final_kernel(terms_ref, own_slope, sent_slope, own_ref, sent_ref, grad_hbm, threshold_ref, grad_ref, sems):
    first = lax.axis_index("core") == 0
    low, high = terms_ref[0].astype(F32), terms_ref[1].astype(F32)
    for k in range(2, terms_ref.shape[0], 2):
        low += terms_ref[k].astype(F32)
        high += terms_ref[k + 1].astype(F32)
    own = jnp.where(first, low, high) * own_slope[...]
    sent = jnp.where(first, high, low) * sent_slope[...]
    lows, highs = own.astype(BF16), sent.astype(BF16)
    results = []
    for k, part in enumerate(columns(sems.shape[0], own_ref.shape[1] // sems.shape[0])):
        grad_ref[:, part] = dot(lows, own_ref[:, part], ((1,), (0,))) + dot(highs, sent_ref[:, part], ((1,), (0,)))
        results.append(start(grad_ref.at[:, part], grad_hbm.at[:, part], sems.at[k]))
    total = -jnp.sum(own + sent, axis=1, keepdims=True)
    threshold_ref[...] = jnp.broadcast_to(total, (total.shape[0], 128)).T[:1]
    for copy in results:
        copy.wait()


def body(inputs, targets, encoder, threshold, decoders, out_bias, positions):
    layers = lax.axis_size("layer")
    width, tokens = inputs.shape[2], inputs.shape[1]
    half = tokens // 2
    latents, model = encoder.shape[1], encoder.shape[2]
    xs, zh, zl, yh = (lax.axis_size(name) for name in ("x", "zh", "zl", "yh"))
    near, far = xs * zl, zh * yh
    wide = model // near

    side = struct((width + 8, 128), F32)
    sends, own_sides, sent_sides = call(
        split_kernel,
        [struct((2 * far, width, half), BF16), side, side],
        [inputs[0].T, targets[0].T, out_bias, threshold],
        mib=62,
    )
    own_encoder = encoder[0]
    own_decoders = decoders[0].reshape(layers * latents, model)
    own_encoder = encoder[0]
    sends, own_decoders = lax.optimization_barrier((sends, decoders[0]))
    other_decoders = [swap(own_decoders[layer]) for layer in range(layers)]
    own_decoders = own_decoders.reshape(layers * latents, model)
    block = exchange(sends, FAR + ("core",)).reshape(-1, half)
    held = (block, own_encoder, own_decoders, sent_sides)
    block, sent_encoder, sent_decoders, sent_sides = lax.optimization_barrier(held)
    other_sides = swap(sent_sides)
    other_encoder = swap(sent_encoder)
    other_decoders = swap(sent_decoders)
    (sends,) = call(flip_kernel, [struct((near, half, wide), BF16)], [block])
    blocks = exchange(sends, NEAR)
    whole, codes, own_slope, sent_slope = call(
        functools.partial(encode_kernel, (xs, zh, zl, wide // zh, width)),
        [
            struct((half, model), BF16),
            struct((layers, half, 2 * latents), BF16),
            struct((latents, half), F32),
            struct((latents, half), F32),
        ],
        [blocks, own_encoder, other_encoder, own_sides, other_sides],
        scratch=[
            pltpu.VMEM((2 * latents, model), BF16),
            pltpu.VMEM((half, model), BF16),
            pltpu.SemaphoreType.DMA((3,)),
        ],
        remote=[1, 2],
        remote_outs=[0],
        flops=4 * half * latents * model,
    )
    codes = exchange(codes, ("layer",))
    (offset,) = call(offset_kernel, [struct((2 * width, half), F32)], [own_sides, other_sides])
    offset = to_owner(offset)
    other_whole = swap(whole)
    other_slope = swap(sent_slope)

    (parts,) = call(
        decode_kernel,
        [struct((near, half, wide), BF16)],
        [codes, own_decoders, other_decoders],
        scratch=[
            pltpu.VMEM((layers * latents, model), BF16),
            pltpu.VMEM((layers * latents, model), BF16),
            pltpu.VMEM((near, half, wide), F32),
            pltpu.VMEM((near, half, wide), BF16),
            pltpu.SemaphoreType.DMA((3, near)),
        ],
        remote=[1, 2],
        remote_outs=[0],
        mib=62,
        flops=4 * layers * half * latents * model,
    )
    parts = exchange(parts, NEAR)
    parts, offset, other_whole, other_slope = lax.optimization_barrier((parts, offset, other_whole, other_slope))
    (parts,) = call(
        reduce_kernel,
        [struct((far, half, wide), BF16)],
        [parts, offset],
        scratch=[pltpu.VMEM((near, half, wide), BF16), pltpu.SemaphoreType.DMA((near,))],
        remote=[0],
    )
    parts = exchange(parts, FAR)
    (parts,) = call(
        functools.partial(error_kernel, 1.0 / layers), [struct((near, half, wide), BF16)], [positions[None], parts]
    )
    error = exchange(parts, NEAR)
    (terms,) = call(
        back_kernel,
        [struct((2 * layers, latents, half), BF16)],
        [error, own_decoders, other_decoders],
        flops=4 * layers * half * latents * model,
    )
    terms = exchange(terms, ("layer", "core"))
    grad_encoder, grad_threshold = call(
        final_kernel,
        [struct((latents, model), F32), struct((1, latents), F32)],
        [terms, own_slope, other_slope, whole, other_whole],
        scratch=[pltpu.VMEM((latents, model), F32), pltpu.SemaphoreType.DMA((8,))],
        remote_outs=[0],
        flops=4 * half * latents * model,
    )
    return (grad_encoder[None], grad_threshold)


LATENT = ("x", "zh", "zl", "yh", "core")


def solution(mesh, parts=(4, 4, 2, 2, 2)):
    in_specs = (
        P("layer", None, LATENT),
        P("layer", None, LATENT),
        P("layer", LATENT, None),
        P("layer", LATENT),
        P("layer", None, LATENT, None),
        P("layer", LATENT),
        P(),
    )
    out_specs = (P("layer", LATENT, None), P("layer", LATENT))
    devices = mesh.devices.reshape((mesh.devices.shape[0],) + parts)
    fine = Mesh(devices, ("layer",) + LATENT)
    return jax.shard_map(body, mesh=fine, in_specs=in_specs, out_specs=out_specs, check_vma=False)
```

time: 160 us -> 161 us (level)
  blocking collectives: 101 us -> 104 us
  local copies, waits for them, and re-layouts: 3.79 us -> 1.96 us
    all_to_all x6 -> x5, blocking collectives: 101 us -> 104 us  [exchange(): return lax.all_to_all(blocks, axes, 0, 0, tiled=True)]
    unnamed x18 -> x20, local copies, waits for them, and re-layouts: 3.79 us -> 1.96 us
    pallas_call x10 -> x9, Pallas kernels: 17.6 us -> 16.5 us  [call(): pl.pallas_call(run, out_shape=outs, in_specs=[ANY if k in remote else VME...]
where the time goes in v5:
time: 161 us; the launch traced here: 160 us
  blocking collectives  104 us (65%)
  starting transfers between devices  22.2 us (14%)
  Pallas kernels  16.5 us (10%)
  waiting for transfers between devices  13.9 us (9%)
  local copies, waits for them, and re-layouts  1.96 us (1%)
    all_to_all x5, blocking collectives, exchange(): return lax.all_to_all(blocks, axes, 0, 0, tiled=True)  104 us
    pallas_call x9, Pallas kernels, call(): pl.pallas_call(run, out_shape=outs, in_specs=[ANY if k in remote else VME...  16.5 us
    ppermute x5, starting transfers between devices, swap(): return lax.ppermute(block, 'core', [(0, 1), (1, 0)])  13 us
    all_to_all x2, waiting for transfers between devices, exchange(): return lax.all_to_all(blocks, axes, 0, 0, tiled=True)  11.4 us
    all_to_all x2, starting transfers between devices, exchange(): return lax.all_to_all(blocks, axes, 0, 0, tiled=True)  8.51 us
  transfers between devices with their start and end apart: 8, of which 4 were waited for; matrix products, arithmetic and copies ran while one was open for 0% of the time, Pallas kernels for 2%

profile of v5, /device:TPU:1, one launch (start us, length us, event | category | flops | bytes accessed | tf_op | source)
XLA Modules:
  0.0 159.9 jit_solution(2444544422172635043)
XLA Ops:
  0.6 0.0 copy-start.1
  0.6 1.6 shard_map.86
  2.2 0.0 copy-start.9
  2.2 0.0 copy-start.4
  2.2 30.2 %all_to_all.35 = bf16[16,40,96]{2,1,0:T(8,128)(2,1)S(1)} all-to-all(bf16[16,40,96]{2,1,0:T(8,128)(2,1)} %get-tuple-element.22), channel_id=1, replica_groups=mesh['layer'=4,'x'=4,'zh'=4,'zl'=2,'yh'=2,'core'=2] {'zh','yh','core'}, dimensions={0} | all-to-all | bytes 245760 | tf_op jit(solution)/shard_map/all_to_all | solution.py:31
  32.4 1.9 %collective-permute-start.2 = (bf16[256,5120]{1,0:T(8,128)(2,1)}, bf16[256,5120]{1,0:T(8,128)(2,1)}, u32[]{:S(2)}, u32[]{:S(2)}) collective-permute-start(bf16[256,5120]{1,0:T(8,128)(2,1)} %bitcast.12), channel_id=1, source_target_pairs={{0,1},{1,0},{2,3},{3,2},{4,5},{5,4},{6,7},{7,6},{8,9},{9,8},{10,11... | collective-permute-start | bytes 7864328 | tf_op jit(solution)/shard_map/ppermute | solution.py:35
  34.3 1.1 shard_map.87
  35.4 4.9 %all-to-all-start.1 = ((bf16[8,96,640]{2,1,0:T(8,128)(2,1)}), bf16[8,96,640]{2,1,0:T(8,128)(2,1)S(1)}, u32[]{:S(2)}, u32[]{:S(2)}) async-start(bf16[8,96,640]{2,1,0:T(8,128)(2,1)} %shard_map.87), calls=%async_computation.1 | async-start | bytes 1966080 | tf_op jit(solution)/shard_map/all_to_all | solution.py:31
  40.4 0.0 copy-done.1
  40.4 2.5 %collective-permute-start = (bf16[64,5120]{1,0:T(8,128)(2,1)S(1)}, bf16[64,5120]{1,0:T(8,128)(2,1)S(1)}, u32[]{:S(2)}, u32[]{:S(2)}) collective-permute-start(bf16[64,5120]{1,0:T(8,128)(2,1)S(1)} %bitcast.16), channel_id=1, source_target_pairs={{0,1},{1,0},{2,3},{3,2},{4,5},{5,4},{6,7},{7,6},{8,9},{9,8},{10,11... | collective-permute-start | bytes 1966088 | tf_op jit(solution)/shard_map/ppermute | solution.py:35
  42.9 0.0 copy-done.9
  42.9 1.9 %collective-permute-start.1 = (f32[48,128]{1,0:T(8,128)S(1)}, f32[48,128]{1,0:T(8,128)S(1)}, u32[]{:S(2)}, u32[]{:S(2)}) collective-permute-start(f32[48,128]{1,0:T(8,128)S(1)} %copy-done.9), channel_id=1, source_target_pairs={{0,1},{1,0},{2,3},{3,2},{4,5},{5,4},{6,7},{7,6},{8,9},{9,8},{10,11... | collective-permute-start | bytes 73736 | tf_op jit(solution)/shard_map/ppermute | solution.py:35
  44.8 1.2 collective-permute-done.1.refs_4_.refs_1_
  46.0 0.0 collective-permute-done.refs_2_
  46.0 0.0 copy-start.2
  46.0 0.8 copy-done.2
  46.8 8.1 %all-to-all-done.1.refs_0_ = bf16[8,96,640]{2,1,0:T(8,128)(2,1)S(1)} async-done(((bf16[8,96,640]{2,1,0:T(8,128)(2,1)}), bf16[8,96,640]{2,1,0:T(8,128)(2,1)S(1)}, u32[]{:S(2)}, u32[]{:S(2)}) %all-to-all-start.1) | async-done | bytes 983072 | tf_op jit(solution)/shard_map/all_to_all | solution.py:31
  54.9 0.0 copy-done.4
  54.9 0.0 copy-start.3
  54.9 1.1 copy-done.3
  56.0 1.7 %shard_map.88 = (bf16[96,5120]{1,0:T(8,128)(2,1)S(1)}, bf16[4,96,128]{2,1,0:T(8,128)(2,1)S(1)}, f32[64,96]{1,0:T(8,128)S(1)}, f32[64,96]{1,0:T(8,128)S(1)}) custom-call(bf16[8,96,640]{2,1,0:T(8,128)(2,1)S(1)} %all-to-all-done.1.refs_0_, bf16[64,5120]{1,0:T(8,128)(2,1)S(1)} %bitcast.17, bf16[64,5120]{1,0:T(8,128)(2,1)S(1)} %copy-done.3, ...), custom_call_target="tpu_custom_call" | custom-call | flops 125829120 | bytes 3473408 | tf_op jit(solution)/shard_map/pallas_call | solution.py:49
  57.7 0.0 copy-start.5
  57.7 0.0 copy-start.8
  57.7 7.9 %all_to_all.36.refs_0_ = bf16[4,96,128]{2,1,0:T(8,128)(2,1)} all-to-all(bf16[4,96,128]{2,1,0:T(8,128)(2,1)S(1)} %get-tuple-element.29), channel_id=1, replica_groups=mesh['layer'=4,'x'=4,'zh'=4,'zl'=2,'yh'=2,'core'=2] {'layer'}, dimensions={0} | all-to-all | bytes 196608 | tf_op jit(solution)/shard_map/all_to_all | solution.py:31
  65.6 0.0 collective-permute-done.2.refs_2_
  65.6 4.8 %shard_map.89 = bf16[8,96,640]{2,1,0:T(8,128)(2,1)} custom-call(bf16[4,96,128]{2,1,0:T(8,128)(2,1)} %all_to_all.36.refs_0_, bf16[256,5120]{1,0:T(8,128)(2,1)} %bitcast.13, bf16[256,5120]{1,0:T(8,128)(2,1)} %collective-permute-done.2.refs_2_), custom_call_target="tpu_custom_call" | custom-call | flops 503316480 | bytes 6324224 | tf_op jit(solution)/shard_map/pallas_call | solution.py:49
  70.4 0.0 copy-done.5
  70.5 0.0 copy-done.8
  70.5 0.0 copy-start.7
  70.5 3.6 %all-to-all-start.3 = ((bf16[8,96,640]{2,1,0:T(8,128)(2,1)}), bf16[8,96,640]{2,1,0:T(8,128)(2,1)S(1)}, u32[]{:S(2)}, u32[]{:S(2)}) async-start(bf16[8,96,640]{2,1,0:T(8,128)(2,1)} %shard_map.89), calls=%async_computation.3 | async-start | bytes 1966080 | tf_op jit(solution)/shard_map/all_to_all | solution.py:31
  74.1 4.8 %collective-permute-start.4 = (bf16[96,5120]{1,0:T(8,128)(2,1)S(1)}, bf16[96,5120]{1,0:T(8,128)(2,1)S(1)}, u32[]{:S(2)}, u32[]{:S(2)}) collective-permute-start(bf16[96,5120]{1,0:T(8,128)(2,1)S(1)} %get-tuple-element.31.refs_3_), channel_id=1, source_target_pairs={{0,1},{1,0},{2,3},{3,2},{4,5},{5,4},{6,7},{7,6},{8,9},{9,8},{10,11... | collective-permute-start | bytes 2949128 | tf_op jit(solution)/shard_map/ppermute | solution.py:35
  78.8 0.2 shard_map.90
  79.0 0.7 collective-permute-start.3
  79.7 1.9 %collective-permute-start.5 = (f32[64,96]{1,0:T(8,128)}, f32[64,96]{1,0:T(8,128)S(1)}, u32[]{:S(2)}, u32[]{:S(2)}) collective-permute-start(f32[64,96]{1,0:T(8,128)} %copy-done.8), channel_id=1, source_target_pairs={{0,1},{1,0},{2,3},{3,2},{4,5},{5,4},{6,7},{7,6},{8,9},{9,8},{10,11... | collective-permute-start | bytes 73736 | tf_op jit(solution)/shard_map/ppermute | solution.py:35
  81.6 0.0 collective-permute-done.3.refs_1_
  81.6 1.4 collective-permute-done.5.refs_2_
  83.0 0.0 collective-permute-done.4.refs_4_
  83.0 3.2 %all-to-all-done.3.refs_0_ = bf16[8,96,640]{2,1,0:T(8,128)(2,1)S(1)} async-done(((bf16[8,96,640]{2,1,0:T(8,128)(2,1)}), bf16[8,96,640]{2,1,0:T(8,128)(2,1)S(1)}, u32[]{:S(2)}, u32[]{:S(2)}) %all-to-all-start.3) | async-done | bytes 983072 | tf_op jit(solution)/shard_map/all_to_all | solution.py:31
  86.2 1.8 %shard_map.91 = bf16[8,96,640]{2,1,0:T(8,128)(2,1)S(1)} custom-call(bf16[8,96,640]{2,1,0:T(8,128)(2,1)S(1)} %all-to-all-done.3.refs_0_, f32[80,96]{1,0:T(8,128)S(1)} %collective-permute-done.3.refs_1_), custom_call_target="tpu_custom_call" | custom-call | bytes 1996800 | tf_op jit(solution)/shard_map/pallas_call | solution.py:49
  88.1 0.0 copy-start
  88.1 30.7 %all_to_all.37.refs_1_ = bf16[8,96,640]{2,1,0:T(8,128)(2,1)S(1)} all-to-all(bf16[8,96,640]{2,1,0:T(8,128)(2,1)S(1)} %shard_map.91), channel_id=1, replica_groups=mesh['layer'=4,'x'=4,'zh'=4,'zl'=2,'yh'=2,'core'=2] {'zh','yh'}, dimensions={0} | all-to-all | bytes 1966080 | tf_op jit(solution)/shard_map/all_to_all | solution.py:31
  118.8 0.0 copy-done.7
  118.8 0.3 shard_map.92
  119.1 13.9 %all_to_all.38.refs_0_ = bf16[8,96,640]{2,1,0:T(8,128)(2,1)S(1)} all-to-all(bf16[8,96,640]{2,1,0:T(8,128)(2,1)S(1)} %shard_map.92), channel_id=1, replica_groups=mesh['layer'=4,'x'=4,'zh'=4,'zl'=2,'yh'=2,'core'=2] {'x','zl'}, dimensions={0} | all-to-all | bytes 1966080 | tf_op jit(solution)/shard_map/all_to_all | solution.py:31
  133.0 0.0 copy-done
  133.0 0.0 copy-start.6
  133.0 3.2 %shard_map.93 = bf16[8,64,96]{2,1,0:T(8,128)(2,1)S(1)} custom-call(bf16[8,96,640]{2,1,0:T(8,128)(2,1)S(1)} %all_to_all.38.refs_0_, bf16[256,5120]{1,0:T(8,128)(2,1)S(1)} %bitcast.14, bf16[256,5120]{1,0:T(8,128)(2,1)} %collective-permute-done.2.refs_2_), custom_call_target="tpu_custom_call" | custom-call | flops 503316480 | bytes 6324224 | tf_op jit(solution)/shard_map/pallas_call | solution.py:49
  136.3 21.8 %all_to_all.39.refs_0_ = bf16[8,64,96]{2,1,0:T(8,128)(2,1)S(1)} all-to-all(bf16[8,64,96]{2,1,0:T(8,128)(2,1)S(1)} %shard_map.93), channel_id=1, replica_groups=mesh['layer'=4,'x'=4,'zh'=4,'zl'=2,'yh'=2,'core'=2] {'layer','core'}, dimensions={0} | all-to-all | bytes 196608 | tf_op jit(solution)/shard_map/all_to_all | solution.py:31
  158.0 0.0 copy-done.6
  158.0 1.8 %shard_map.94 = (f32[64,5120]{1,0:T(8,128)}, f32[1,64]{1,0:T(1,128)}) custom-call(bf16[8,64,96]{2,1,0:T(8,128)(2,1)S(1)} %all_to_all.39.refs_0_, f32[64,96]{1,0:T(8,128)S(1)} %copy-done.6, f32[64,96]{1,0:T(8,128)S(1)} %collective-permute-done.5.refs_2_, bf16[96,5120]{1,0:T(8,128)(2,1)S(1)} %get-tuple-element.31.refs_3_, ...), custom_call_target="tpu_custom_call" | custom-call | flops 125829120 | bytes 3424512 | tf_op jit(solution)/shard_map/pallas_call | solution.py:49
Async XLA Ops:
  0.6 39.7 %copy-start.1 = (bf16[1,64,5120]{2,1,0:T(8,128)(2,1)S(1)}, bf16[1,64,5120]{2,1,0:T(8,128)(2,1)}, u32[]{:S(2)}) copy-start(bf16[1,64,5120]{2,1,0:T(8,128)(2,1)} %param.9) | copy-start | bytes 1966084
  2.2 40.7 %copy-start.9 = (f32[48,128]{1,0:T(8,128)S(1)}, f32[48,128]{1,0:T(8,128)}, u32[]{:S(2)}) copy-start(f32[48,128]{1,0:T(8,128)} %get-tuple-element.28) | copy-start | bytes 73732
  2.2 52.7 %copy-start.4 = (f32[48,128]{1,0:T(8,128)S(1)}, f32[48,128]{1,0:T(8,128)}, u32[]{:S(2)}) copy-start(f32[48,128]{1,0:T(8,128)} %get-tuple-element.27.refs_3_.refs_0_) | copy-start | bytes 73732
  32.4 33.2 %collective-permute-start.2 = (bf16[256,5120]{1,0:T(8,128)(2,1)}, bf16[256,5120]{1,0:T(8,128)(2,1)}, u32[]{:S(2)}, u32[]{:S(2)}) collective-permute-start(bf16[256,5120]{1,0:T(8,128)(2,1)} %bitcast.12), channel_id=1, source_target_pairs={{0,1},{1,0},{2,3},{3,2},{4,5},{5,4},{6,7},{7,6},{8,9},{9,8},{10,11... | collective-permute-start | bytes 7864328 | tf_op jit(solution)/shard_map/ppermute | solution.py:35
  35.4 19.5 %all-to-all-start.1 = ((bf16[8,96,640]{2,1,0:T(8,128)(2,1)}), bf16[8,96,640]{2,1,0:T(8,128)(2,1)S(1)}, u32[]{:S(2)}, u32[]{:S(2)}) async-start(bf16[8,96,640]{2,1,0:T(8,128)(2,1)} %shard_map.87), calls=%async_computation.1 | async-start | bytes 1966080 | tf_op jit(solution)/shard_map/all_to_all | solution.py:31
  40.4 5.6 %collective-permute-start = (bf16[64,5120]{1,0:T(8,128)(2,1)S(1)}, bf16[64,5120]{1,0:T(8,128)(2,1)S(1)}, u32[]{:S(2)}, u32[]{:S(2)}) collective-permute-start(bf16[64,5120]{1,0:T(8,128)(2,1)S(1)} %bitcast.16), channel_id=1, source_target_pairs={{0,1},{1,0},{2,3},{3,2},{4,5},{5,4},{6,7},{7,6},{8,9},{9,8},{10,11... | collective-permute-start | bytes 1966088 | tf_op jit(solution)/shard_map/ppermute | solution.py:35
  42.9 3.1 %collective-permute-start.1 = (f32[48,128]{1,0:T(8,128)S(1)}, f32[48,128]{1,0:T(8,128)S(1)}, u32[]{:S(2)}, u32[]{:S(2)}) collective-permute-start(f32[48,128]{1,0:T(8,128)S(1)} %copy-done.9), channel_id=1, source_target_pairs={{0,1},{1,0},{2,3},{3,2},{4,5},{5,4},{6,7},{7,6},{8,9},{9,8},{10,11... | collective-permute-start | bytes 73736 | tf_op jit(solution)/shard_map/ppermute | solution.py:35
  46.0 0.8 copy-start.2
  54.9 1.1 copy-start.3
  57.7 12.7 %copy-start.5 = (f32[64,96]{1,0:T(8,128)}, f32[64,96]{1,0:T(8,128)S(1)}, u32[]{:S(2)}) copy-start(f32[64,96]{1,0:T(8,128)S(1)} %get-tuple-element.35.refs_1_) | copy-start | bytes 73732
  57.7 12.7 %copy-start.8 = (f32[64,96]{1,0:T(8,128)}, f32[64,96]{1,0:T(8,128)S(1)}, u32[]{:S(2)}) copy-start(f32[64,96]{1,0:T(8,128)S(1)} %get-tuple-element.32) | copy-start | bytes 73732
  70.5 48.3 %copy-start.7 = (s32[192]{0:T(256)S(1)}, s32[192]{0:T(256)}, u32[]{:S(2)}) copy-start(s32[192]{0:T(256)} %param.13) | copy-start | bytes 2308
  70.5 15.8 %all-to-all-start.3 = ((bf16[8,96,640]{2,1,0:T(8,128)(2,1)}), bf16[8,96,640]{2,1,0:T(8,128)(2,1)S(1)}, u32[]{:S(2)}, u32[]{:S(2)}) async-start(bf16[8,96,640]{2,1,0:T(8,128)(2,1)} %shard_map.89), calls=%async_computation.3 | async-start | bytes 1966080 | tf_op jit(solution)/shard_map/all_to_all | solution.py:31
  74.1 8.9 %collective-permute-start.4 = (bf16[96,5120]{1,0:T(8,128)(2,1)S(1)}, bf16[96,5120]{1,0:T(8,128)(2,1)S(1)}, u32[]{:S(2)}, u32[]{:S(2)}) collective-permute-start(bf16[96,5120]{1,0:T(8,128)(2,1)S(1)} %get-tuple-element.31.refs_3_), channel_id=1, source_target_pairs={{0,1},{1,0},{2,3},{3,2},{4,5},{5,4},{6,7},{7,6},{8,9},{9,8},{10,11... | collective-permute-start | bytes 2949128 | tf_op jit(solution)/shard_map/ppermute | solution.py:35
  79.0 2.6 %collective-permute-start.3 = (f32[80,96]{1,0:T(8,128)S(1)}, f32[80,96]{1,0:T(8,128)S(1)}, u32[]{:S(2)}, u32[]{:S(2)}) collective-permute-start(f32[80,96]{1,0:T(8,128)S(1)} %shard_map.90), channel_id=1, source_target_pairs={{0,0},{4,8},{8,16},{12,24},{16,4},{20,12},{24,20},{28,28},{1,1},{5... | collective-permute-start | bytes 92168 | tf_op jit(solution)/shard_map/ppermute | solution.py:41
  79.7 3.3 %collective-permute-start.5 = (f32[64,96]{1,0:T(8,128)}, f32[64,96]{1,0:T(8,128)S(1)}, u32[]{:S(2)}, u32[]{:S(2)}) collective-permute-start(f32[64,96]{1,0:T(8,128)} %copy-done.8), channel_id=1, source_target_pairs={{0,1},{1,0},{2,3},{3,2},{4,5},{5,4},{6,7},{7,6},{8,9},{9,8},{10,11... | collective-permute-start | bytes 73736 | tf_op jit(solution)/shard_map/ppermute | solution.py:35
  88.1 45.0 %copy-start = (bf16[1,4,64,5120]{3,2,1,0:T(8,128)(2,1)S(1)}, bf16[1,4,64,5120]{3,2,1,0:T(8,128)(2,1)}, u32[]{:S(2)}) copy-start(bf16[1,4,64,5120]{3,2,1,0:T(8,128)(2,1)} %param.11) | copy-start | bytes 7864324
  133.0 25.0 %copy-start.6 = (f32[64,96]{1,0:T(8,128)S(1)}, f32[64,96]{1,0:T(8,128)}, u32[]{:S(2)}) copy-start(f32[64,96]{1,0:T(8,128)} %copy-done.5) | copy-start | bytes 73732

commit v6 on v5

--- a/solution.py
+++ b/solution.py
@@ -178,19 +178,31 @@
     for k, copy in enumerate(copies):
         copy.wait()
         total += parts[k].astype(F32)
+    rows = out_ref.shape[1]
+    for k in range(out_ref.shape[0]):
+        out_ref[k] = total[k * rows : (k + 1) * rows]
+
+
+def sum_kernel(parts_ref, out_ref):
+    total = parts_ref[0]
+    for k in range(1, parts_ref.shape[0]):
+        total += parts_ref[k]
     total = total.astype(BF16)
     for k in range(out_ref.shape[0]):
         out_ref[k] = total
 
 
-def error_kernel(scale, positions_ref, parts_ref, out_ref):
-    half = parts_ref.shape[1]
+def error_kernel(pair, scale, positions_ref, parts_ref, out_ref):
+    half = out_ref.shape[1]
     token_mask = (positions_ref[...] > 0).astype(F32)
     mask = jnp.where(lax.axis_index("core") == 0, token_mask[:, :half], token_mask[:, half:])
-    total = parts_ref[0].astype(F32)
-    for k in range(1, parts_ref.shape[0]):
-        total += parts_ref[k].astype(F32)
-    error = (column(mask) * total * scale).astype(BF16)
+    totals = []
+    for k in range(0, parts_ref.shape[0], pair):
+        total = parts_ref[k].astype(F32)
+        for j in range(k + 1, k + pair):
+            total += parts_ref[j].astype(F32)
+        totals.append(total)
+    error = (column(mask) * jnp.concatenate(totals, axis=0) * scale).astype(BF16)
     for k in range(out_ref.shape[0]):
         out_ref[k] = error
 
@@ -302,14 +314,18 @@
     parts, offset, other_whole, other_slope = lax.optimization_barrier((parts, offset, other_whole, other_slope))
     (parts,) = call(
         reduce_kernel,
-        [struct((far, half, wide), BF16)],
+        [struct((zh, half // zh, wide), F32)],
         [parts, offset],
         scratch=[pltpu.VMEM((near, half, wide), BF16), pltpu.SemaphoreType.DMA((near,))],
         remote=[0],
     )
+    parts = exchange(parts, ("zh",))
+    (parts,) = call(sum_kernel, [struct((far, half // zh, wide), BF16)], [parts])
     parts = exchange(parts, FAR)
     (parts,) = call(
-        functools.partial(error_kernel, 1.0 / layers), [struct((near, half, wide), BF16)], [positions[None], parts]
+        functools.partial(error_kernel, yh, 1.0 / layers),
+        [struct((near, half, wide), BF16)],
+        [positions[None], parts],
     )
     error = exchange(parts, NEAR)
     (terms,) = call(

time: 161 us -> 154 us (0.957)
  blocking collectives: 104 us -> 98.2 us
    all_to_all x5 -> x6, blocking collectives: 104 us -> 98.2 us  [exchange(): return lax.all_to_all(blocks, axes, 0, 0, tiled=True)]
    pallas_call x9 -> x10, Pallas kernels: 16.5 us -> 16.5 us  [call(): pl.pallas_call(run, out_shape=outs, in_specs=[ANY if k in remote else VME...]
where the time goes in v6:
time: 154 us
  blocking collectives  98.2 us (64%)
  starting transfers between devices  22.2 us (14%)
  Pallas kernels  16.5 us (11%)
  waiting for transfers between devices  13.9 us (9%)
  local copies, waits for them, and re-layouts  1.96 us (1%)
    all_to_all x6, blocking collectives, exchange(): return lax.all_to_all(blocks, axes, 0, 0, tiled=True)  98.2 us
    pallas_call x10, Pallas kernels, call(): pl.pallas_call(run, out_shape=outs, in_specs=[ANY if k in remote else VME...  16.5 us
    ppermute x5, starting transfers between devices, swap(): return lax.ppermute(block, 'core', [(0, 1), (1, 0)])  13 us
    all_to_all x2, waiting for transfers between devices, exchange(): return lax.all_to_all(blocks, axes, 0, 0, tiled=True)  11.4 us
    all_to_all x2, starting transfers between devices, exchange(): return lax.all_to_all(blocks, axes, 0, 0, tiled=True)  8.51 us
  transfers between devices with their start and end apart: 8, of which 4 were waited for; matrix products, arithmetic and copies ran while one was open for 0% of the time, Pallas kernels for 2%

profile of v6, /device:TPU:1, one launch (start us, length us, event | category | flops | bytes accessed | tf_op | source)
XLA Modules:
  0.0 153.5 jit_solution(17948924754850086432)
XLA Ops:
  0.6 0.0 copy-start.1
  0.6 1.6 %shard_map.86 = (bf16[16,40,96]{2,1,0:T(8,128)(2,1)}, f32[48,128]{1,0:T(8,128)}, f32[48,128]{1,0:T(8,128)}) custom-call(bf16[40,192]{1,0:T(8,128)(2,1)} %bitcast.19, bf16[40,192]{1,0:T(8,128)(2,1)} %bitcast.20, bf16[1,40]{1,0:T(2,128)(2,1)} %refs_2_.1, f32[1,64]{1,0:T(1,128)} %refs_3_.1), custom_call_target="tpu_custom_call" | custom-call | bytes 203088 | tf_op jit(solution)/shard_map/pallas_call | solution.py:49
  2.2 0.0 copy-start.9
  2.2 0.0 copy-start.4
  2.2 30.2 %all_to_all.40 = bf16[16,40,96]{2,1,0:T(8,128)(2,1)S(1)} all-to-all(bf16[16,40,96]{2,1,0:T(8,128)(2,1)} %get-tuple-element.22), channel_id=1, replica_groups=mesh['layer'=4,'x'=4,'zh'=4,'zl'=2,'yh'=2,'core'=2] {'zh','yh','core'}, dimensions={0} | all-to-all | bytes 245760 | tf_op jit(solution)/shard_map/all_to_all | solution.py:31
  32.4 1.9 %collective-permute-start.2 = (bf16[256,5120]{1,0:T(8,128)(2,1)}, bf16[256,5120]{1,0:T(8,128)(2,1)}, u32[]{:S(2)}, u32[]{:S(2)}) collective-permute-start(bf16[256,5120]{1,0:T(8,128)(2,1)} %bitcast.12), channel_id=1, source_target_pairs={{0,1},{1,0},{2,3},{3,2},{4,5},{5,4},{6,7},{7,6},{8,9},{9,8},{10,11... | collective-permute-start | bytes 7864328 | tf_op jit(solution)/shard_map/ppermute | solution.py:35
  34.3 1.1 shard_map.87
  35.4 4.9 %all-to-all-start.1 = ((bf16[8,96,640]{2,1,0:T(8,128)(2,1)}), bf16[8,96,640]{2,1,0:T(8,128)(2,1)S(1)}, u32[]{:S(2)}, u32[]{:S(2)}) async-start(bf16[8,96,640]{2,1,0:T(8,128)(2,1)} %shard_map.87), calls=%async_computation.1 | async-start | bytes 1966080 | tf_op jit(solution)/shard_map/all_to_all | solution.py:31
  40.4 0.0 copy-done.1
  40.4 2.5 %collective-permute-start = (bf16[64,5120]{1,0:T(8,128)(2,1)S(1)}, bf16[64,5120]{1,0:T(8,128)(2,1)S(1)}, u32[]{:S(2)}, u32[]{:S(2)}) collective-permute-start(bf16[64,5120]{1,0:T(8,128)(2,1)S(1)} %bitcast.16), channel_id=1, source_target_pairs={{0,1},{1,0},{2,3},{3,2},{4,5},{5,4},{6,7},{7,6},{8,9},{9,8},{10,11... | collective-permute-start | bytes 1966088 | tf_op jit(solution)/shard_map/ppermute | solution.py:35
  42.9 0.0 copy-done.9
  42.9 1.9 %collective-permute-start.1 = (f32[48,128]{1,0:T(8,128)S(1)}, f32[48,128]{1,0:T(8,128)S(1)}, u32[]{:S(2)}, u32[]{:S(2)}) collective-permute-start(f32[48,128]{1,0:T(8,128)S(1)} %copy-done.9), channel_id=1, source_target_pairs={{0,1},{1,0},{2,3},{3,2},{4,5},{5,4},{6,7},{7,6},{8,9},{9,8},{10,11... | collective-permute-start | bytes 73736 | tf_op jit(solution)/shard_map/ppermute | solution.py:35
  44.8 1.2 collective-permute-done.1.refs_4_.refs_1_
  46.0 0.0 collective-permute-done.refs_2_
  46.0 0.0 copy-start.2
  46.0 0.8 copy-done.2
  46.8 8.1 %all-to-all-done.1.refs_0_ = bf16[8,96,640]{2,1,0:T(8,128)(2,1)S(1)} async-done(((bf16[8,96,640]{2,1,0:T(8,128)(2,1)}), bf16[8,96,640]{2,1,0:T(8,128)(2,1)S(1)}, u32[]{:S(2)}, u32[]{:S(2)}) %all-to-all-start.1) | async-done | bytes 983072 | tf_op jit(solution)/shard_map/all_to_all | solution.py:31
  54.9 0.0 copy-done.4
  54.9 0.0 copy-start.3
  54.9 1.1 copy-done.3
  56.0 1.7 %shard_map.88 = (bf16[96,5120]{1,0:T(8,128)(2,1)S(1)}, bf16[4,96,128]{2,1,0:T(8,128)(2,1)S(1)}, f32[64,96]{1,0:T(8,128)S(1)}, f32[64,96]{1,0:T(8,128)S(1)}) custom-call(bf16[8,96,640]{2,1,0:T(8,128)(2,1)S(1)} %all-to-all-done.1.refs_0_, bf16[64,5120]{1,0:T(8,128)(2,1)S(1)} %bitcast.17, bf16[64,5120]{1,0:T(8,128)(2,1)S(1)} %copy-done.3, ...), custom_call_target="tpu_custom_call" | custom-call | flops 125829120 | bytes 3473408 | tf_op jit(solution)/shard_map/pallas_call | solution.py:49
  57.7 0.0 copy-start.5
  57.7 0.0 copy-start.8
  57.7 7.9 %all_to_all.41.refs_0_ = bf16[4,96,128]{2,1,0:T(8,128)(2,1)} all-to-all(bf16[4,96,128]{2,1,0:T(8,128)(2,1)S(1)} %get-tuple-element.29), channel_id=1, replica_groups=mesh['layer'=4,'x'=4,'zh'=4,'zl'=2,'yh'=2,'core'=2] {'layer'}, dimensions={0} | all-to-all | bytes 196608 | tf_op jit(solution)/shard_map/all_to_all | solution.py:31
  65.6 0.0 collective-permute-done.2.refs_2_
  65.6 4.8 %shard_map.89 = bf16[8,96,640]{2,1,0:T(8,128)(2,1)} custom-call(bf16[4,96,128]{2,1,0:T(8,128)(2,1)} %all_to_all.41.refs_0_, bf16[256,5120]{1,0:T(8,128)(2,1)} %bitcast.13, bf16[256,5120]{1,0:T(8,128)(2,1)} %collective-permute-done.2.refs_2_), custom_call_target="tpu_custom_call" | custom-call | flops 503316480 | bytes 6324224 | tf_op jit(solution)/shard_map/pallas_call | solution.py:49
  70.4 0.0 copy-done.5
  70.5 0.0 copy-done.8
  70.5 0.0 copy-start.7
  70.5 3.6 %all-to-all-start.3 = ((bf16[8,96,640]{2,1,0:T(8,128)(2,1)}), bf16[8,96,640]{2,1,0:T(8,128)(2,1)S(1)}, u32[]{:S(2)}, u32[]{:S(2)}) async-start(bf16[8,96,640]{2,1,0:T(8,128)(2,1)} %shard_map.89), calls=%async_computation.3 | async-start | bytes 1966080 | tf_op jit(solution)/shard_map/all_to_all | solution.py:31
  74.1 4.8 %collective-permute-start.4 = (bf16[96,5120]{1,0:T(8,128)(2,1)S(1)}, bf16[96,5120]{1,0:T(8,128)(2,1)S(1)}, u32[]{:S(2)}, u32[]{:S(2)}) collective-permute-start(bf16[96,5120]{1,0:T(8,128)(2,1)S(1)} %get-tuple-element.31.refs_3_), channel_id=1, source_target_pairs={{0,1},{1,0},{2,3},{3,2},{4,5},{5,4},{6,7},{7,6},{8,9},{9,8},{10,11... | collective-permute-start | bytes 2949128 | tf_op jit(solution)/shard_map/ppermute | solution.py:35
  78.8 0.2 shard_map.90
  79.0 0.7 collective-permute-start.3
  79.7 1.9 %collective-permute-start.5 = (f32[64,96]{1,0:T(8,128)}, f32[64,96]{1,0:T(8,128)S(1)}, u32[]{:S(2)}, u32[]{:S(2)}) collective-permute-start(f32[64,96]{1,0:T(8,128)} %copy-done.8), channel_id=1, source_target_pairs={{0,1},{1,0},{2,3},{3,2},{4,5},{5,4},{6,7},{7,6},{8,9},{9,8},{10,11... | collective-permute-start | bytes 73736 | tf_op jit(solution)/shard_map/ppermute | solution.py:35
  81.6 0.0 collective-permute-done.3.refs_1_
  81.6 1.4 collective-permute-done.5.refs_2_
  83.0 0.0 collective-permute-done.4.refs_4_
  83.0 3.2 %all-to-all-done.3.refs_0_ = bf16[8,96,640]{2,1,0:T(8,128)(2,1)S(1)} async-done(((bf16[8,96,640]{2,1,0:T(8,128)(2,1)}), bf16[8,96,640]{2,1,0:T(8,128)(2,1)S(1)}, u32[]{:S(2)}, u32[]{:S(2)}) %all-to-all-start.3) | async-done | bytes 983072 | tf_op jit(solution)/shard_map/all_to_all | solution.py:31
  86.2 1.8 %shard_map.91 = f32[4,24,640]{2,1,0:T(8,128)S(1)} custom-call(bf16[8,96,640]{2,1,0:T(8,128)(2,1)S(1)} %all-to-all-done.3.refs_0_, f32[80,96]{1,0:T(8,128)S(1)} %collective-permute-done.3.refs_1_), custom_call_target="tpu_custom_call" | custom-call | bytes 1259520 | tf_op jit(solution)/shard_map/pallas_call | solution.py:49
  88.0 0.0 copy-start
  88.0 13.2 %all_to_all.42.refs_0_ = f32[4,24,640]{2,1,0:T(8,128)S(1)} all-to-all(f32[4,24,640]{2,1,0:T(8,128)S(1)} %shard_map.91), channel_id=1, replica_groups=mesh['layer'=4,'x'=4,'zh'=4,'zl'=2,'yh'=2,'core'=2] {'zh'}, dimensions={0} | all-to-all | bytes 491520 | tf_op jit(solution)/shard_map/all_to_all | solution.py:31
  101.2 15.8 %all_to_all.43.refs_1_ = bf16[8,24,640]{2,1,0:T(8,128)(2,1)S(1)} all-to-all(bf16[8,24,640]{2,1,0:T(8,128)(2,1)S(1)} %shard_map.92), channel_id=1, replica_groups=mesh['layer'=4,'x'=4,'zh'=4,'zl'=2,'yh'=2,'core'=2] {'zh','yh'}, dimensions={0} | all-to-all | bytes 491520 | tf_op jit(solution)/shard_map/all_to_all | solution.py:31
  117.0 0.0 copy-done.7
  117.0 0.3 shard_map.93
  117.3 17.3 %all_to_all.44.refs_0_ = bf16[8,96,640]{2,1,0:T(8,128)(2,1)S(1)} all-to-all(bf16[8,96,640]{2,1,0:T(8,128)(2,1)S(1)} %shard_map.93), channel_id=1, replica_groups=mesh['layer'=4,'x'=4,'zh'=4,'zl'=2,'yh'=2,'core'=2] {'x','zl'}, dimensions={0} | all-to-all | bytes 1966080 | tf_op jit(solution)/shard_map/all_to_all | solution.py:31
  134.6 0.0 copy-done
  134.6 0.0 copy-start.6
  134.6 3.3 %shard_map.94 = bf16[8,64,96]{2,1,0:T(8,128)(2,1)S(1)} custom-call(bf16[8,96,640]{2,1,0:T(8,128)(2,1)S(1)} %all_to_all.44.refs_0_, bf16[256,5120]{1,0:T(8,128)(2,1)S(1)} %bitcast.14, bf16[256,5120]{1,0:T(8,128)(2,1)} %collective-permute-done.2.refs_2_), custom_call_target="tpu_custom_call" | custom-call | flops 503316480 | bytes 6324224 | tf_op jit(solution)/shard_map/pallas_call | solution.py:49
  137.9 13.8 %all_to_all.45.refs_0_ = bf16[8,64,96]{2,1,0:T(8,128)(2,1)S(1)} all-to-all(bf16[8,64,96]{2,1,0:T(8,128)(2,1)S(1)} %shard_map.94), channel_id=1, replica_groups=mesh['layer'=4,'x'=4,'zh'=4,'zl'=2,'yh'=2,'core'=2] {'layer','core'}, dimensions={0} | all-to-all | bytes 196608 | tf_op jit(solution)/shard_map/all_to_all | solution.py:31
  151.7 0.0 copy-done.6
  151.7 1.8 %shard_map.95 = (f32[64,5120]{1,0:T(8,128)}, f32[1,64]{1,0:T(1,128)}) custom-call(bf16[8,64,96]{2,1,0:T(8,128)(2,1)S(1)} %all_to_all.45.refs_0_, f32[64,96]{1,0:T(8,128)S(1)} %copy-done.6, f32[64,96]{1,0:T(8,128)S(1)} %collective-permute-done.5.refs_2_, bf16[96,5120]{1,0:T(8,128)(2,1)S(1)} %get-tuple-element.31.refs_3_, ...), custom_call_target="tpu_custom_call" | custom-call | flops 125829120 | bytes 3424512 | tf_op jit(solution)/shard_map/pallas_call | solution.py:49
  (1 shorter events, 0.0 us)
Async XLA Ops:
  0.6 39.7 %copy-start.1 = (bf16[1,64,5120]{2,1,0:T(8,128)(2,1)S(1)}, bf16[1,64,5120]{2,1,0:T(8,128)(2,1)}, u32[]{:S(2)}) copy-start(bf16[1,64,5120]{2,1,0:T(8,128)(2,1)} %param.9) | copy-start | bytes 1966084
  2.2 40.7 %copy-start.9 = (f32[48,128]{1,0:T(8,128)S(1)}, f32[48,128]{1,0:T(8,128)}, u32[]{:S(2)}) copy-start(f32[48,128]{1,0:T(8,128)} %get-tuple-element.28) | copy-start | bytes 73732
  2.2 52.7 %copy-start.4 = (f32[48,128]{1,0:T(8,128)S(1)}, f32[48,128]{1,0:T(8,128)}, u32[]{:S(2)}) copy-start(f32[48,128]{1,0:T(8,128)} %get-tuple-element.27.refs_3_.refs_0_) | copy-start | bytes 73732
  32.4 33.2 %collective-permute-start.2 = (bf16[256,5120]{1,0:T(8,128)(2,1)}, bf16[256,5120]{1,0:T(8,128)(2,1)}, u32[]{:S(2)}, u32[]{:S(2)}) collective-permute-start(bf16[256,5120]{1,0:T(8,128)(2,1)} %bitcast.12), channel_id=1, source_target_pairs={{0,1},{1,0},{2,3},{3,2},{4,5},{5,4},{6,7},{7,6},{8,9},{9,8},{10,11... | collective-permute-start | bytes 7864328 | tf_op jit(solution)/shard_map/ppermute | solution.py:35
  35.4 19.5 %all-to-all-start.1 = ((bf16[8,96,640]{2,1,0:T(8,128)(2,1)}), bf16[8,96,640]{2,1,0:T(8,128)(2,1)S(1)}, u32[]{:S(2)}, u32[]{:S(2)}) async-start(bf16[8,96,640]{2,1,0:T(8,128)(2,1)} %shard_map.87), calls=%async_computation.1 | async-start | bytes 1966080 | tf_op jit(solution)/shard_map/all_to_all | solution.py:31
  40.4 5.6 %collective-permute-start = (bf16[64,5120]{1,0:T(8,128)(2,1)S(1)}, bf16[64,5120]{1,0:T(8,128)(2,1)S(1)}, u32[]{:S(2)}, u32[]{:S(2)}) collective-permute-start(bf16[64,5120]{1,0:T(8,128)(2,1)S(1)} %bitcast.16), channel_id=1, source_target_pairs={{0,1},{1,0},{2,3},{3,2},{4,5},{5,4},{6,7},{7,6},{8,9},{9,8},{10,11... | collective-permute-start | bytes 1966088 | tf_op jit(solution)/shard_map/ppermute | solution.py:35
  42.9 3.1 %collective-permute-start.1 = (f32[48,128]{1,0:T(8,128)S(1)}, f32[48,128]{1,0:T(8,128)S(1)}, u32[]{:S(2)}, u32[]{:S(2)}) collective-permute-start(f32[48,128]{1,0:T(8,128)S(1)} %copy-done.9), channel_id=1, source_target_pairs={{0,1},{1,0},{2,3},{3,2},{4,5},{5,4},{6,7},{7,6},{8,9},{9,8},{10,11... | collective-permute-start | bytes 73736 | tf_op jit(solution)/shard_map/ppermute | solution.py:35
  46.0 0.8 copy-start.2
  54.9 1.1 copy-start.3
  57.7 12.7 %copy-start.5 = (f32[64,96]{1,0:T(8,128)}, f32[64,96]{1,0:T(8,128)S(1)}, u32[]{:S(2)}) copy-start(f32[64,96]{1,0:T(8,128)S(1)} %get-tuple-element.35.refs_1_) | copy-start | bytes 73732
  57.7 12.7 %copy-start.8 = (f32[64,96]{1,0:T(8,128)}, f32[64,96]{1,0:T(8,128)S(1)}, u32[]{:S(2)}) copy-start(f32[64,96]{1,0:T(8,128)S(1)} %get-tuple-element.32) | copy-start | bytes 73732
  70.5 46.5 %copy-start.7 = (s32[192]{0:T(256)S(1)}, s32[192]{0:T(256)}, u32[]{:S(2)}) copy-start(s32[192]{0:T(256)} %param.13) | copy-start | bytes 2308
  70.5 15.8 %all-to-all-start.3 = ((bf16[8,96,640]{2,1,0:T(8,128)(2,1)}), bf16[8,96,640]{2,1,0:T(8,128)(2,1)S(1)}, u32[]{:S(2)}, u32[]{:S(2)}) async-start(bf16[8,96,640]{2,1,0:T(8,128)(2,1)} %shard_map.89), calls=%async_computation.3 | async-start | bytes 1966080 | tf_op jit(solution)/shard_map/all_to_all | solution.py:31
  74.1 8.9 %collective-permute-start.4 = (bf16[96,5120]{1,0:T(8,128)(2,1)S(1)}, bf16[96,5120]{1,0:T(8,128)(2,1)S(1)}, u32[]{:S(2)}, u32[]{:S(2)}) collective-permute-start(bf16[96,5120]{1,0:T(8,128)(2,1)S(1)} %get-tuple-element.31.refs_3_), channel_id=1, source_target_pairs={{0,1},{1,0},{2,3},{3,2},{4,5},{5,4},{6,7},{7,6},{8,9},{9,8},{10,11... | collective-permute-start | bytes 2949128 | tf_op jit(solution)/shard_map/ppermute | solution.py:35
  79.0 2.6 %collective-permute-start.3 = (f32[80,96]{1,0:T(8,128)S(1)}, f32[80,96]{1,0:T(8,128)S(1)}, u32[]{:S(2)}, u32[]{:S(2)}) collective-permute-start(f32[80,96]{1,0:T(8,128)S(1)} %shard_map.90), channel_id=1, source_target_pairs={{0,0},{4,8},{8,16},{12,24},{16,4},{20,12},{24,20},{28,28},{1,1},{5... | collective-permute-start | bytes 92168 | tf_op jit(solution)/shard_map/ppermute | solution.py:41
  79.7 3.3 %collective-permute-start.5 = (f32[64,96]{1,0:T(8,128)}, f32[64,96]{1,0:T(8,128)S(1)}, u32[]{:S(2)}, u32[]{:S(2)}) collective-permute-start(f32[64,96]{1,0:T(8,128)} %copy-done.8), channel_id=1, source_target_pairs={{0,1},{1,0},{2,3},{3,2},{4,5},{5,4},{6,7},{7,6},{8,9},{9,8},{10,11... | collective-permute-start | bytes 73736 | tf_op jit(solution)/shard_map/ppermute | solution.py:35
  88.0 46.6 %copy-start = (bf16[1,4,64,5120]{3,2,1,0:T(8,128)(2,1)S(1)}, bf16[1,4,64,5120]{3,2,1,0:T(8,128)(2,1)}, u32[]{:S(2)}) copy-start(bf16[1,4,64,5120]{3,2,1,0:T(8,128)(2,1)} %param.11) | copy-start | bytes 7864324
  134.6 17.1 %copy-start.6 = (f32[64,96]{1,0:T(8,128)S(1)}, f32[64,96]{1,0:T(8,128)}, u32[]{:S(2)}) copy-start(f32[64,96]{1,0:T(8,128)} %copy-done.5) | copy-start | bytes 73732

commit v7 on v6

--- a/solution.py
+++ b/solution.py
@@ -138,15 +138,16 @@
     out.wait()
 
 
-def decode_kernel(codes_ref, own_hbm, sent_hbm, out_hbm, own_ref, sent_ref, total_ref, out_ref, sems):
+def copy_kernel(source_hbm, out_ref, sems):
+    copy = start(source_hbm, out_ref, sems.at[0])
+    copy.wait()
+
+
+def decode_kernel(codes_ref, own_ref, sent_hbm, out_hbm, sent_ref, total_ref, out_ref, sems):
+    copy = start(sent_hbm, sent_ref, sems.at[0])
+    section = lax.axis_index("layer")
     layers, _, latents = codes_ref.shape
     latents //= 2
-    copies = []
-    for k, (source, target) in enumerate(((own_hbm, own_ref), (sent_hbm, sent_ref))):
-        for layer in range(layers):
-            rows = slice(layer * latents, (layer + 1) * latents)
-            copies.append(start(source.at[rows], target.at[rows], sems.at[k, layer]))
-    section = lax.axis_index("layer")
     codes = []
     for layer in range(layers):
         code = codes_ref[layer]
@@ -154,30 +155,25 @@
     own = jnp.concatenate([code[:, :latents] for code in codes], axis=1)
     sent = jnp.concatenate([code[:, latents:] for code in codes], axis=1)
     parts = columns(out_ref.shape[0], out_ref.shape[2])
-    for copy in copies[:layers]:
-        copy.wait()
     for k, part in enumerate(parts):
         total_ref[k] = dot(own, own_ref[:, part], ((1,), (0,)))
-    for copy in copies[layers:]:
-        copy.wait()
+    copy.wait()
     results = []
     for k, part in enumerate(parts):
         out_ref[k] = (total_ref[k] + dot(sent, sent_ref[:, part], ((1,), (0,)))).astype(BF16)
-        results.append(start(out_ref.at[k], out_hbm.at[k], sems.at[2, k]))
+        results.append(start(out_ref.at[k], out_hbm.at[k], sems.at[1 + k]))
     for copy in results:
         copy.wait()
 
 
-def reduce_kernel(parts_hbm, offset_ref, out_ref, parts, sems):
+def reduce_kernel(parts_ref, offset_ref, out_ref):
     place = lax.axis_index(FAR)
-    copies = [start(parts_hbm.at[k], parts.at[k], sems.at[k]) for k in range(parts.shape[0])]
     size = offset_ref.shape[0]
-    tile = jnp.concatenate([offset_ref[...].T] * (parts.shape[2] // size), axis=1)
+    tile = jnp.concatenate([offset_ref[...].T] * (parts_ref.shape[2] // size), axis=1)
     lane = lax.broadcasted_iota(jnp.int32, tile.shape, 1)
     total = jnp.where((lane >= place * size) & (lane < (place + 1) * size), -tile, jnp.zeros_like(tile))
-    for k, copy in enumerate(copies):
-        copy.wait()
-        total += parts[k].astype(F32)
+    for k in range(parts_ref.shape[0]):
+        total += parts_ref[k].astype(F32)
     rows = out_ref.shape[1]
     for k in range(out_ref.shape[0]):
         out_ref[k] = total[k * rows : (k + 1) * rows]
@@ -207,11 +203,13 @@
         out_ref[k] = error
 
 
-def back_kernel(error_ref, own_ref, sent_ref, out_ref):
+def back_kernel(error_ref, own_ref, sent_hbm, out_ref, sent_ref, sems):
+    copy = start(sent_hbm, sent_ref, sems.at[0])
     section = lax.axis_index("layer")
     first = lax.axis_index("core") == 0
     error = jnp.concatenate([error_ref[k] for k in range(error_ref.shape[0])], axis=1)
     own = dot(own_ref[...], error, ((1,), (1,)))
+    copy.wait()
     sent = dot(sent_ref[...], error, ((1,), (1,)))
     latents = out_ref.shape[1]
     for layer in range(out_ref.shape[0] // 2):
@@ -270,6 +268,14 @@
     other_decoders = swap(sent_decoders)
     (sends,) = call(flip_kernel, [struct((near, half, wide), BF16)], [block])
     blocks = exchange(sends, NEAR)
+    (held_decoders,) = call(
+        copy_kernel,
+        [struct((layers * latents, model), BF16)],
+        [sent_decoders],
+        scratch=[pltpu.SemaphoreType.DMA((1,))],
+        remote=[0],
+    )
+    blocks, held_decoders = lax.optimization_barrier((blocks, held_decoders))
     whole, codes, own_slope, sent_slope = call(
         functools.partial(encode_kernel, (xs, zh, zl, wide // zh, width)),
         [
@@ -297,17 +303,16 @@
     (parts,) = call(
         decode_kernel,
         [struct((near, half, wide), BF16)],
-        [codes, own_decoders, other_decoders],
+        [codes, held_decoders, other_decoders],
         scratch=[
-            pltpu.VMEM((layers * latents, model), BF16),
             pltpu.VMEM((layers * latents, model), BF16),
             pltpu.VMEM((near, half, wide), F32),
             pltpu.VMEM((near, half, wide), BF16),
-            pltpu.SemaphoreType.DMA((3, near)),
+            pltpu.SemaphoreType.DMA((1 + near,)),
         ],
-        remote=[1, 2],
+        remote=[2],
         remote_outs=[0],
-        mib=62,
+        mib=24,
         flops=4 * layers * half * latents * model,
     )
     parts = exchange(parts, NEAR)
@@ -316,8 +321,6 @@
         reduce_kernel,
         [struct((zh, half // zh, wide), F32)],
         [parts, offset],
-        scratch=[pltpu.VMEM((near, half, wide), BF16), pltpu.SemaphoreType.DMA((near,))],
-        remote=[0],
     )
     parts = exchange(parts, ("zh",))
     (parts,) = call(sum_kernel, [struct((far, half // zh, wide), BF16)], [parts])
@@ -331,7 +334,9 @@
     (terms,) = call(
         back_kernel,
         [struct((2 * layers, latents, half), BF16)],
-        [error, own_decoders, other_decoders],
+        [error, held_decoders, other_decoders],
+        scratch=[pltpu.VMEM((layers * latents, model), BF16), pltpu.SemaphoreType.DMA((1,))],
+        remote=[2],
         flops=4 * layers * half * latents * model,
     )
     terms = exchange(terms, ("layer", "core"))

time: 154 us -> 157 us (1.019)
  waiting for transfers between devices: 13.9 us -> 12 us
  Pallas kernels: 16.5 us -> 18.4 us
  local copies, waits for them, and re-layouts: 1.96 us -> 3.66 us
    pallas_call x10 -> x11, Pallas kernels: 16.5 us -> 18.4 us  [call(): pl.pallas_call(run, out_shape=outs, in_specs=[ANY if k in remote else VME...]
    unnamed x20, local copies, waits for them, and re-layouts: 1.96 us -> 3.66 us
  transfers between devices with their start and end apart: 8 -> 8, of which waited for: 4 -> 3; matrix products, arithmetic and copies ran while one was open for 0% -> 0% of each run, Pallas kernels for 2% -> 3%
where the time goes in v7:
time: 157 us; the launch traced here: 156 us
  blocking collectives  97.9 us (62%)
  starting transfers between devices  23.1 us (15%)
  Pallas kernels  18.4 us (12%)
  waiting for transfers between devices  12 us (8%)
  local copies, waits for them, and re-layouts  3.66 us (2%)
    all_to_all x6, blocking collectives, exchange(): return lax.all_to_all(blocks, axes, 0, 0, tiled=True)  97.9 us
    pallas_call x11, Pallas kernels, call(): pl.pallas_call(run, out_shape=outs, in_specs=[ANY if k in remote else VME...  18.4 us
    ppermute x5, starting transfers between devices, swap(): return lax.ppermute(block, 'core', [(0, 1), (1, 0)])  13 us
    all_to_all x2, waiting for transfers between devices, exchange(): return lax.all_to_all(blocks, axes, 0, 0, tiled=True)  10.8 us
    all_to_all x2, starting transfers between devices, exchange(): return lax.all_to_all(blocks, axes, 0, 0, tiled=True)  9.44 us
    unnamed x20, local copies, waits for them, and re-layouts  3.66 us
  transfers between devices with their start and end apart: 8, of which 3 were waited for; matrix products, arithmetic and copies ran while one was open for 0% of the time, Pallas kernels for 3%

profile of v7, /device:TPU:1, one launch (start us, length us, event | category | flops | bytes accessed | tf_op | source)
XLA Modules:
  0.0 156.0 jit_solution(10677697646128254921)
XLA Ops:
  0.6 0.0 copy-start.6
  0.6 1.6 %shard_map.86 = (bf16[16,40,96]{2,1,0:T(8,128)(2,1)}, f32[48,128]{1,0:T(8,128)}, f32[48,128]{1,0:T(8,128)}) custom-call(bf16[40,192]{1,0:T(8,128)(2,1)} %bitcast.18, bf16[40,192]{1,0:T(8,128)(2,1)} %bitcast.19, bf16[1,40]{1,0:T(2,128)(2,1)} %refs_2_.1, f32[1,64]{1,0:T(1,128)} %refs_3_.1), custom_call_target="tpu_custom_call" | custom-call | bytes 203088 | tf_op jit(solution)/shard_map/pallas_call | solution.py:49
  2.2 0.0 copy-start.9
  2.2 30.2 %all_to_all.40 = bf16[16,40,96]{2,1,0:T(8,128)(2,1)S(1)} all-to-all(bf16[16,40,96]{2,1,0:T(8,128)(2,1)} %get-tuple-element.24), channel_id=1, replica_groups=mesh['layer'=4,'x'=4,'zh'=4,'zl'=2,'yh'=2,'core'=2] {'zh','yh','core'}, dimensions={0} | all-to-all | bytes 245760 | tf_op jit(solution)/shard_map/all_to_all | solution.py:31
  32.4 1.9 %collective-permute-start.2 = (bf16[256,5120]{1,0:T(8,128)(2,1)}, bf16[256,5120]{1,0:T(8,128)(2,1)}, u32[]{:S(2)}, u32[]{:S(2)}) collective-permute-start(bf16[256,5120]{1,0:T(8,128)(2,1)} %bitcast.12), channel_id=1, source_target_pairs={{0,1},{1,0},{2,3},{3,2},{4,5},{5,4},{6,7},{7,6},{8,9},{9,8},{10,11... | collective-permute-start | bytes 7864328 | tf_op jit(solution)/shard_map/ppermute | solution.py:35
  34.3 1.1 shard_map.87
  35.4 0.0 copy-start.7
  35.4 5.1 %all-to-all-start.1 = ((bf16[8,96,640]{2,1,0:T(8,128)(2,1)}), bf16[8,96,640]{2,1,0:T(8,128)(2,1)}, u32[]{:S(2)}, u32[]{:S(2)}) async-start(bf16[8,96,640]{2,1,0:T(8,128)(2,1)} %shard_map.87), calls=%async_computation.1 | async-start | bytes 1966080 | tf_op jit(solution)/shard_map/all_to_all | solution.py:31
  40.5 0.0 copy-done.6
  40.5 2.5 %collective-permute-start = (bf16[64,5120]{1,0:T(8,128)(2,1)S(1)}, bf16[64,5120]{1,0:T(8,128)(2,1)}, u32[]{:S(2)}, u32[]{:S(2)}) collective-permute-start(bf16[64,5120]{1,0:T(8,128)(2,1)S(1)} %bitcast.15), channel_id=1, source_target_pairs={{0,1},{1,0},{2,3},{3,2},{4,5},{5,4},{6,7},{7,6},{8,9},{9,8},{10,11... | collective-permute-start | bytes 1966088 | tf_op jit(solution)/shard_map/ppermute | solution.py:35
  43.0 0.0 copy-done.9
  43.0 1.9 %collective-permute-start.1 = (f32[48,128]{1,0:T(8,128)S(1)}, f32[48,128]{1,0:T(8,128)S(1)}, u32[]{:S(2)}, u32[]{:S(2)}) collective-permute-start(f32[48,128]{1,0:T(8,128)S(1)} %copy-done.9), channel_id=1, source_target_pairs={{0,1},{1,0},{2,3},{3,2},{4,5},{5,4},{6,7},{7,6},{8,9},{9,8},{10,11... | collective-permute-start | bytes 73736 | tf_op jit(solution)/shard_map/ppermute | solution.py:35
  44.9 0.0 copy-start.1
  45.0 1.7 %copy-done.1 = bf16[1,4,64,5120]{3,2,1,0:T(8,128)(2,1)S(1)} copy-done((bf16[1,4,64,5120]{3,2,1,0:T(8,128)(2,1)S(1)}, bf16[1,4,64,5120]{3,2,1,0:T(8,128)(2,1)}, u32[]{:S(2)}) %copy-start.1) | copy-done | bytes 2621464
  46.7 0.2 shard_map.88.refs_1_
  46.9 8.3 %all-to-all-done.1.refs_0_ = bf16[8,96,640]{2,1,0:T(8,128)(2,1)} async-done(((bf16[8,96,640]{2,1,0:T(8,128)(2,1)}), bf16[8,96,640]{2,1,0:T(8,128)(2,1)}, u32[]{:S(2)}, u32[]{:S(2)}) %all-to-all-start.1) | async-done | bytes 983072 | tf_op jit(solution)/shard_map/all_to_all | solution.py:31
  55.2 0.0 collective-permute-done.1.refs_4_.refs_1_
  55.2 0.0 collective-permute-done.refs_2_
  55.2 0.0 copy-done.7
  55.2 3.2 %shard_map.89 = (bf16[96,5120]{1,0:T(8,128)(2,1)S(1)}, bf16[4,96,128]{2,1,0:T(8,128)(2,1)S(1)}, f32[64,96]{1,0:T(8,128)S(1)}, f32[64,96]{1,0:T(8,128)S(1)}) custom-call(bf16[8,96,640]{2,1,0:T(8,128)(2,1)} %all-to-all-done.1.refs_0_, bf16[64,5120]{1,0:T(8,128)(2,1)S(1)} %bitcast.16, bf16[64,5120]{1,0:T(8,128)(2,1)} %collective-permute-done.refs_2_, ...), custom_call_target="tpu_custom_call" | custom-call | flops 125829120 | bytes 3473408 | tf_op jit(solution)/shard_map/pallas_call | solution.py:49
  58.4 0.0 copy-start.2
  58.4 7.8 %all_to_all.41.refs_0_ = bf16[4,96,128]{2,1,0:T(8,128)(2,1)S(1)} all-to-all(bf16[4,96,128]{2,1,0:T(8,128)(2,1)S(1)} %get-tuple-element.33), channel_id=1, replica_groups=mesh['layer'=4,'x'=4,'zh'=4,'zl'=2,'yh'=2,'core'=2] {'layer'}, dimensions={0} | all-to-all | bytes 196608 | tf_op jit(solution)/shard_map/all_to_all | solution.py:31
  66.2 0.0 copy-done.2
  66.2 0.0 collective-permute-done.2.refs_2_
  66.2 5.2 %shard_map.90 = bf16[8,96,640]{2,1,0:T(8,128)(2,1)S(1)} custom-call(bf16[4,96,128]{2,1,0:T(8,128)(2,1)S(1)} %all_to_all.41.refs_0_, bf16[256,5120]{1,0:T(8,128)(2,1)S(1)} %shard_map.88.refs_1_, bf16[256,5120]{1,0:T(8,128)(2,1)} %collective-permute-done.2.refs_2_), custom_call_target="tpu_custom_call" | custom-call | flops 503316480 | bytes 6324224 | tf_op jit(solution)/shard_map/pallas_call | solution.py:49
  71.4 0.0 copy-start
  71.4 0.9 copy-done
  72.3 0.0 copy-start.8
  72.3 4.4 %all-to-all-start.3 = ((bf16[8,96,640]{2,1,0:T(8,128)(2,1)}), bf16[8,96,640]{2,1,0:T(8,128)(2,1)}, u32[]{:S(2)}, u32[]{:S(2)}) async-start(bf16[8,96,640]{2,1,0:T(8,128)(2,1)} %copy-done), calls=%async_computation.3 | async-start | bytes 1966080 | tf_op jit(solution)/shard_map/all_to_all | solution.py:31
  76.7 4.8 %collective-permute-start.4 = (bf16[96,5120]{1,0:T(8,128)(2,1)}, bf16[96,5120]{1,0:T(8,128)(2,1)S(1)}, u32[]{:S(2)}, u32[]{:S(2)}) collective-permute-start(bf16[96,5120]{1,0:T(8,128)(2,1)} %copy-done.2), channel_id=1, source_target_pairs={{0,1},{1,0},{2,3},{3,2},{4,5},{5,4},{6,7},{7,6},{8,9},{9,8},{10,11... | collective-permute-start | bytes 2949128 | tf_op jit(solution)/shard_map/ppermute | solution.py:35
  81.5 0.2 shard_map.91
  81.7 0.7 collective-permute-start.3
  82.4 1.9 %collective-permute-start.5 = (f32[64,96]{1,0:T(8,128)S(1)}, f32[64,96]{1,0:T(8,128)S(1)}, u32[]{:S(2)}, u32[]{:S(2)}) collective-permute-start(f32[64,96]{1,0:T(8,128)S(1)} %get-tuple-element.36), channel_id=1, source_target_pairs={{0,1},{1,0},{2,3},{3,2},{4,5},{5,4},{6,7},{7,6},{8,9},{9,8},{10,11... | collective-permute-start | bytes 73736 | tf_op jit(solution)/shard_map/ppermute | solution.py:35
  84.3 0.0 collective-permute-done.3.refs_1_
  84.3 1.2 collective-permute-done.5.refs_2_
  85.5 0.0 collective-permute-done.4.refs_4_
  85.5 0.0 copy-start.4
  85.5 1.0 copy-done.4
  86.4 2.5 %all-to-all-done.3.refs_0_ = bf16[8,96,640]{2,1,0:T(8,128)(2,1)} async-done(((bf16[8,96,640]{2,1,0:T(8,128)(2,1)}), bf16[8,96,640]{2,1,0:T(8,128)(2,1)}, u32[]{:S(2)}, u32[]{:S(2)}) %all-to-all-start.3) | async-done | bytes 983072 | tf_op jit(solution)/shard_map/all_to_all | solution.py:31
  89.0 1.5 shard_map.92
  90.5 14.4 %all_to_all.42.refs_0_ = f32[4,24,640]{2,1,0:T(8,128)S(1)} all-to-all(f32[4,24,640]{2,1,0:T(8,128)S(1)} %shard_map.92), channel_id=1, replica_groups=mesh['layer'=4,'x'=4,'zh'=4,'zl'=2,'yh'=2,'core'=2] {'zh'}, dimensions={0} | all-to-all | bytes 491520 | tf_op jit(solution)/shard_map/all_to_all | solution.py:31
  104.9 15.8 %all_to_all.43.refs_1_ = bf16[8,24,640]{2,1,0:T(8,128)(2,1)S(1)} all-to-all(bf16[8,24,640]{2,1,0:T(8,128)(2,1)S(1)} %shard_map.93), channel_id=1, replica_groups=mesh['layer'=4,'x'=4,'zh'=4,'zl'=2,'yh'=2,'core'=2] {'zh','yh'}, dimensions={0} | all-to-all | bytes 491520 | tf_op jit(solution)/shard_map/all_to_all | solution.py:31
  120.7 0.0 copy-done.8
  120.7 0.3 shard_map.94
  121.0 16.1 %all_to_all.44.refs_0_ = bf16[8,96,640]{2,1,0:T(8,128)(2,1)S(1)} all-to-all(bf16[8,96,640]{2,1,0:T(8,128)(2,1)S(1)} %shard_map.94), channel_id=1, replica_groups=mesh['layer'=4,'x'=4,'zh'=4,'zl'=2,'yh'=2,'core'=2] {'x','zl'}, dimensions={0} | all-to-all | bytes 1966080 | tf_op jit(solution)/shard_map/all_to_all | solution.py:31
  137.1 0.0 copy-start.3
  137.1 0.0 copy-start.5
  137.1 3.4 %shard_map.95 = bf16[8,64,96]{2,1,0:T(8,128)(2,1)S(1)} custom-call(bf16[8,96,640]{2,1,0:T(8,128)(2,1)S(1)} %all_to_all.44.refs_0_, bf16[256,5120]{1,0:T(8,128)(2,1)S(1)} %shard_map.88.refs_1_, bf16[256,5120]{1,0:T(8,128)(2,1)} %collective-permute-done.2.refs_2_), custom_call_target="tpu_custom_call" | custom-call | flops 503316480 | bytes 6324224 | tf_op jit(solution)/shard_map/pallas_call | solution.py:49
  140.5 13.6 %all_to_all.45.refs_0_ = bf16[8,64,96]{2,1,0:T(8,128)(2,1)S(1)} all-to-all(bf16[8,64,96]{2,1,0:T(8,128)(2,1)S(1)} %shard_map.95), channel_id=1, replica_groups=mesh['layer'=4,'x'=4,'zh'=4,'zl'=2,'yh'=2,'core'=2] {'layer','core'}, dimensions={0} | all-to-all | bytes 196608 | tf_op jit(solution)/shard_map/all_to_all | solution.py:31
  154.1 0.0 copy-done.3
  154.1 0.0 copy-done.5
  154.1 1.8 %shard_map.96 = (f32[64,5120]{1,0:T(8,128)}, f32[1,64]{1,0:T(1,128)}) custom-call(bf16[8,64,96]{2,1,0:T(8,128)(2,1)S(1)} %all_to_all.45.refs_0_, f32[64,96]{1,0:T(8,128)S(1)} %get-tuple-element.39.refs_1_, f32[64,96]{1,0:T(8,128)S(1)} %collective-permute-done.5.refs_2_, bf16[96,5120]{1,0:T(8,128)(2,1)S(1)} %copy-done.3, bf16[96,5120]{1,0:T(8,128)(2,1)S(1)} %copy-done.5), custom_call_target="tpu_custom_call" | custom-call | flops 125829120 | bytes 3424512 | tf_op jit(solution)/shard_map/pallas_call | solution.py:49
  (1 shorter events, 0.0 us)
Async XLA Ops:
  0.6 39.9 %copy-start.6 = (bf16[1,64,5120]{2,1,0:T(8,128)(2,1)S(1)}, bf16[1,64,5120]{2,1,0:T(8,128)(2,1)}, u32[]{:S(2)}) copy-start(bf16[1,64,5120]{2,1,0:T(8,128)(2,1)} %param.9) | copy-start | bytes 1966084
  2.2 40.8 %copy-start.9 = (f32[48,128]{1,0:T(8,128)S(1)}, f32[48,128]{1,0:T(8,128)}, u32[]{:S(2)}) copy-start(f32[48,128]{1,0:T(8,128)} %get-tuple-element.32) | copy-start | bytes 73732
  32.4 33.7 %collective-permute-start.2 = (bf16[256,5120]{1,0:T(8,128)(2,1)}, bf16[256,5120]{1,0:T(8,128)(2,1)}, u32[]{:S(2)}, u32[]{:S(2)}) collective-permute-start(bf16[256,5120]{1,0:T(8,128)(2,1)} %bitcast.12), channel_id=1, source_target_pairs={{0,1},{1,0},{2,3},{3,2},{4,5},{5,4},{6,7},{7,6},{8,9},{9,8},{10,11... | collective-permute-start | bytes 7864328 | tf_op jit(solution)/shard_map/ppermute | solution.py:35
  35.4 19.7 %copy-start.7 = (f32[48,128]{1,0:T(8,128)S(1)}, f32[48,128]{1,0:T(8,128)}, u32[]{:S(2)}) copy-start(f32[48,128]{1,0:T(8,128)} %get-tuple-element.31.refs_3_.refs_0_) | copy-start | bytes 73732
  35.4 19.7 %all-to-all-start.1 = ((bf16[8,96,640]{2,1,0:T(8,128)(2,1)}), bf16[8,96,640]{2,1,0:T(8,128)(2,1)}, u32[]{:S(2)}, u32[]{:S(2)}) async-start(bf16[8,96,640]{2,1,0:T(8,128)(2,1)} %shard_map.87), calls=%async_computation.1 | async-start | bytes 1966080 | tf_op jit(solution)/shard_map/all_to_all | solution.py:31
  40.5 14.7 %collective-permute-start = (bf16[64,5120]{1,0:T(8,128)(2,1)S(1)}, bf16[64,5120]{1,0:T(8,128)(2,1)}, u32[]{:S(2)}, u32[]{:S(2)}) collective-permute-start(bf16[64,5120]{1,0:T(8,128)(2,1)S(1)} %bitcast.15), channel_id=1, source_target_pairs={{0,1},{1,0},{2,3},{3,2},{4,5},{5,4},{6,7},{7,6},{8,9},{9,8},{10,11... | collective-permute-start | bytes 1966088 | tf_op jit(solution)/shard_map/ppermute | solution.py:35
  43.0 12.2 %collective-permute-start.1 = (f32[48,128]{1,0:T(8,128)S(1)}, f32[48,128]{1,0:T(8,128)S(1)}, u32[]{:S(2)}, u32[]{:S(2)}) collective-permute-start(f32[48,128]{1,0:T(8,128)S(1)} %copy-done.9), channel_id=1, source_target_pairs={{0,1},{1,0},{2,3},{3,2},{4,5},{5,4},{6,7},{7,6},{8,9},{9,8},{10,11... | collective-permute-start | bytes 73736 | tf_op jit(solution)/shard_map/ppermute | solution.py:35
  44.9 1.7 %copy-start.1 = (bf16[1,4,64,5120]{3,2,1,0:T(8,128)(2,1)S(1)}, bf16[1,4,64,5120]{3,2,1,0:T(8,128)(2,1)}, u32[]{:S(2)}) copy-start(bf16[1,4,64,5120]{3,2,1,0:T(8,128)(2,1)} %param.11) | copy-start | bytes 7864324
  58.4 7.8 %copy-start.2 = (bf16[96,5120]{1,0:T(8,128)(2,1)}, bf16[96,5120]{1,0:T(8,128)(2,1)S(1)}, u32[]{:S(2)}) copy-start(bf16[96,5120]{1,0:T(8,128)(2,1)S(1)} %get-tuple-element.35.refs_3_) | copy-start | bytes 2949124
  71.4 0.9 copy-start
  72.3 48.4 %copy-start.8 = (s32[192]{0:T(256)S(1)}, s32[192]{0:T(256)}, u32[]{:S(2)}) copy-start(s32[192]{0:T(256)} %param.13) | copy-start | bytes 2308
  72.3 16.6 %all-to-all-start.3 = ((bf16[8,96,640]{2,1,0:T(8,128)(2,1)}), bf16[8,96,640]{2,1,0:T(8,128)(2,1)}, u32[]{:S(2)}, u32[]{:S(2)}) async-start(bf16[8,96,640]{2,1,0:T(8,128)(2,1)} %copy-done), calls=%async_computation.3 | async-start | bytes 1966080 | tf_op jit(solution)/shard_map/all_to_all | solution.py:31
  76.7 8.7 %collective-permute-start.4 = (bf16[96,5120]{1,0:T(8,128)(2,1)}, bf16[96,5120]{1,0:T(8,128)(2,1)S(1)}, u32[]{:S(2)}, u32[]{:S(2)}) collective-permute-start(bf16[96,5120]{1,0:T(8,128)(2,1)} %copy-done.2), channel_id=1, source_target_pairs={{0,1},{1,0},{2,3},{3,2},{4,5},{5,4},{6,7},{7,6},{8,9},{9,8},{10,11... | collective-permute-start | bytes 2949128 | tf_op jit(solution)/shard_map/ppermute | solution.py:35
  81.7 2.6 %collective-permute-start.3 = (f32[80,96]{1,0:T(8,128)S(1)}, f32[80,96]{1,0:T(8,128)S(1)}, u32[]{:S(2)}, u32[]{:S(2)}) collective-permute-start(f32[80,96]{1,0:T(8,128)S(1)} %shard_map.91), channel_id=1, source_target_pairs={{0,0},{4,8},{8,16},{12,24},{16,4},{20,12},{24,20},{28,28},{1,1},{5... | collective-permute-start | bytes 92168 | tf_op jit(solution)/shard_map/ppermute | solution.py:41
  82.4 3.1 %collective-permute-start.5 = (f32[64,96]{1,0:T(8,128)S(1)}, f32[64,96]{1,0:T(8,128)S(1)}, u32[]{:S(2)}, u32[]{:S(2)}) collective-permute-start(f32[64,96]{1,0:T(8,128)S(1)} %get-tuple-element.36), channel_id=1, source_target_pairs={{0,1},{1,0},{2,3},{3,2},{4,5},{5,4},{6,7},{7,6},{8,9},{9,8},{10,11... | collective-permute-start | bytes 73736 | tf_op jit(solution)/shard_map/ppermute | solution.py:35
  85.5 1.0 copy-start.4
  137.1 17.0 %copy-start.3 = (bf16[96,5120]{1,0:T(8,128)(2,1)S(1)}, bf16[96,5120]{1,0:T(8,128)(2,1)}, u32[]{:S(2)}) copy-start(bf16[96,5120]{1,0:T(8,128)(2,1)} %copy-done.2) | copy-start | bytes 2949124
  137.1 17.0 %copy-start.5 = (bf16[96,5120]{1,0:T(8,128)(2,1)S(1)}, bf16[96,5120]{1,0:T(8,128)(2,1)}, u32[]{:S(2)}) copy-start(bf16[96,5120]{1,0:T(8,128)(2,1)} %copy-done.4) | copy-start | bytes 2949124

commit v8 on v6

--- a/solution.py
+++ b/solution.py
@@ -349,7 +349,7 @@
 LATENT = ("x", "zh", "zl", "yh", "core")
 
 
-def solution(mesh, parts=(4, 4, 2, 2, 2)):
+def solution(mesh, parts=(4, 8, 1, 2, 2)):
     in_specs = (
         P("layer", None, LATENT),
         P("layer", None, LATENT),

time: 154 us -> 179 us (1.16)
  blocking collectives: 98.2 us -> 118 us
  waiting for transfers between devices: 13.9 us -> 18.4 us
    all_to_all x6, blocking collectives: 98.2 us -> 118 us  [exchange(): return lax.all_to_all(blocks, axes, 0, 0, tiled=True)]
    all_to_all x2, waiting for transfers between devices: 11.4 us -> 16.3 us  [exchange(): return lax.all_to_all(blocks, axes, 0, 0, tiled=True)]
  transfers between devices with their start and end apart: 8 -> 8, of which waited for: 4 -> 4; matrix products, arithmetic and copies ran while one was open for 0% -> 0% of each run, Pallas kernels for 2% -> 4%
where the time goes in v8:
time: 179 us; the launch traced here: 178 us
  blocking collectives  118 us (66%)
  starting transfers between devices  21 us (12%)
  waiting for transfers between devices  18.4 us (10%)
  Pallas kernels  16.2 us (9%)
  local copies, waits for them, and re-layouts  3.16 us (2%)
    all_to_all x6, blocking collectives, exchange(): return lax.all_to_all(blocks, axes, 0, 0, tiled=True)  118 us
    all_to_all x2, waiting for transfers between devices, exchange(): return lax.all_to_all(blocks, axes, 0, 0, tiled=True)  16.3 us
    pallas_call x10, Pallas kernels, call(): pl.pallas_call(run, out_shape=outs, in_specs=[ANY if k in remote else VME...  16.2 us
    ppermute x5, starting transfers between devices, swap(): return lax.ppermute(block, 'core', [(0, 1), (1, 0)])  13.4 us
    all_to_all x2, starting transfers between devices, exchange(): return lax.all_to_all(blocks, axes, 0, 0, tiled=True)  7.54 us
  transfers between devices with their start and end apart: 8, of which 4 were waited for; matrix products, arithmetic and copies ran while one was open for 0% of the time, Pallas kernels for 4%

profile of v8, /device:TPU:1, one launch (start us, length us, event | category | flops | bytes accessed | tf_op | source)
XLA Modules:
  0.0 177.8 jit_solution(2305620122623759925)
XLA Ops:
  0.6 0.0 copy-start.1
  0.6 1.6 shard_map.86
  2.3 0.0 copy-start.9
  2.3 0.0 copy-start.4
  2.3 31.6 %all_to_all.40 = bf16[32,40,96]{2,1,0:T(8,128)(2,1)S(1)} all-to-all(bf16[32,40,96]{2,1,0:T(8,128)(2,1)} %get-tuple-element.22), channel_id=1, replica_groups=mesh['layer'=4,'x'=4,'zh'=8,'zl'=1,'yh'=2,'core'=2] {'zh','yh','core'}, dimensions={0} | all-to-all | bytes 491520 | tf_op jit(solution)/shard_map/all_to_all | solution.py:31
  33.9 2.7 %collective-permute-start.2 = (bf16[256,5120]{1,0:T(8,128)(2,1)}, bf16[256,5120]{1,0:T(8,128)(2,1)}, u32[]{:S(2)}, u32[]{:S(2)}) collective-permute-start(bf16[256,5120]{1,0:T(8,128)(2,1)} %bitcast.12), channel_id=1, source_target_pairs={{0,1},{1,0},{2,3},{3,2},{4,5},{5,4},{6,7},{7,6},{8,9},{9,8},{10,11... | collective-permute-start | bytes 7864328 | tf_op jit(solution)/shard_map/ppermute | solution.py:35
  36.6 1.1 shard_map.87
  37.7 4.0 %all-to-all-start.1 = ((bf16[4,96,1280]{2,1,0:T(8,128)(2,1)}), bf16[4,96,1280]{2,1,0:T(8,128)(2,1)S(1)}, u32[]{:S(2)}, u32[]{:S(2)}) async-start(bf16[4,96,1280]{2,1,0:T(8,128)(2,1)} %shard_map.87), calls=%async_computation.1 | async-start | bytes 1966080 | tf_op jit(solution)/shard_map/all_to_all | solution.py:31
  41.7 0.0 copy-done.1
  41.7 2.2 %collective-permute-start = (bf16[64,5120]{1,0:T(8,128)(2,1)S(1)}, bf16[64,5120]{1,0:T(8,128)(2,1)S(1)}, u32[]{:S(2)}, u32[]{:S(2)}) collective-permute-start(bf16[64,5120]{1,0:T(8,128)(2,1)S(1)} %bitcast.16), channel_id=1, source_target_pairs={{0,1},{1,0},{2,3},{3,2},{4,5},{5,4},{6,7},{7,6},{8,9},{9,8},{10,11... | collective-permute-start | bytes 1966088 | tf_op jit(solution)/shard_map/ppermute | solution.py:35
  43.9 0.0 copy-done.9
  43.9 2.1 %collective-permute-start.1 = (f32[48,128]{1,0:T(8,128)S(1)}, f32[48,128]{1,0:T(8,128)S(1)}, u32[]{:S(2)}, u32[]{:S(2)}) collective-permute-start(f32[48,128]{1,0:T(8,128)S(1)} %copy-done.9), channel_id=1, source_target_pairs={{0,1},{1,0},{2,3},{3,2},{4,5},{5,4},{6,7},{7,6},{8,9},{9,8},{10,11... | collective-permute-start | bytes 73736 | tf_op jit(solution)/shard_map/ppermute | solution.py:35
  46.1 1.0 collective-permute-done.1.refs_4_.refs_1_
  47.0 0.0 collective-permute-done.refs_2_
  47.0 0.0 copy-start.2
  47.0 0.8 copy-done.2
  47.9 8.1 %all-to-all-done.1.refs_0_ = bf16[4,96,1280]{2,1,0:T(8,128)(2,1)S(1)} async-done(((bf16[4,96,1280]{2,1,0:T(8,128)(2,1)}), bf16[4,96,1280]{2,1,0:T(8,128)(2,1)S(1)}, u32[]{:S(2)}, u32[]{:S(2)}) %all-to-all-start.1) | async-done | bytes 983072 | tf_op jit(solution)/shard_map/all_to_all | solution.py:31
  56.0 0.0 copy-done.4
  56.0 0.0 copy-start.3
  56.0 1.1 copy-done.3
  57.0 1.4 shard_map.88
  58.5 0.0 copy-start.5
  58.5 0.6 copy-done.5
  59.1 0.0 copy-start.8
  59.1 0.6 copy-done.8
  59.7 3.0 %collective-permute-start.4 = (bf16[96,5120]{1,0:T(8,128)(2,1)S(1)}, bf16[96,5120]{1,0:T(8,128)(2,1)S(1)}, u32[]{:S(2)}, u32[]{:S(2)}) collective-permute-start(bf16[96,5120]{1,0:T(8,128)(2,1)S(1)} %get-tuple-element.31.refs_3_), channel_id=1, source_target_pairs={{0,1},{1,0},{2,3},{3,2},{4,5},{5,4},{6,7},{7,6},{8,9},{9,8},{10,11... | collective-permute-start | bytes 2949128 | tf_op jit(solution)/shard_map/ppermute | solution.py:35
  62.7 9.9 %all_to_all.41.refs_0_ = bf16[4,96,128]{2,1,0:T(8,128)(2,1)} all-to-all(bf16[4,96,128]{2,1,0:T(8,128)(2,1)S(1)} %get-tuple-element.29), channel_id=1, replica_groups=mesh['layer'=4,'x'=4,'zh'=8,'zl'=1,'yh'=2,'core'=2] {'layer'}, dimensions={0} | all-to-all | bytes 196608 | tf_op jit(solution)/shard_map/all_to_all | solution.py:31
  72.6 0.0 collective-permute-done.2.refs_2_
  72.6 4.7 %shard_map.89 = bf16[4,96,1280]{2,1,0:T(8,128)(2,1)} custom-call(bf16[4,96,128]{2,1,0:T(8,128)(2,1)} %all_to_all.41.refs_0_, bf16[256,5120]{1,0:T(8,128)(2,1)} %bitcast.13, bf16[256,5120]{1,0:T(8,128)(2,1)} %collective-permute-done.2.refs_2_), custom_call_target="tpu_custom_call" | custom-call | flops 503316480 | bytes 6324224 | tf_op jit(solution)/shard_map/pallas_call | solution.py:49
  77.3 3.5 %all-to-all-start.3 = ((bf16[4,96,1280]{2,1,0:T(8,128)(2,1)}), bf16[4,96,1280]{2,1,0:T(8,128)(2,1)S(1)}, u32[]{:S(2)}, u32[]{:S(2)}) async-start(bf16[4,96,1280]{2,1,0:T(8,128)(2,1)} %shard_map.89), calls=%async_computation.3 | async-start | bytes 1966080 | tf_op jit(solution)/shard_map/all_to_all | solution.py:31
  80.9 0.2 shard_map.90
  81.0 0.0 collective-permute-start.3
  81.0 0.0 copy-start.7
  81.1 3.4 %collective-permute-start.5 = (f32[64,96]{1,0:T(8,128)}, f32[64,96]{1,0:T(8,128)S(1)}, u32[]{:S(2)}, u32[]{:S(2)}) collective-permute-start(f32[64,96]{1,0:T(8,128)} %copy-done.8), channel_id=1, source_target_pairs={{0,1},{1,0},{2,3},{3,2},{4,5},{5,4},{6,7},{7,6},{8,9},{9,8},{10,11... | collective-permute-start | bytes 73736 | tf_op jit(solution)/shard_map/ppermute | solution.py:35
  84.5 0.0 collective-permute-done.3.refs_1_
  84.5 1.0 collective-permute-done.5.refs_2_
  85.5 0.0 collective-permute-done.4.refs_4_
  85.5 8.3 %all-to-all-done.3.refs_0_ = bf16[4,96,1280]{2,1,0:T(8,128)(2,1)S(1)} async-done(((bf16[4,96,1280]{2,1,0:T(8,128)(2,1)}), bf16[4,96,1280]{2,1,0:T(8,128)(2,1)S(1)}, u32[]{:S(2)}, u32[]{:S(2)}) %all-to-all-start.3) | async-done | bytes 983072 | tf_op jit(solution)/shard_map/all_to_all | solution.py:31
  93.8 1.8 shard_map.91
  95.5 19.8 %all_to_all.42.refs_0_ = f32[8,12,1280]{2,1,0:T(8,128)S(1)} all-to-all(f32[8,12,1280]{2,1,0:T(8,128)S(1)} %shard_map.91), channel_id=1, replica_groups=mesh['layer'=4,'x'=4,'zh'=8,'zl'=1,'yh'=2,'core'=2] {'zh'}, dimensions={0} | all-to-all | bytes 983040 | tf_op jit(solution)/shard_map/all_to_all | solution.py:31
  115.4 0.1 shard_map.92
  115.4 0.0 copy-start
  115.4 20.5 %all_to_all.43.refs_1_ = bf16[16,12,1280]{2,1,0:T(8,128)(2,1)S(1)} all-to-all(bf16[16,12,1280]{2,1,0:T(8,128)(2,1)S(1)} %shard_map.92), channel_id=1, replica_groups=mesh['layer'=4,'x'=4,'zh'=8,'zl'=1,'yh'=2,'core'=2] {'zh','yh'}, dimensions={0} | all-to-all | bytes 983040 | tf_op jit(solution)/shard_map/all_to_all | solution.py:31
  135.9 0.0 copy-done.7
  135.9 0.3 shard_map.93
  136.2 11.8 %all_to_all.44.refs_0_ = bf16[4,96,1280]{2,1,0:T(8,128)(2,1)S(1)} all-to-all(bf16[4,96,1280]{2,1,0:T(8,128)(2,1)S(1)} %shard_map.93), channel_id=1, replica_groups=mesh['layer'=4,'x'=4,'zh'=8,'zl'=1,'yh'=2,'core'=2] {'x','zl'}, dimensions={0} | all-to-all | bytes 1966080 | tf_op jit(solution)/shard_map/all_to_all | solution.py:31
  148.0 0.0 copy-done
  148.0 0.0 copy-start.6
  148.0 3.2 %shard_map.94 = bf16[8,64,96]{2,1,0:T(8,128)(2,1)S(1)} custom-call(bf16[4,96,1280]{2,1,0:T(8,128)(2,1)S(1)} %all_to_all.44.refs_0_, bf16[256,5120]{1,0:T(8,128)(2,1)S(1)} %bitcast.14, bf16[256,5120]{1,0:T(8,128)(2,1)} %collective-permute-done.2.refs_2_), custom_call_target="tpu_custom_call" | custom-call | flops 503316480 | bytes 6324224 | tf_op jit(solution)/shard_map/pallas_call | solution.py:49
  151.2 24.7 %all_to_all.45.refs_0_ = bf16[8,64,96]{2,1,0:T(8,128)(2,1)S(1)} all-to-all(bf16[8,64,96]{2,1,0:T(8,128)(2,1)S(1)} %shard_map.94), channel_id=1, replica_groups=mesh['layer'=4,'x'=4,'zh'=8,'zl'=1,'yh'=2,'core'=2] {'layer','core'}, dimensions={0} | all-to-all | bytes 196608 | tf_op jit(solution)/shard_map/all_to_all | solution.py:31
  176.0 0.0 copy-done.6
  176.0 1.8 %shard_map.95 = (f32[64,5120]{1,0:T(8,128)}, f32[1,64]{1,0:T(1,128)}) custom-call(bf16[8,64,96]{2,1,0:T(8,128)(2,1)S(1)} %all_to_all.45.refs_0_, f32[64,96]{1,0:T(8,128)S(1)} %copy-done.6, f32[64,96]{1,0:T(8,128)S(1)} %collective-permute-done.5.refs_2_, bf16[96,5120]{1,0:T(8,128)(2,1)S(1)} %get-tuple-element.31.refs_3_, ...), custom_call_target="tpu_custom_call" | custom-call | flops 125829120 | bytes 3424512 | tf_op jit(solution)/shard_map/pallas_call | solution.py:49
Async XLA Ops:
  0.6 41.1 %copy-start.1 = (bf16[1,64,5120]{2,1,0:T(8,128)(2,1)S(1)}, bf16[1,64,5120]{2,1,0:T(8,128)(2,1)}, u32[]{:S(2)}) copy-start(bf16[1,64,5120]{2,1,0:T(8,128)(2,1)} %param.9) | copy-start | bytes 1966084
  2.3 41.6 %copy-start.9 = (f32[48,128]{1,0:T(8,128)S(1)}, f32[48,128]{1,0:T(8,128)}, u32[]{:S(2)}) copy-start(f32[48,128]{1,0:T(8,128)} %get-tuple-element.28) | copy-start | bytes 73732
  2.3 53.7 %copy-start.4 = (f32[48,128]{1,0:T(8,128)S(1)}, f32[48,128]{1,0:T(8,128)}, u32[]{:S(2)}) copy-start(f32[48,128]{1,0:T(8,128)} %get-tuple-element.27.refs_3_.refs_0_) | copy-start | bytes 73732
  33.9 38.7 %collective-permute-start.2 = (bf16[256,5120]{1,0:T(8,128)(2,1)}, bf16[256,5120]{1,0:T(8,128)(2,1)}, u32[]{:S(2)}, u32[]{:S(2)}) collective-permute-start(bf16[256,5120]{1,0:T(8,128)(2,1)} %bitcast.12), channel_id=1, source_target_pairs={{0,1},{1,0},{2,3},{3,2},{4,5},{5,4},{6,7},{7,6},{8,9},{9,8},{10,11... | collective-permute-start | bytes 7864328 | tf_op jit(solution)/shard_map/ppermute | solution.py:35
  37.7 18.2 %all-to-all-start.1 = ((bf16[4,96,1280]{2,1,0:T(8,128)(2,1)}), bf16[4,96,1280]{2,1,0:T(8,128)(2,1)S(1)}, u32[]{:S(2)}, u32[]{:S(2)}) async-start(bf16[4,96,1280]{2,1,0:T(8,128)(2,1)} %shard_map.87), calls=%async_computation.1 | async-start | bytes 1966080 | tf_op jit(solution)/shard_map/all_to_all | solution.py:31
  41.7 5.3 %collective-permute-start = (bf16[64,5120]{1,0:T(8,128)(2,1)S(1)}, bf16[64,5120]{1,0:T(8,128)(2,1)S(1)}, u32[]{:S(2)}, u32[]{:S(2)}) collective-permute-start(bf16[64,5120]{1,0:T(8,128)(2,1)S(1)} %bitcast.16), channel_id=1, source_target_pairs={{0,1},{1,0},{2,3},{3,2},{4,5},{5,4},{6,7},{7,6},{8,9},{9,8},{10,11... | collective-permute-start | bytes 1966088 | tf_op jit(solution)/shard_map/ppermute | solution.py:35
  43.9 3.1 %collective-permute-start.1 = (f32[48,128]{1,0:T(8,128)S(1)}, f32[48,128]{1,0:T(8,128)S(1)}, u32[]{:S(2)}, u32[]{:S(2)}) collective-permute-start(f32[48,128]{1,0:T(8,128)S(1)} %copy-done.9), channel_id=1, source_target_pairs={{0,1},{1,0},{2,3},{3,2},{4,5},{5,4},{6,7},{7,6},{8,9},{9,8},{10,11... | collective-permute-start | bytes 73736 | tf_op jit(solution)/shard_map/ppermute | solution.py:35
  47.0 0.8 copy-start.2
  56.0 1.1 copy-start.3
  58.5 0.6 copy-start.5
  59.1 0.6 copy-start.8
  59.7 25.8 %collective-permute-start.4 = (bf16[96,5120]{1,0:T(8,128)(2,1)S(1)}, bf16[96,5120]{1,0:T(8,128)(2,1)S(1)}, u32[]{:S(2)}, u32[]{:S(2)}) collective-permute-start(bf16[96,5120]{1,0:T(8,128)(2,1)S(1)} %get-tuple-element.31.refs_3_), channel_id=1, source_target_pairs={{0,1},{1,0},{2,3},{3,2},{4,5},{5,4},{6,7},{7,6},{8,9},{9,8},{10,11... | collective-permute-start | bytes 2949128 | tf_op jit(solution)/shard_map/ppermute | solution.py:35
  77.3 16.4 %all-to-all-start.3 = ((bf16[4,96,1280]{2,1,0:T(8,128)(2,1)}), bf16[4,96,1280]{2,1,0:T(8,128)(2,1)S(1)}, u32[]{:S(2)}, u32[]{:S(2)}) async-start(bf16[4,96,1280]{2,1,0:T(8,128)(2,1)} %shard_map.89), calls=%async_computation.3 | async-start | bytes 1966080 | tf_op jit(solution)/shard_map/all_to_all | solution.py:31
  81.0 3.4 %collective-permute-start.3 = (f32[80,96]{1,0:T(8,128)S(1)}, f32[80,96]{1,0:T(8,128)S(1)}, u32[]{:S(2)}, u32[]{:S(2)}) collective-permute-start(f32[80,96]{1,0:T(8,128)S(1)} %shard_map.90), channel_id=1, source_target_pairs={{0,0},{4,4},{8,8},{12,12},{16,16},{20,20},{24,24},{28,28},{1,1},{5... | collective-permute-start | bytes 92168 | tf_op jit(solution)/shard_map/ppermute | solution.py:41
  81.0 54.9 %copy-start.7 = (s32[192]{0:T(256)S(1)}, s32[192]{0:T(256)}, u32[]{:S(2)}) copy-start(s32[192]{0:T(256)} %param.13) | copy-start | bytes 2308
  81.1 4.5 %collective-permute-start.5 = (f32[64,96]{1,0:T(8,128)}, f32[64,96]{1,0:T(8,128)S(1)}, u32[]{:S(2)}, u32[]{:S(2)}) collective-permute-start(f32[64,96]{1,0:T(8,128)} %copy-done.8), channel_id=1, source_target_pairs={{0,1},{1,0},{2,3},{3,2},{4,5},{5,4},{6,7},{7,6},{8,9},{9,8},{10,11... | collective-permute-start | bytes 73736 | tf_op jit(solution)/shard_map/ppermute | solution.py:35
  115.4 32.6 %copy-start = (bf16[1,4,64,5120]{3,2,1,0:T(8,128)(2,1)S(1)}, bf16[1,4,64,5120]{3,2,1,0:T(8,128)(2,1)}, u32[]{:S(2)}) copy-start(bf16[1,4,64,5120]{3,2,1,0:T(8,128)(2,1)} %param.11) | copy-start | bytes 7864324
  148.0 28.0 %copy-start.6 = (f32[64,96]{1,0:T(8,128)S(1)}, f32[64,96]{1,0:T(8,128)}, u32[]{:S(2)}) copy-start(f32[64,96]{1,0:T(8,128)} %copy-done.5) | copy-start | bytes 73732

commit v9 on v6

--- a/solution.py
+++ b/solution.py
@@ -168,16 +168,14 @@
         copy.wait()
 
 
-def reduce_kernel(parts_hbm, offset_ref, out_ref, parts, sems):
+def reduce_kernel(parts_ref, offset_ref, out_ref):
     place = lax.axis_index(FAR)
-    copies = [start(parts_hbm.at[k], parts.at[k], sems.at[k]) for k in range(parts.shape[0])]
     size = offset_ref.shape[0]
-    tile = jnp.concatenate([offset_ref[...].T] * (parts.shape[2] // size), axis=1)
+    tile = jnp.concatenate([offset_ref[...].T] * (parts_ref.shape[2] // size), axis=1)
     lane = lax.broadcasted_iota(jnp.int32, tile.shape, 1)
     total = jnp.where((lane >= place * size) & (lane < (place + 1) * size), -tile, jnp.zeros_like(tile))
-    for k, copy in enumerate(copies):
-        copy.wait()
-        total += parts[k].astype(F32)
+    for k in range(parts_ref.shape[0]):
+        total += parts_ref[k].astype(F32)
     rows = out_ref.shape[1]
     for k in range(out_ref.shape[0]):
         out_ref[k] = total[k * rows : (k + 1) * rows]
@@ -262,12 +260,13 @@
     sends, own_decoders = lax.optimization_barrier((sends, decoders[0]))
     other_decoders = [swap(own_decoders[layer]) for layer in range(layers)]
     own_decoders = own_decoders.reshape(layers * latents, model)
+    sends, sent_decoders = lax.optimization_barrier((sends, own_decoders))
+    other_decoders = swap(sent_decoders)
     block = exchange(sends, FAR + ("core",)).reshape(-1, half)
-    held = (block, own_encoder, own_decoders, sent_sides)
-    block, sent_encoder, sent_decoders, sent_sides = lax.optimization_barrier(held)
+    held = (block, own_encoder, sent_sides)
+    block, sent_encoder, sent_sides = lax.optimization_barrier(held)
     other_sides = swap(sent_sides)
     other_encoder = swap(sent_encoder)
-    other_decoders = swap(sent_decoders)
     (sends,) = call(flip_kernel, [struct((near, half, wide), BF16)], [block])
     blocks = exchange(sends, NEAR)
     whole, codes, own_slope, sent_slope = call(
@@ -316,8 +315,6 @@
         reduce_kernel,
         [struct((zh, half // zh, wide), F32)],
         [parts, offset],
-        scratch=[pltpu.VMEM((near, half, wide), BF16), pltpu.SemaphoreType.DMA((near,))],
-        remote=[0],
     )
     parts = exchange(parts, ("zh",))
     (parts,) = call(sum_kernel, [struct((far, half // zh, wide), BF16)], [parts])

time: 154 us -> 155 us (level)
  starting transfers between devices: 22.2 us -> 28.8 us
  blocking collectives: 98.2 us -> 93.2 us
    ppermute x5, starting transfers between devices: 13 us -> 19.8 us  [swap(): return lax.ppermute(block, 'core', [(0, 1), (1, 0)])]
    all_to_all x6, blocking collectives: 98.2 us -> 93.2 us  [exchange(): return lax.all_to_all(blocks, axes, 0, 0, tiled=True)]
where the time goes in v9:
time: 155 us; the launch traced here: 154 us
  blocking collectives  93.2 us (60%)
  starting transfers between devices  28.8 us (19%)
  Pallas kernels  15 us (10%)
  waiting for transfers between devices  14.3 us (9%)
  local copies, waits for them, and re-layouts  1.96 us (1%)
    all_to_all x6, blocking collectives, exchange(): return lax.all_to_all(blocks, axes, 0, 0, tiled=True)  93.2 us
    ppermute x5, starting transfers between devices, swap(): return lax.ppermute(block, 'core', [(0, 1), (1, 0)])  19.8 us
    pallas_call x10, Pallas kernels, call(): pl.pallas_call(run, out_shape=outs, in_specs=[ANY if k in remote else VME...  15 us
    all_to_all x2, waiting for transfers between devices, exchange(): return lax.all_to_all(blocks, axes, 0, 0, tiled=True)  11.8 us
    all_to_all x2, starting transfers between devices, exchange(): return lax.all_to_all(blocks, axes, 0, 0, tiled=True)  8.31 us
  transfers between devices with their start and end apart: 8, of which 4 were waited for; matrix products, arithmetic and copies ran while one was open for 0% of the time, Pallas kernels for 2%

profile of v9, /device:TPU:1, one launch (start us, length us, event | category | flops | bytes accessed | tf_op | source)
XLA Modules:
  0.0 154.1 jit_solution(383130738133922422)
XLA Ops:
  0.6 0.0 copy-start.1
  0.6 1.6 %shard_map.86 = (bf16[16,40,96]{2,1,0:T(8,128)(2,1)}, f32[48,128]{1,0:T(8,128)}, f32[48,128]{1,0:T(8,128)}) custom-call(bf16[40,192]{1,0:T(8,128)(2,1)} %bitcast.19, bf16[40,192]{1,0:T(8,128)(2,1)} %bitcast.20, bf16[1,40]{1,0:T(2,128)(2,1)} %refs_2_.1, f32[1,64]{1,0:T(1,128)} %refs_3_.1), custom_call_target="tpu_custom_call" | custom-call | bytes 203088 | tf_op jit(solution)/shard_map/pallas_call | solution.py:49
  2.2 0.0 copy-start.9
  2.2 0.0 copy-start.4
  2.2 8.9 %collective-permute-start.2 = (bf16[256,5120]{1,0:T(8,128)(2,1)}, bf16[256,5120]{1,0:T(8,128)(2,1)}, u32[]{:S(2)}, u32[]{:S(2)}) collective-permute-start(bf16[256,5120]{1,0:T(8,128)(2,1)} %bitcast.12), channel_id=1, source_target_pairs={{0,1},{1,0},{2,3},{3,2},{4,5},{5,4},{6,7},{7,6},{8,9},{9,8},{10,11... | collective-permute-start | bytes 7864328 | tf_op jit(solution)/shard_map/ppermute | solution.py:35
  11.1 23.3 %all_to_all.40 = bf16[16,40,96]{2,1,0:T(8,128)(2,1)S(1)} all-to-all(bf16[16,40,96]{2,1,0:T(8,128)(2,1)} %get-tuple-element.25), channel_id=1, replica_groups=mesh['layer'=4,'x'=4,'zh'=4,'zl'=2,'yh'=2,'core'=2] {'zh','yh','core'}, dimensions={0} | all-to-all | bytes 245760 | tf_op jit(solution)/shard_map/all_to_all | solution.py:31
  34.5 1.1 shard_map.87
  35.5 4.7 %all-to-all-start.1 = ((bf16[8,96,640]{2,1,0:T(8,128)(2,1)}), bf16[8,96,640]{2,1,0:T(8,128)(2,1)S(1)}, u32[]{:S(2)}, u32[]{:S(2)}) async-start(bf16[8,96,640]{2,1,0:T(8,128)(2,1)} %shard_map.87), calls=%async_computation.1 | async-start | bytes 1966080 | tf_op jit(solution)/shard_map/all_to_all | solution.py:31
  40.3 0.0 copy-done.1
  40.3 2.4 %collective-permute-start = (bf16[64,5120]{1,0:T(8,128)(2,1)S(1)}, bf16[64,5120]{1,0:T(8,128)(2,1)S(1)}, u32[]{:S(2)}, u32[]{:S(2)}) collective-permute-start(bf16[64,5120]{1,0:T(8,128)(2,1)S(1)} %bitcast.16), channel_id=1, source_target_pairs={{0,1},{1,0},{2,3},{3,2},{4,5},{5,4},{6,7},{7,6},{8,9},{9,8},{10,11... | collective-permute-start | bytes 1966088 | tf_op jit(solution)/shard_map/ppermute | solution.py:35
  42.7 0.0 copy-done.9
  42.7 1.9 %collective-permute-start.1 = (f32[48,128]{1,0:T(8,128)S(1)}, f32[48,128]{1,0:T(8,128)S(1)}, u32[]{:S(2)}, u32[]{:S(2)}) collective-permute-start(f32[48,128]{1,0:T(8,128)S(1)} %copy-done.9), channel_id=1, source_target_pairs={{0,1},{1,0},{2,3},{3,2},{4,5},{5,4},{6,7},{7,6},{8,9},{9,8},{10,11... | collective-permute-start | bytes 73736 | tf_op jit(solution)/shard_map/ppermute | solution.py:35
  44.6 1.2 collective-permute-done.1.refs_4_.refs_1_
  45.8 0.0 collective-permute-done.refs_2_
  45.8 0.0 copy-start.2
  45.8 0.8 copy-done.2
  46.6 8.3 %all-to-all-done.1.refs_0_ = bf16[8,96,640]{2,1,0:T(8,128)(2,1)S(1)} async-done(((bf16[8,96,640]{2,1,0:T(8,128)(2,1)}), bf16[8,96,640]{2,1,0:T(8,128)(2,1)S(1)}, u32[]{:S(2)}, u32[]{:S(2)}) %all-to-all-start.1) | async-done | bytes 983072 | tf_op jit(solution)/shard_map/all_to_all | solution.py:31
  54.9 0.0 copy-done.4
  54.9 0.0 copy-start.3
  54.9 1.1 copy-done.3
  56.0 1.7 %shard_map.88 = (bf16[96,5120]{1,0:T(8,128)(2,1)S(1)}, bf16[4,96,128]{2,1,0:T(8,128)(2,1)S(1)}, f32[64,96]{1,0:T(8,128)S(1)}, f32[64,96]{1,0:T(8,128)S(1)}) custom-call(bf16[8,96,640]{2,1,0:T(8,128)(2,1)S(1)} %all-to-all-done.1.refs_0_, bf16[64,5120]{1,0:T(8,128)(2,1)S(1)} %bitcast.17, bf16[64,5120]{1,0:T(8,128)(2,1)S(1)} %copy-done.3, ...), custom_call_target="tpu_custom_call" | custom-call | flops 125829120 | bytes 3473408 | tf_op jit(solution)/shard_map/pallas_call | solution.py:49
  57.7 0.0 copy-start.5
  57.7 0.0 copy-start.8
  57.8 7.9 %all_to_all.41.refs_0_ = bf16[4,96,128]{2,1,0:T(8,128)(2,1)} all-to-all(bf16[4,96,128]{2,1,0:T(8,128)(2,1)S(1)} %get-tuple-element.31), channel_id=1, replica_groups=mesh['layer'=4,'x'=4,'zh'=4,'zl'=2,'yh'=2,'core'=2] {'layer'}, dimensions={0} | all-to-all | bytes 196608 | tf_op jit(solution)/shard_map/all_to_all | solution.py:31
  65.6 0.0 collective-permute-done.2.refs_2_
  65.6 4.8 %shard_map.89 = bf16[8,96,640]{2,1,0:T(8,128)(2,1)} custom-call(bf16[4,96,128]{2,1,0:T(8,128)(2,1)} %all_to_all.41.refs_0_, bf16[256,5120]{1,0:T(8,128)(2,1)} %bitcast.13, bf16[256,5120]{1,0:T(8,128)(2,1)} %collective-permute-done.2.refs_2_), custom_call_target="tpu_custom_call" | custom-call | flops 503316480 | bytes 6324224 | tf_op jit(solution)/shard_map/pallas_call | solution.py:49
  70.5 0.0 copy-done.5
  70.5 0.0 copy-done.8
  70.5 0.0 copy-start.7
  70.5 3.6 %all-to-all-start.3 = ((bf16[8,96,640]{2,1,0:T(8,128)(2,1)}), bf16[8,96,640]{2,1,0:T(8,128)(2,1)S(1)}, u32[]{:S(2)}, u32[]{:S(2)}) async-start(bf16[8,96,640]{2,1,0:T(8,128)(2,1)} %shard_map.89), calls=%async_computation.3 | async-start | bytes 1966080 | tf_op jit(solution)/shard_map/all_to_all | solution.py:31
  74.1 4.7 %collective-permute-start.4 = (bf16[96,5120]{1,0:T(8,128)(2,1)S(1)}, bf16[96,5120]{1,0:T(8,128)(2,1)S(1)}, u32[]{:S(2)}, u32[]{:S(2)}) collective-permute-start(bf16[96,5120]{1,0:T(8,128)(2,1)S(1)} %get-tuple-element.33.refs_3_), channel_id=1, source_target_pairs={{0,1},{1,0},{2,3},{3,2},{4,5},{5,4},{6,7},{7,6},{8,9},{9,8},{10,11... | collective-permute-start | bytes 2949128 | tf_op jit(solution)/shard_map/ppermute | solution.py:35
  78.8 0.2 shard_map.90
  78.9 0.7 collective-permute-start.3
  79.6 1.9 %collective-permute-start.5 = (f32[64,96]{1,0:T(8,128)}, f32[64,96]{1,0:T(8,128)S(1)}, u32[]{:S(2)}, u32[]{:S(2)}) collective-permute-start(f32[64,96]{1,0:T(8,128)} %copy-done.8), channel_id=1, source_target_pairs={{0,1},{1,0},{2,3},{3,2},{4,5},{5,4},{6,7},{7,6},{8,9},{9,8},{10,11... | collective-permute-start | bytes 73736 | tf_op jit(solution)/shard_map/ppermute | solution.py:35
  81.5 0.0 collective-permute-done.3.refs_1_
  81.5 1.4 collective-permute-done.5.refs_2_
  82.9 0.0 collective-permute-done.4.refs_4_
  82.9 3.4 %all-to-all-done.3.refs_0_ = bf16[8,96,640]{2,1,0:T(8,128)(2,1)S(1)} async-done(((bf16[8,96,640]{2,1,0:T(8,128)(2,1)}), bf16[8,96,640]{2,1,0:T(8,128)(2,1)S(1)}, u32[]{:S(2)}, u32[]{:S(2)}) %all-to-all-start.3) | async-done | bytes 983072 | tf_op jit(solution)/shard_map/all_to_all | solution.py:31
  86.4 0.3 shard_map.91
  86.7 0.0 copy-start
  86.7 13.4 %all_to_all.42.refs_0_ = f32[4,24,640]{2,1,0:T(8,128)S(1)} all-to-all(f32[4,24,640]{2,1,0:T(8,128)S(1)} %shard_map.91), channel_id=1, replica_groups=mesh['layer'=4,'x'=4,'zh'=4,'zl'=2,'yh'=2,'core'=2] {'zh'}, dimensions={0} | all-to-all | bytes 491520 | tf_op jit(solution)/shard_map/all_to_all | solution.py:31
  100.2 16.0 %all_to_all.43.refs_1_ = bf16[8,24,640]{2,1,0:T(8,128)(2,1)S(1)} all-to-all(bf16[8,24,640]{2,1,0:T(8,128)(2,1)S(1)} %shard_map.92), channel_id=1, replica_groups=mesh['layer'=4,'x'=4,'zh'=4,'zl'=2,'yh'=2,'core'=2] {'zh','yh'}, dimensions={0} | all-to-all | bytes 491520 | tf_op jit(solution)/shard_map/all_to_all | solution.py:31
  116.2 0.0 copy-done.7
  116.2 0.3 shard_map.93
  116.5 18.2 %all_to_all.44.refs_0_ = bf16[8,96,640]{2,1,0:T(8,128)(2,1)S(1)} all-to-all(bf16[8,96,640]{2,1,0:T(8,128)(2,1)S(1)} %shard_map.93), channel_id=1, replica_groups=mesh['layer'=4,'x'=4,'zh'=4,'zl'=2,'yh'=2,'core'=2] {'x','zl'}, dimensions={0} | all-to-all | bytes 1966080 | tf_op jit(solution)/shard_map/all_to_all | solution.py:31
  134.6 0.0 copy-done
  134.6 0.0 copy-start.6
  134.6 3.3 %shard_map.94 = bf16[8,64,96]{2,1,0:T(8,128)(2,1)S(1)} custom-call(bf16[8,96,640]{2,1,0:T(8,128)(2,1)S(1)} %all_to_all.44.refs_0_, bf16[256,5120]{1,0:T(8,128)(2,1)S(1)} %bitcast.14, bf16[256,5120]{1,0:T(8,128)(2,1)} %collective-permute-done.2.refs_2_), custom_call_target="tpu_custom_call" | custom-call | flops 503316480 | bytes 6324224 | tf_op jit(solution)/shard_map/pallas_call | solution.py:49
  137.9 14.4 %all_to_all.45.refs_0_ = bf16[8,64,96]{2,1,0:T(8,128)(2,1)S(1)} all-to-all(bf16[8,64,96]{2,1,0:T(8,128)(2,1)S(1)} %shard_map.94), channel_id=1, replica_groups=mesh['layer'=4,'x'=4,'zh'=4,'zl'=2,'yh'=2,'core'=2] {'layer','core'}, dimensions={0} | all-to-all | bytes 196608 | tf_op jit(solution)/shard_map/all_to_all | solution.py:31
  152.3 0.0 copy-done.6
  152.3 1.8 %shard_map.95 = (f32[64,5120]{1,0:T(8,128)}, f32[1,64]{1,0:T(1,128)}) custom-call(bf16[8,64,96]{2,1,0:T(8,128)(2,1)S(1)} %all_to_all.45.refs_0_, f32[64,96]{1,0:T(8,128)S(1)} %copy-done.6, f32[64,96]{1,0:T(8,128)S(1)} %collective-permute-done.5.refs_2_, bf16[96,5120]{1,0:T(8,128)(2,1)S(1)} %get-tuple-element.33.refs_3_, ...), custom_call_target="tpu_custom_call" | custom-call | flops 125829120 | bytes 3424512 | tf_op jit(solution)/shard_map/pallas_call | solution.py:49
  (1 shorter events, 0.0 us)
Async XLA Ops:
  0.6 39.7 %copy-start.1 = (bf16[1,64,5120]{2,1,0:T(8,128)(2,1)S(1)}, bf16[1,64,5120]{2,1,0:T(8,128)(2,1)}, u32[]{:S(2)}) copy-start(bf16[1,64,5120]{2,1,0:T(8,128)(2,1)} %param.9) | copy-start | bytes 1966084
  2.2 40.5 %copy-start.9 = (f32[48,128]{1,0:T(8,128)S(1)}, f32[48,128]{1,0:T(8,128)}, u32[]{:S(2)}) copy-start(f32[48,128]{1,0:T(8,128)} %get-tuple-element.30) | copy-start | bytes 73732
  2.2 52.7 %copy-start.4 = (f32[48,128]{1,0:T(8,128)S(1)}, f32[48,128]{1,0:T(8,128)}, u32[]{:S(2)}) copy-start(f32[48,128]{1,0:T(8,128)} %get-tuple-element.29.refs_3_.refs_0_) | copy-start | bytes 73732
  2.2 63.4 %collective-permute-start.2 = (bf16[256,5120]{1,0:T(8,128)(2,1)}, bf16[256,5120]{1,0:T(8,128)(2,1)}, u32[]{:S(2)}, u32[]{:S(2)}) collective-permute-start(bf16[256,5120]{1,0:T(8,128)(2,1)} %bitcast.12), channel_id=1, source_target_pairs={{0,1},{1,0},{2,3},{3,2},{4,5},{5,4},{6,7},{7,6},{8,9},{9,8},{10,11... | collective-permute-start | bytes 7864328 | tf_op jit(solution)/shard_map/ppermute | solution.py:35
  35.5 19.4 %all-to-all-start.1 = ((bf16[8,96,640]{2,1,0:T(8,128)(2,1)}), bf16[8,96,640]{2,1,0:T(8,128)(2,1)S(1)}, u32[]{:S(2)}, u32[]{:S(2)}) async-start(bf16[8,96,640]{2,1,0:T(8,128)(2,1)} %shard_map.87), calls=%async_computation.1 | async-start | bytes 1966080 | tf_op jit(solution)/shard_map/all_to_all | solution.py:31
  40.3 5.5 %collective-permute-start = (bf16[64,5120]{1,0:T(8,128)(2,1)S(1)}, bf16[64,5120]{1,0:T(8,128)(2,1)S(1)}, u32[]{:S(2)}, u32[]{:S(2)}) collective-permute-start(bf16[64,5120]{1,0:T(8,128)(2,1)S(1)} %bitcast.16), channel_id=1, source_target_pairs={{0,1},{1,0},{2,3},{3,2},{4,5},{5,4},{6,7},{7,6},{8,9},{9,8},{10,11... | collective-permute-start | bytes 1966088 | tf_op jit(solution)/shard_map/ppermute | solution.py:35
  42.7 3.1 %collective-permute-start.1 = (f32[48,128]{1,0:T(8,128)S(1)}, f32[48,128]{1,0:T(8,128)S(1)}, u32[]{:S(2)}, u32[]{:S(2)}) collective-permute-start(f32[48,128]{1,0:T(8,128)S(1)} %copy-done.9), channel_id=1, source_target_pairs={{0,1},{1,0},{2,3},{3,2},{4,5},{5,4},{6,7},{7,6},{8,9},{9,8},{10,11... | collective-permute-start | bytes 73736 | tf_op jit(solution)/shard_map/ppermute | solution.py:35
  45.8 0.8 copy-start.2
  54.9 1.1 copy-start.3
  57.7 12.7 %copy-start.5 = (f32[64,96]{1,0:T(8,128)}, f32[64,96]{1,0:T(8,128)S(1)}, u32[]{:S(2)}) copy-start(f32[64,96]{1,0:T(8,128)S(1)} %get-tuple-element.37.refs_1_) | copy-start | bytes 73732
  57.7 12.7 %copy-start.8 = (f32[64,96]{1,0:T(8,128)}, f32[64,96]{1,0:T(8,128)S(1)}, u32[]{:S(2)}) copy-start(f32[64,96]{1,0:T(8,128)S(1)} %get-tuple-element.34) | copy-start | bytes 73732
  70.5 45.7 %copy-start.7 = (s32[192]{0:T(256)S(1)}, s32[192]{0:T(256)}, u32[]{:S(2)}) copy-start(s32[192]{0:T(256)} %param.13) | copy-start | bytes 2308
  70.5 15.9 %all-to-all-start.3 = ((bf16[8,96,640]{2,1,0:T(8,128)(2,1)}), bf16[8,96,640]{2,1,0:T(8,128)(2,1)S(1)}, u32[]{:S(2)}, u32[]{:S(2)}) async-start(bf16[8,96,640]{2,1,0:T(8,128)(2,1)} %shard_map.89), calls=%async_computation.3 | async-start | bytes 1966080 | tf_op jit(solution)/shard_map/all_to_all | solution.py:31
  74.1 8.8 %collective-permute-start.4 = (bf16[96,5120]{1,0:T(8,128)(2,1)S(1)}, bf16[96,5120]{1,0:T(8,128)(2,1)S(1)}, u32[]{:S(2)}, u32[]{:S(2)}) collective-permute-start(bf16[96,5120]{1,0:T(8,128)(2,1)S(1)} %get-tuple-element.33.refs_3_), channel_id=1, source_target_pairs={{0,1},{1,0},{2,3},{3,2},{4,5},{5,4},{6,7},{7,6},{8,9},{9,8},{10,11... | collective-permute-start | bytes 2949128 | tf_op jit(solution)/shard_map/ppermute | solution.py:35
  78.9 2.6 %collective-permute-start.3 = (f32[80,96]{1,0:T(8,128)S(1)}, f32[80,96]{1,0:T(8,128)S(1)}, u32[]{:S(2)}, u32[]{:S(2)}) collective-permute-start(f32[80,96]{1,0:T(8,128)S(1)} %shard_map.90), channel_id=1, source_target_pairs={{0,0},{4,8},{8,16},{12,24},{16,4},{20,12},{24,20},{28,28},{1,1},{5... | collective-permute-start | bytes 92168 | tf_op jit(solution)/shard_map/ppermute | solution.py:41
  79.6 3.3 %collective-permute-start.5 = (f32[64,96]{1,0:T(8,128)}, f32[64,96]{1,0:T(8,128)S(1)}, u32[]{:S(2)}, u32[]{:S(2)}) collective-permute-start(f32[64,96]{1,0:T(8,128)} %copy-done.8), channel_id=1, source_target_pairs={{0,1},{1,0},{2,3},{3,2},{4,5},{5,4},{6,7},{7,6},{8,9},{9,8},{10,11... | collective-permute-start | bytes 73736 | tf_op jit(solution)/shard_map/ppermute | solution.py:35
  86.7 48.0 %copy-start = (bf16[1,4,64,5120]{3,2,1,0:T(8,128)(2,1)S(1)}, bf16[1,4,64,5120]{3,2,1,0:T(8,128)(2,1)}, u32[]{:S(2)}) copy-start(bf16[1,4,64,5120]{3,2,1,0:T(8,128)(2,1)} %param.11) | copy-start | bytes 7864324
  134.6 17.6 %copy-start.6 = (f32[64,96]{1,0:T(8,128)S(1)}, f32[64,96]{1,0:T(8,128)}, u32[]{:S(2)}) copy-start(f32[64,96]{1,0:T(8,128)} %copy-done.5) | copy-start | bytes 73732

commit v10 on v9

--- a/solution.py
+++ b/solution.py
@@ -178,13 +178,13 @@
         total += parts_ref[k].astype(F32)
     rows = out_ref.shape[1]
     for k in range(out_ref.shape[0]):
-        out_ref[k] = total[k * rows : (k + 1) * rows]
+        out_ref[k] = total[k * rows : (k + 1) * rows].astype(out_ref.dtype)
 
 
 def sum_kernel(parts_ref, out_ref):
-    total = parts_ref[0]
+    total = parts_ref[0].astype(F32)
     for k in range(1, parts_ref.shape[0]):
-        total += parts_ref[k]
+        total += parts_ref[k].astype(F32)
     total = total.astype(BF16)
     for k in range(out_ref.shape[0]):
         out_ref[k] = total
@@ -260,13 +260,12 @@
     sends, own_decoders = lax.optimization_barrier((sends, decoders[0]))
     other_decoders = [swap(own_decoders[layer]) for layer in range(layers)]
     own_decoders = own_decoders.reshape(layers * latents, model)
-    sends, sent_decoders = lax.optimization_barrier((sends, own_decoders))
-    other_decoders = swap(sent_decoders)
     block = exchange(sends, FAR + ("core",)).reshape(-1, half)
-    held = (block, own_encoder, sent_sides)
-    block, sent_encoder, sent_sides = lax.optimization_barrier(held)
+    held = (block, own_encoder, own_decoders, sent_sides)
+    block, sent_encoder, sent_decoders, sent_sides = lax.optimization_barrier(held)
     other_sides = swap(sent_sides)
     other_encoder = swap(sent_encoder)
+    other_decoders = swap(sent_decoders)
     (sends,) = call(flip_kernel, [struct((near, half, wide), BF16)], [block])
     blocks = exchange(sends, NEAR)
     whole, codes, own_slope, sent_slope = call(
@@ -313,7 +312,7 @@
     parts, offset, other_whole, other_slope = lax.optimization_barrier((parts, offset, other_whole, other_slope))
     (parts,) = call(
         reduce_kernel,
-        [struct((zh, half // zh, wide), F32)],
+        [struct((zh, half // zh, wide), BF16)],
         [parts, offset],
     )
     parts = exchange(parts, ("zh",))

time: 155 us -> 152 us (0.981)
  starting transfers between devices: 28.8 us -> 23.1 us
  Pallas kernels: 15 us -> 17.6 us
  blocking collectives: 93.2 us -> 95.3 us
    ppermute x5, starting transfers between devices: 19.8 us -> 13.3 us  [swap(): return lax.ppermute(block, 'core', [(0, 1), (1, 0)])]
    pallas_call x10, Pallas kernels: 15 us -> 17.6 us  [call(): pl.pallas_call(run, out_shape=outs, in_specs=[ANY if k in remote else VME...]
    all_to_all x6, blocking collectives: 93.2 us -> 95.3 us  [exchange(): return lax.all_to_all(blocks, axes, 0, 0, tiled=True)]
where the time goes in v10:
time: 152 us; the launch traced here: 151 us
  blocking collectives  95.3 us (63%)
  starting transfers between devices  23.1 us (15%)
  Pallas kernels  17.6 us (12%)
  waiting for transfers between devices  13.6 us (9%)
    all_to_all x6, blocking collectives, exchange(): return lax.all_to_all(blocks, axes, 0, 0, tiled=True)  95.3 us
    pallas_call x10, Pallas kernels, call(): pl.pallas_call(run, out_shape=outs, in_specs=[ANY if k in remote else VME...  17.6 us
    ppermute x5, starting transfers between devices, swap(): return lax.ppermute(block, 'core', [(0, 1), (1, 0)])  13.3 us
    all_to_all x2, waiting for transfers between devices, exchange(): return lax.all_to_all(blocks, axes, 0, 0, tiled=True)  11.2 us
    all_to_all x2, starting transfers between devices, exchange(): return lax.all_to_all(blocks, axes, 0, 0, tiled=True)  9.19 us
  transfers between devices with their start and end apart: 8, of which 4 were waited for; matrix products, arithmetic and copies ran while one was open for 0% of the time, Pallas kernels for 2%

profile of v10, /device:TPU:1, one launch (start us, length us, event | category | flops | bytes accessed | tf_op | source)
XLA Modules:
  0.0 151.3 jit_solution(16847434789435262265)
XLA Ops:
  0.6 0.0 copy-start.3
  0.6 1.6 %shard_map.86 = (bf16[16,40,96]{2,1,0:T(8,128)(2,1)}, f32[48,128]{1,0:T(8,128)}, f32[48,128]{1,0:T(8,128)}) custom-call(bf16[40,192]{1,0:T(8,128)(2,1)} %bitcast.19, bf16[40,192]{1,0:T(8,128)(2,1)} %bitcast.20, bf16[1,40]{1,0:T(2,128)(2,1)} %refs_2_.1, f32[1,64]{1,0:T(1,128)} %refs_3_.1), custom_call_target="tpu_custom_call" | custom-call | bytes 203088 | tf_op jit(solution)/shard_map/pallas_call | solution.py:49
  2.2 0.0 copy-start.6
  2.2 0.0 copy-start.4
  2.2 30.2 %all_to_all.40 = bf16[16,40,96]{2,1,0:T(8,128)(2,1)S(1)} all-to-all(bf16[16,40,96]{2,1,0:T(8,128)(2,1)} %get-tuple-element.22), channel_id=1, replica_groups=mesh['layer'=4,'x'=4,'zh'=4,'zl'=2,'yh'=2,'core'=2] {'zh','yh','core'}, dimensions={0} | all-to-all | bytes 245760 | tf_op jit(solution)/shard_map/all_to_all | solution.py:31
  32.4 1.9 %collective-permute-start.2 = (bf16[256,5120]{1,0:T(8,128)(2,1)}, bf16[256,5120]{1,0:T(8,128)(2,1)}, u32[]{:S(2)}, u32[]{:S(2)}) collective-permute-start(bf16[256,5120]{1,0:T(8,128)(2,1)} %bitcast.12), channel_id=1, source_target_pairs={{0,1},{1,0},{2,3},{3,2},{4,5},{5,4},{6,7},{7,6},{8,9},{9,8},{10,11... | collective-permute-start | bytes 7864328 | tf_op jit(solution)/shard_map/ppermute | solution.py:35
  34.3 1.1 shard_map.87
  35.4 4.9 %all-to-all-start.1 = ((bf16[8,96,640]{2,1,0:T(8,128)(2,1)}), bf16[8,96,640]{2,1,0:T(8,128)(2,1)S(1)}, u32[]{:S(2)}, u32[]{:S(2)}) async-start(bf16[8,96,640]{2,1,0:T(8,128)(2,1)} %shard_map.87), calls=%async_computation.1 | async-start | bytes 1966080 | tf_op jit(solution)/shard_map/all_to_all | solution.py:31
  40.4 0.0 copy-done.3
  40.4 2.5 %collective-permute-start = (bf16[64,5120]{1,0:T(8,128)(2,1)S(1)}, bf16[64,5120]{1,0:T(8,128)(2,1)S(1)}, u32[]{:S(2)}, u32[]{:S(2)}) collective-permute-start(bf16[64,5120]{1,0:T(8,128)(2,1)S(1)} %bitcast.16), channel_id=1, source_target_pairs={{0,1},{1,0},{2,3},{3,2},{4,5},{5,4},{6,7},{7,6},{8,9},{9,8},{10,11... | collective-permute-start | bytes 1966088 | tf_op jit(solution)/shard_map/ppermute | solution.py:35
  42.9 0.0 copy-done.6
  42.9 1.9 %collective-permute-start.1 = (f32[48,128]{1,0:T(8,128)S(1)}, f32[48,128]{1,0:T(8,128)S(1)}, u32[]{:S(2)}, u32[]{:S(2)}) collective-permute-start(f32[48,128]{1,0:T(8,128)S(1)} %copy-done.6), channel_id=1, source_target_pairs={{0,1},{1,0},{2,3},{3,2},{4,5},{5,4},{6,7},{7,6},{8,9},{9,8},{10,11... | collective-permute-start | bytes 73736 | tf_op jit(solution)/shard_map/ppermute | solution.py:35
  44.8 1.2 collective-permute-done.1.refs_4_.refs_1_
  46.0 0.0 collective-permute-done.refs_2_
  46.0 9.0 %all-to-all-done.1.refs_0_ = bf16[8,96,640]{2,1,0:T(8,128)(2,1)S(1)} async-done(((bf16[8,96,640]{2,1,0:T(8,128)(2,1)}), bf16[8,96,640]{2,1,0:T(8,128)(2,1)S(1)}, u32[]{:S(2)}, u32[]{:S(2)}) %all-to-all-start.1) | async-done | bytes 983072 | tf_op jit(solution)/shard_map/all_to_all | solution.py:31
  54.9 0.0 copy-done.4
  54.9 1.8 %shard_map.88 = (bf16[96,5120]{1,0:T(8,128)(2,1)}, bf16[4,96,128]{2,1,0:T(8,128)(2,1)S(1)}, f32[64,96]{1,0:T(8,128)S(1)}, f32[64,96]{1,0:T(8,128)S(1)}) custom-call(bf16[8,96,640]{2,1,0:T(8,128)(2,1)S(1)} %all-to-all-done.1.refs_0_, bf16[64,5120]{1,0:T(8,128)(2,1)S(1)} %bitcast.17, bf16[64,5120]{1,0:T(8,128)(2,1)S(1)} %collective-permute-done.refs_2_, ...), custom_call_target="tpu_custom_call" | custom-call | flops 125829120 | bytes 3473408 | tf_op jit(solution)/shard_map/pallas_call | solution.py:49
  56.7 7.9 %all_to_all.41.refs_0_ = bf16[4,96,128]{2,1,0:T(8,128)(2,1)} all-to-all(bf16[4,96,128]{2,1,0:T(8,128)(2,1)S(1)} %get-tuple-element.29), channel_id=1, replica_groups=mesh['layer'=4,'x'=4,'zh'=4,'zl'=2,'yh'=2,'core'=2] {'layer'}, dimensions={0} | all-to-all | bytes 196608 | tf_op jit(solution)/shard_map/all_to_all | solution.py:31
  64.6 0.0 collective-permute-done.2.refs_2_
  64.6 4.8 %shard_map.89 = bf16[8,96,640]{2,1,0:T(8,128)(2,1)} custom-call(bf16[4,96,128]{2,1,0:T(8,128)(2,1)} %all_to_all.41.refs_0_, bf16[256,5120]{1,0:T(8,128)(2,1)} %bitcast.13, bf16[256,5120]{1,0:T(8,128)(2,1)} %collective-permute-done.2.refs_2_), custom_call_target="tpu_custom_call" | custom-call | flops 503316480 | bytes 6324224 | tf_op jit(solution)/shard_map/pallas_call | solution.py:49
  69.4 0.0 copy-start.5
  69.4 4.3 %all-to-all-start.3 = ((bf16[8,96,640]{2,1,0:T(8,128)(2,1)}), bf16[8,96,640]{2,1,0:T(8,128)(2,1)}, u32[]{:S(2)}, u32[]{:S(2)}) async-start(bf16[8,96,640]{2,1,0:T(8,128)(2,1)} %shard_map.89), calls=%async_computation.3 | async-start | bytes 1966080 | tf_op jit(solution)/shard_map/all_to_all | solution.py:31
  73.7 4.8 %collective-permute-start.4 = (bf16[96,5120]{1,0:T(8,128)(2,1)}, bf16[96,5120]{1,0:T(8,128)(2,1)S(1)}, u32[]{:S(2)}, u32[]{:S(2)}) collective-permute-start(bf16[96,5120]{1,0:T(8,128)(2,1)} %get-tuple-element.31.refs_3_), channel_id=1, source_target_pairs={{0,1},{1,0},{2,3},{3,2},{4,5},{5,4},{6,7},{7,6},{8,9},{9,8},{10,11... | collective-permute-start | bytes 2949128 | tf_op jit(solution)/shard_map/ppermute | solution.py:35
  78.5 0.2 shard_map.90
  78.6 0.7 collective-permute-start.3
  79.3 0.0 copy-start
  79.3 2.2 %collective-permute-start.5 = (f32[64,96]{1,0:T(8,128)S(1)}, f32[64,96]{1,0:T(8,128)S(1)}, u32[]{:S(2)}, u32[]{:S(2)}) collective-permute-start(f32[64,96]{1,0:T(8,128)S(1)} %get-tuple-element.32), channel_id=1, source_target_pairs={{0,1},{1,0},{2,3},{3,2},{4,5},{5,4},{6,7},{7,6},{8,9},{9,8},{10,11... | collective-permute-start | bytes 73736 | tf_op jit(solution)/shard_map/ppermute | solution.py:35
  81.5 0.0 collective-permute-done.3.refs_1_
  81.5 1.2 collective-permute-done.5.refs_2_
  82.7 0.0 collective-permute-done.4.refs_4_
  82.7 0.0 copy-start.1
  82.7 1.0 copy-done.1
  83.6 2.3 %all-to-all-done.3.refs_0_ = bf16[8,96,640]{2,1,0:T(8,128)(2,1)} async-done(((bf16[8,96,640]{2,1,0:T(8,128)(2,1)}), bf16[8,96,640]{2,1,0:T(8,128)(2,1)}, u32[]{:S(2)}, u32[]{:S(2)}) %all-to-all-start.3) | async-done | bytes 983072 | tf_op jit(solution)/shard_map/all_to_all | solution.py:31
  85.9 1.5 shard_map.91
  87.4 13.1 %all_to_all.42.refs_0_ = bf16[4,24,640]{2,1,0:T(8,128)(2,1)S(1)} all-to-all(bf16[4,24,640]{2,1,0:T(8,128)(2,1)S(1)} %shard_map.91), channel_id=1, replica_groups=mesh['layer'=4,'x'=4,'zh'=4,'zl'=2,'yh'=2,'core'=2] {'zh'}, dimensions={0} | all-to-all | bytes 245760 | tf_op jit(solution)/shard_map/all_to_all | solution.py:31
  100.6 15.1 %all_to_all.43.refs_1_ = bf16[8,24,640]{2,1,0:T(8,128)(2,1)S(1)} all-to-all(bf16[8,24,640]{2,1,0:T(8,128)(2,1)S(1)} %shard_map.92), channel_id=1, replica_groups=mesh['layer'=4,'x'=4,'zh'=4,'zl'=2,'yh'=2,'core'=2] {'zh','yh'}, dimensions={0} | all-to-all | bytes 491520 | tf_op jit(solution)/shard_map/all_to_all | solution.py:31
  115.7 0.0 copy-done.5
  115.7 0.3 shard_map.93
  116.0 14.7 %all_to_all.44.refs_0_ = bf16[8,96,640]{2,1,0:T(8,128)(2,1)S(1)} all-to-all(bf16[8,96,640]{2,1,0:T(8,128)(2,1)S(1)} %shard_map.93), channel_id=1, replica_groups=mesh['layer'=4,'x'=4,'zh'=4,'zl'=2,'yh'=2,'core'=2] {'x','zl'}, dimensions={0} | all-to-all | bytes 1966080 | tf_op jit(solution)/shard_map/all_to_all | solution.py:31
  130.6 0.0 copy-done
  130.6 0.0 copy-start.2
  130.6 3.3 %shard_map.94 = bf16[8,64,96]{2,1,0:T(8,128)(2,1)S(1)} custom-call(bf16[8,96,640]{2,1,0:T(8,128)(2,1)S(1)} %all_to_all.44.refs_0_, bf16[256,5120]{1,0:T(8,128)(2,1)S(1)} %bitcast.14, bf16[256,5120]{1,0:T(8,128)(2,1)} %collective-permute-done.2.refs_2_), custom_call_target="tpu_custom_call" | custom-call | flops 503316480 | bytes 6324224 | tf_op jit(solution)/shard_map/pallas_call | solution.py:49
  134.0 14.3 %all_to_all.45.refs_0_ = bf16[8,64,96]{2,1,0:T(8,128)(2,1)S(1)} all-to-all(bf16[8,64,96]{2,1,0:T(8,128)(2,1)S(1)} %shard_map.94), channel_id=1, replica_groups=mesh['layer'=4,'x'=4,'zh'=4,'zl'=2,'yh'=2,'core'=2] {'layer','core'}, dimensions={0} | all-to-all | bytes 196608 | tf_op jit(solution)/shard_map/all_to_all | solution.py:31
  148.3 0.0 copy-done.2
  148.3 3.0 %shard_map.95 = (f32[64,5120]{1,0:T(8,128)}, f32[1,64]{1,0:T(1,128)}) custom-call(bf16[8,64,96]{2,1,0:T(8,128)(2,1)S(1)} %all_to_all.45.refs_0_, f32[64,96]{1,0:T(8,128)S(1)} %get-tuple-element.35.refs_1_, f32[64,96]{1,0:T(8,128)S(1)} %collective-permute-done.5.refs_2_, bf16[96,5120]{1,0:T(8,128)(2,1)} %get-tuple-element.31.refs_3_, ...), custom_call_target="tpu_custom_call" | custom-call | flops 125829120 | bytes 3424512 | tf_op jit(solution)/shard_map/pallas_call | solution.py:49
  (1 shorter events, 0.0 us)
Async XLA Ops:
  0.6 39.7 %copy-start.3 = (bf16[1,64,5120]{2,1,0:T(8,128)(2,1)S(1)}, bf16[1,64,5120]{2,1,0:T(8,128)(2,1)}, u32[]{:S(2)}) copy-start(bf16[1,64,5120]{2,1,0:T(8,128)(2,1)} %param.9) | copy-start | bytes 1966084
  2.2 40.7 %copy-start.6 = (f32[48,128]{1,0:T(8,128)S(1)}, f32[48,128]{1,0:T(8,128)}, u32[]{:S(2)}) copy-start(f32[48,128]{1,0:T(8,128)} %get-tuple-element.28) | copy-start | bytes 73732
  2.2 52.7 %copy-start.4 = (f32[48,128]{1,0:T(8,128)S(1)}, f32[48,128]{1,0:T(8,128)}, u32[]{:S(2)}) copy-start(f32[48,128]{1,0:T(8,128)} %get-tuple-element.27.refs_3_.refs_0_) | copy-start | bytes 73732
  32.4 32.2 %collective-permute-start.2 = (bf16[256,5120]{1,0:T(8,128)(2,1)}, bf16[256,5120]{1,0:T(8,128)(2,1)}, u32[]{:S(2)}, u32[]{:S(2)}) collective-permute-start(bf16[256,5120]{1,0:T(8,128)(2,1)} %bitcast.12), channel_id=1, source_target_pairs={{0,1},{1,0},{2,3},{3,2},{4,5},{5,4},{6,7},{7,6},{8,9},{9,8},{10,11... | collective-permute-start | bytes 7864328 | tf_op jit(solution)/shard_map/ppermute | solution.py:35
  35.4 19.5 %all-to-all-start.1 = ((bf16[8,96,640]{2,1,0:T(8,128)(2,1)}), bf16[8,96,640]{2,1,0:T(8,128)(2,1)S(1)}, u32[]{:S(2)}, u32[]{:S(2)}) async-start(bf16[8,96,640]{2,1,0:T(8,128)(2,1)} %shard_map.87), calls=%async_computation.1 | async-start | bytes 1966080 | tf_op jit(solution)/shard_map/all_to_all | solution.py:31
  40.4 5.6 %collective-permute-start = (bf16[64,5120]{1,0:T(8,128)(2,1)S(1)}, bf16[64,5120]{1,0:T(8,128)(2,1)S(1)}, u32[]{:S(2)}, u32[]{:S(2)}) collective-permute-start(bf16[64,5120]{1,0:T(8,128)(2,1)S(1)} %bitcast.16), channel_id=1, source_target_pairs={{0,1},{1,0},{2,3},{3,2},{4,5},{5,4},{6,7},{7,6},{8,9},{9,8},{10,11... | collective-permute-start | bytes 1966088 | tf_op jit(solution)/shard_map/ppermute | solution.py:35
  42.9 3.1 %collective-permute-start.1 = (f32[48,128]{1,0:T(8,128)S(1)}, f32[48,128]{1,0:T(8,128)S(1)}, u32[]{:S(2)}, u32[]{:S(2)}) collective-permute-start(f32[48,128]{1,0:T(8,128)S(1)} %copy-done.6), channel_id=1, source_target_pairs={{0,1},{1,0},{2,3},{3,2},{4,5},{5,4},{6,7},{7,6},{8,9},{9,8},{10,11... | collective-permute-start | bytes 73736 | tf_op jit(solution)/shard_map/ppermute | solution.py:35
  69.4 46.3 %copy-start.5 = (s32[192]{0:T(256)S(1)}, s32[192]{0:T(256)}, u32[]{:S(2)}) copy-start(s32[192]{0:T(256)} %param.13) | copy-start | bytes 2308
  69.4 16.5 %all-to-all-start.3 = ((bf16[8,96,640]{2,1,0:T(8,128)(2,1)}), bf16[8,96,640]{2,1,0:T(8,128)(2,1)}, u32[]{:S(2)}, u32[]{:S(2)}) async-start(bf16[8,96,640]{2,1,0:T(8,128)(2,1)} %shard_map.89), calls=%async_computation.3 | async-start | bytes 1966080 | tf_op jit(solution)/shard_map/all_to_all | solution.py:31
  73.7 9.0 %collective-permute-start.4 = (bf16[96,5120]{1,0:T(8,128)(2,1)}, bf16[96,5120]{1,0:T(8,128)(2,1)S(1)}, u32[]{:S(2)}, u32[]{:S(2)}) collective-permute-start(bf16[96,5120]{1,0:T(8,128)(2,1)} %get-tuple-element.31.refs_3_), channel_id=1, source_target_pairs={{0,1},{1,0},{2,3},{3,2},{4,5},{5,4},{6,7},{7,6},{8,9},{9,8},{10,11... | collective-permute-start | bytes 2949128 | tf_op jit(solution)/shard_map/ppermute | solution.py:35
  78.6 2.9 %collective-permute-start.3 = (f32[80,96]{1,0:T(8,128)S(1)}, f32[80,96]{1,0:T(8,128)S(1)}, u32[]{:S(2)}, u32[]{:S(2)}) collective-permute-start(f32[80,96]{1,0:T(8,128)S(1)} %shard_map.90), channel_id=1, source_target_pairs={{0,0},{4,8},{8,16},{12,24},{16,4},{20,12},{24,20},{28,28},{1,1},{5... | collective-permute-start | bytes 92168 | tf_op jit(solution)/shard_map/ppermute | solution.py:41
  79.3 51.3 %copy-start = (bf16[1,4,64,5120]{3,2,1,0:T(8,128)(2,1)S(1)}, bf16[1,4,64,5120]{3,2,1,0:T(8,128)(2,1)}, u32[]{:S(2)}) copy-start(bf16[1,4,64,5120]{3,2,1,0:T(8,128)(2,1)} %param.11) | copy-start | bytes 7864324
  79.3 3.4 %collective-permute-start.5 = (f32[64,96]{1,0:T(8,128)S(1)}, f32[64,96]{1,0:T(8,128)S(1)}, u32[]{:S(2)}, u32[]{:S(2)}) collective-permute-start(f32[64,96]{1,0:T(8,128)S(1)} %get-tuple-element.32), channel_id=1, source_target_pairs={{0,1},{1,0},{2,3},{3,2},{4,5},{5,4},{6,7},{7,6},{8,9},{9,8},{10,11... | collective-permute-start | bytes 73736 | tf_op jit(solution)/shard_map/ppermute | solution.py:35
  82.7 1.0 copy-start.1
  130.6 17.6 %copy-start.2 = (bf16[96,5120]{1,0:T(8,128)(2,1)S(1)}, bf16[96,5120]{1,0:T(8,128)(2,1)}, u32[]{:S(2)}) copy-start(bf16[96,5120]{1,0:T(8,128)(2,1)} %copy-done.1) | copy-start | bytes 2949124
